TPU v7x, 256 devices: a whole 4x4x8 slice. The times are simulated.
256 devices in a mesh: gx: 32 (over z, y), gy: 8 (over x, core).
Axes of the slice: x: 4, y: 4, z: 8, core: 2. Of those that a mesh axis runs over, the one named last changes fastest.
Arguments:
- forcing: float32 [2, 256, 32768], P(None, 'gy', 'gx'), may hold values from -6 to 6
- ice_mask: int32 [256, 32768], P('gy', 'gx'), may hold values from 0 to 1, as said below
- viscosity_class: int32 [256, 32768], P('gy', 'gx'), may hold values from 0 to 15
- drag_class: int32 [256, 32768], P('gy', 'gx'), may hold values from 0 to 15
- viscosity_table: float32 [16], replicated, may hold values from 0.5 to 8
- drag_table: float32 [16], replicated, may hold values from 0.05 to 2
Outputs:
- velocity: float32 [2, 256, 32768], P(None, 'gy', 'gx')
Inputs may be any that keep to these rules, and one draw needn't show every extreme that they name: `ice_mask`: ice lies in tiles of 32 rows and 256 columns; whole tiles may be empty, and a tile may be partly covered behind a ragged front.
All inputs are finite; a program needn't handle non-finite values.
Results may differ from a plain program's by a relative error of at most 0.0001.
Values sent between devices are 32-bit elements; how exact they have to be, the bound alone decides.
No kernel may reach another device: no remote copies, remote signals or barrier semaphores. Data moves between devices by JAX's collectives and lax.ppermute only.
A program may use at most 128 MiB of HBM per device.

v0:
```python
import jax
import jax.numpy as jnp
from jax import lax
from jax.sharding import PartitionSpec as P

NU = 2
COARSE_SWEEPS = 6


OMEGA = 0.6


def padded(cells, sides, width):
    for axis, dim in sides:
        count = lax.axis_size(axis)
        ends = count - 1
        head = lax.slice_in_dim(cells, 0, width, axis=dim)
        tail = lax.slice_in_dim(cells, cells.shape[dim] - width, cells.shape[dim], axis=dim)
        cells = jnp.concatenate(
            [
                lax.ppermute(tail, axis, [(i, (i + 1) % count) for i in range(ends)]),
                cells,
                lax.ppermute(head, axis, [((i + 1) % count, i) for i in range(ends)]),
            ],
            axis=dim,
        )
    return cells


def field_edges(x):
    return padded(x, (("gy", 1), ("gx", 2)), 1)


def coefficient_border(x):
    return padded(x, (("gy", 1), ("gx", 2)), 2)


def shifted(a, dr, dc):
    rows = a.shape[-2]
    cols = a.shape[-1]
    return a[..., 1 + dr : rows - 1 + dr, 1 + dc : cols - 1 + dc]


def apply_operator(w_pad, coef_pad, beta):
    eta_pad = coef_pad[0]
    mask_pad = coef_pad[1]
    eta_here = shifted(eta_pad, 0, 0)
    mask_here = shifted(mask_pad, 0, 0)
    center = shifted(w_pad, 0, 0)
    flux = jnp.zeros_like(center)
    face_sum = jnp.zeros_like(eta_here)
    for dr, dc in ((1, 0), (-1, 0), (0, 1), (0, -1)):
        face = 0.5 * (eta_here + shifted(eta_pad, dr, dc)) * mask_here * shifted(mask_pad, dr, dc)
        flux = flux + face * (center - shifted(w_pad, dr, dc))
        face_sum = face_sum + face
    other = w_pad[::-1]
    mixed = 0.25 * (
        shifted(other, 1, 1)
        - shifted(other, 1, -1)
        - shifted(other, -1, 1)
        + shifted(other, -1, -1)
    )
    base = beta + 1.0 - mask_here
    image = base * center + flux + 0.2 * eta_here * mask_here * mixed
    return (image, base + face_sum)


def block_sum(x):
    shape = x.shape
    return x.reshape(shape[:-2] + (shape[-2] // 2, 2, shape[-1] // 2, 2)).sum(axis=(-3, -1))


def block_max(x):
    shape = x.shape
    return x.reshape(shape[:-2] + (shape[-2] // 2, 2, shape[-1] // 2, 2)).max(axis=(-3, -1))


def sweep(w_field, right, coef_pad, beta, padder):
    image, diag = apply_operator(padder(w_field), coef_pad, beta)
    return w_field + OMEGA * (right - image) / diag


def inner_coef(coef_wide):
    return coef_wide[0:2, 1:-1, 1:-1]


def smooth(w_field, right, coef_wide, beta, count):
    coef_inner = inner_coef(coef_wide)

    def one_step(index, current):
        return sweep(current, right, coef_inner, beta, field_edges)

    return lax.fori_loop(0, count, one_step, w_field)


def coarsest(right, levels):
    coef_wide, beta = levels[3]
    w_field = jnp.zeros_like(right)
    return smooth(w_field, right, coef_wide, beta, COARSE_SWEEPS)


def solve_level(level, right, levels, raw_coarse):
    if level == 3:
        return coarsest(right, levels)
    coef_wide, beta = levels[level]
    w_field = jnp.zeros_like(right)
    w_field = smooth(w_field, right, coef_wide, beta, NU)
    image, diag = apply_operator(field_edges(w_field), inner_coef(coef_wide), beta)
    coarse = solve_level(level + 1, block_sum(right - image), levels, raw_coarse)
    w_field = w_field + jnp.repeat(jnp.repeat(coarse, 2, axis=-2), 2, axis=-1)
    return smooth(w_field, right, coef_wide, beta, NU)


def lookup(classes, table):
    picks = jnp.arange(table.shape[0], dtype=jnp.int32)[:, None, None] == classes[None]
    return jnp.sum(jnp.where(picks, table[:, None, None], 0.0), axis=0)


def local(forcing, ice_mask, viscosity_class, drag_class, viscosity_table, drag_table):
    mask = ice_mask.astype(jnp.float32)
    eta = lookup(viscosity_class, viscosity_table) * mask
    beta = lookup(drag_class, drag_table) * mask
    levels = []
    raw_coarse = None
    for level in range(4):
        if level == 3:
            raw_coarse = (eta, mask, beta)
        levels.append((coefficient_border(jnp.stack([eta, mask, beta])), beta))
        mask = block_max(mask)
        eta = 0.5 * block_sum(eta)
        beta = block_sum(beta)
    return solve_level(0, forcing, levels, raw_coarse)


def solution(mesh):
    in_specs = (P(None, "gy", "gx"), P("gy", "gx"), P("gy", "gx"), P("gy", "gx"), P(), P())
    out_specs = P(None, "gy", "gx")
    return jax.shard_map(local, mesh=mesh, in_specs=in_specs, out_specs=out_specs, check_vma=False)
```

profile of v0, /device:TPU:128, one launch (start us, length us, event | category | flops | bytes accessed | tf_op | source)
XLA Modules:
  0.0 572.1 jit_solution(2660016158249634239)
XLA Ops:
  6.5 9.8 %reshape.154 = f32[16,2,512,2]{3,2,1,0:T(8,128)} reshape(f32[32,1024]{1,0:T(8,128)S(1)} %get-tuple-element.1863) | data formatting | bytes 262144 | tf_op jit(solution)/shard_map/reshape | solution.py:70
  16.3 9.7 %reshape.155 = f32[16,2,512,2]{3,2,1,0:T(8,128)} reshape(f32[32,1024]{1,0:T(8,128)S(1)} %get-tuple-element.962) | data formatting | bytes 262144 | tf_op jit(solution)/shard_map/reshape | solution.py:70
  35.1 9.8 %reshape.156 = f32[16,2,512,2]{3,2,1,0:T(8,128)} reshape(f32[32,1024]{1,0:T(8,128)S(1)} %get-tuple-element.960) | data formatting | bytes 262144 | tf_op jit(solution)/shard_map/reshape | solution.py:75
  93.0 7.2 %collective-permute-start.43 = (f32[3,12,2]{2,1,0:T(8,128)S(1)}, f32[3,12,2]{2,1,0:T(8,128)S(1)}, u32[]{:S(2)}, u32[]{:S(2)}) collective-permute-start(f32[3,12,2]{2,1,0:T(8,128)S(1)} %get-tuple-element.999), channel_id=1, source_target_pairs={{8,0},{16,8},{24,16},{32,24},{40,32},{48,40},{56,48},{64,56},{72,6... | collective-permute-start | bytes 872 | tf_op jit(solution)/shard_map/ppermute | solution.py:23
  109.2 7.2 %collective-permute-start.35 = (f32[3,20,2]{2,1,0:T(8,128)S(1)}, f32[3,20,2]{2,1,0:T(8,128)S(1)}, u32[]{:S(2)}, u32[]{:S(2)}) collective-permute-start(f32[3,20,2]{2,1,0:T(8,128)S(1)} %get-tuple-element.976), channel_id=1, source_target_pairs={{8,0},{16,8},{24,16},{32,24},{40,32},{48,40},{56,48},{64,56},{72,6... | collective-permute-start | bytes 1448 | tf_op jit(solution)/shard_map/ppermute | solution.py:23
  120.3 7.6 %collective-permute-start.31 = (f32[3,36,2]{2,1,0:T(8,128)S(1)}, f32[3,36,2]{2,1,0:T(8,128)S(1)}, u32[]{:S(2)}, u32[]{:S(2)}) collective-permute-start(f32[3,36,2]{2,1,0:T(8,128)S(1)} %get-tuple-element.937), channel_id=1, source_target_pairs={{8,0},{16,8},{24,16},{32,24},{40,32},{48,40},{56,48},{64,56},{72,6... | collective-permute-start | bytes 2600 | tf_op jit(solution)/shard_map/ppermute | solution.py:23
  132.0 40.6 %while.84 = (s32[]{:T(128)}, f32[2,32,1024]{2,1,0:T(8,128)S(1)}, f32[32,1024]{1,0:T(8,128)S(1)}, f32[2,34,1026]{2,1,0:T(8,128)S(1)}, f32[32,1024]{1,0:T(8,128)S(...) while((s32[]{:T(128)}, f32[2,32,1024]{2,1,0:T(8,128)S(1)}, ...), condition=%wide.region_3.4_spmd.clone, body=%wide.region_2.3_spmd.clone.sunk | while | flops 2745003 | bytes 10048567 | solution.py:93
  137.2 7.7 %collective-permute-start.14 = (f32[2,34,1]{2,1,0:T(8,128)S(1)}, f32[2,34,1]{2,1,0:T(8,128)S(1)}, u32[]{:S(2)}, u32[]{:S(2)}) collective-permute-start(f32[2,34,1]{2,1,0:T(8,128)S(1)} %get-tuple-element.1570), channel_id=1, source_target_pairs={{8,0},{16,8},{24,16},{32,24},{40,32},{48,40},{56,48},{64,56},{72,6... | collective-permute-start | bytes 824 | tf_op jit(solution)/shard_map/while/body/eval_jaxpr/ppermute | solution.py:23
  147.2 7.3 %collective-permute-done.15 = f32[2,34,1]{2,1,0:T(8,128)S(1)} collective-permute-done((f32[2,34,1]{2,1,0:T(8,128)S(1)}, f32[2,34,1]{2,1,0:T(8,128)S(1)}, u32[]{:S(2)}, u32[]{:S(2)}) %collective-permute-start.15) | collective-permute-done | bytes 304 | tf_op jit(solution)/shard_map/while/body/eval_jaxpr/ppermute | solution.py:21
  191.2 18.3 %reshape.157 = f32[2,16,2,512,2]{4,3,2,1,0:T(8,128)} reshape(f32[2,32,1024]{2,1,0:T(8,128)S(1)} %fusion.121) | data formatting | bytes 524288 | tf_op jit(solution)/shard_map/reshape | solution.py:70
  209.5 8.0 %reduce_sum.103 = f32[2,16,512]{2,1,0:T(8,128)S(1)} reduce(f32[2,16,2,512,2]{4,3,2,1,0:T(8,128)} %reshape.157, f32[]{:T(128)} %constant.175.clone.1), dimensions={2,4}, to_apply=%region_7.8 | reduce | flops 49152 | bytes 327684 | tf_op jit(solution)/shard_map/reduce_sum | solution.py:70
  217.5 36.4 %while.85 = (s32[]{:T(128)}, f32[2,16,512]{2,1,0:T(8,128)S(1)}, f32[16,512]{1,0:T(8,128)S(1)}, f32[2,18,514]{2,1,0:T(8,128)S(1)}, f32[16,512]{1,0:T(8,128)S(1)},...) while((s32[]{:T(128)}, f32[2,16,512]{2,1,0:T(8,128)S(1)}, ...), condition=%wide.region_9.10_spmd.clone, body=%wide.region_8.9_spmd.clone.sunk | while | flops 692587 | bytes 2566967 | solution.py:93
  280.6 36.2 %while.86 = (s32[]{:T(128)}, f32[2,8,256]{2,1,0:T(8,128)S(1)}, f32[8,256]{1,0:T(8,128)S(1)}, f32[2,10,258]{2,1,0:T(8,128)S(1)}, f32[8,256]{1,0:T(8,128)S(1)}, /*...) while((s32[]{:T(128)}, f32[2,8,256]{2,1,0:T(8,128)S(1)}, ...), condition=%wide.region_15.16_spmd.clone, body=%wide.region_14.15_spmd.clone.sunk | while | flops 186491 | bytes 690007 | solution.py:93
  342.5 105.9 %while.87 = (s32[]{:T(128)}, f32[2,4,128]{2,1,0:T(4,128)S(1)}, f32[4,128]{1,0:T(4,128)S(1)}, f32[2,6,130]{2,1,0:T(8,128)S(1)}, f32[4,128]{1,0:T(4,128)S(1)}, /*i...) while((s32[]{:T(128)}, f32[2,4,128]{2,1,0:T(4,128)S(1)}, ...), condition=%wide.region_21.22_spmd.clone, body=%wide.region_20.21_spmd.clone.sunk | while | flops 57859 | bytes 150743 | solution.py:93
  351.7 7.2 %collective-permute-start.27 = (f32[2,6,1]{2,1,0:T(8,128)S(1)}, f32[2,6,1]{2,1,0:T(8,128)S(1)}, u32[]{:S(2)}, u32[]{:S(2)}) collective-permute-start(f32[2,6,1]{2,1,0:T(8,128)S(1)} %get-tuple-element.1655), channel_id=1, source_target_pairs={{8,0},{16,8},{24,16},{32,24},{40,32},{48,40},{56,48},{64,56},{72,6... | collective-permute-start | bytes 152 | tf_op jit(solution)/shard_map/while/body/eval_jaxpr/ppermute | solution.py:23
  367.7 7.5 %collective-permute-start.27 = (f32[2,6,1]{2,1,0:T(8,128)S(1)}, f32[2,6,1]{2,1,0:T(8,128)S(1)}, u32[]{:S(2)}, u32[]{:S(2)}) collective-permute-start(f32[2,6,1]{2,1,0:T(8,128)S(1)} %get-tuple-element.1655), channel_id=1, source_target_pairs={{8,0},{16,8},{24,16},{32,24},{40,32},{48,40},{56,48},{64,56},{72,6... | collective-permute-start | bytes 152 | tf_op jit(solution)/shard_map/while/body/eval_jaxpr/ppermute | solution.py:23
  385.9 7.2 %collective-permute-start.27 = (f32[2,6,1]{2,1,0:T(8,128)S(1)}, f32[2,6,1]{2,1,0:T(8,128)S(1)}, u32[]{:S(2)}, u32[]{:S(2)}) collective-permute-start(f32[2,6,1]{2,1,0:T(8,128)S(1)} %get-tuple-element.1655), channel_id=1, source_target_pairs={{8,0},{16,8},{24,16},{32,24},{40,32},{48,40},{56,48},{64,56},{72,6... | collective-permute-start | bytes 152 | tf_op jit(solution)/shard_map/while/body/eval_jaxpr/ppermute | solution.py:23
  403.8 7.2 %collective-permute-start.27 = (f32[2,6,1]{2,1,0:T(8,128)S(1)}, f32[2,6,1]{2,1,0:T(8,128)S(1)}, u32[]{:S(2)}, u32[]{:S(2)}) collective-permute-start(f32[2,6,1]{2,1,0:T(8,128)S(1)} %get-tuple-element.1655), channel_id=1, source_target_pairs={{8,0},{16,8},{24,16},{32,24},{40,32},{48,40},{56,48},{64,56},{72,6... | collective-permute-start | bytes 152 | tf_op jit(solution)/shard_map/while/body/eval_jaxpr/ppermute | solution.py:23
  421.7 7.2 %collective-permute-start.27 = (f32[2,6,1]{2,1,0:T(8,128)S(1)}, f32[2,6,1]{2,1,0:T(8,128)S(1)}, u32[]{:S(2)}, u32[]{:S(2)}) collective-permute-start(f32[2,6,1]{2,1,0:T(8,128)S(1)} %get-tuple-element.1655), channel_id=1, source_target_pairs={{8,0},{16,8},{24,16},{32,24},{40,32},{48,40},{56,48},{64,56},{72,6... | collective-permute-start | bytes 152 | tf_op jit(solution)/shard_map/while/body/eval_jaxpr/ppermute | solution.py:23
  439.7 7.2 %collective-permute-start.27 = (f32[2,6,1]{2,1,0:T(8,128)S(1)}, f32[2,6,1]{2,1,0:T(8,128)S(1)}, u32[]{:S(2)}, u32[]{:S(2)}) collective-permute-start(f32[2,6,1]{2,1,0:T(8,128)S(1)} %get-tuple-element.1655), channel_id=1, source_target_pairs={{8,0},{16,8},{24,16},{32,24},{40,32},{48,40},{56,48},{64,56},{72,6... | collective-permute-start | bytes 152 | tf_op jit(solution)/shard_map/while/body/eval_jaxpr/ppermute | solution.py:23
  448.8 41.5 %while.81 = (s32[]{:T(128)}, f32[2,8,256]{2,1,0:T(8,128)S(1)}, f32[8,256]{1,0:T(8,128)S(1)}, f32[2,10,258]{2,1,0:T(8,128)S(1)}, f32[8,256]{1,0:T(8,128)S(1)}, /*...) while((s32[]{:T(128)}, f32[2,8,256]{2,1,0:T(8,128)S(1)}, ...), condition=%wide.region_23.24_spmd, body=%wide.region_22.23_spmd.sunk | while | flops 182394 | bytes 689989 | solution.py:93
  456.0 7.2 %collective-permute-start.2 = (f32[2,10,1]{2,1,0:T(8,128)S(1)}, f32[2,10,1]{2,1,0:T(8,128)S(1)}, u32[]{:S(2)}, u32[]{:S(2)}) collective-permute-start(f32[2,10,1]{2,1,0:T(8,128)S(1)} %get-tuple-element.1486), channel_id=1, source_target_pairs={{8,0},{16,8},{24,16},{32,24},{40,32},{48,40},{56,48},{64,56},{72,6... | collective-permute-start | bytes 248 | tf_op jit(solution)/shard_map/while/body/eval_jaxpr/ppermute | solution.py:23
  492.7 36.8 %while.82 = (s32[]{:T(128)}, f32[2,16,512]{2,1,0:T(8,128)S(1)}, f32[16,512]{1,0:T(8,128)S(1)}, f32[2,18,514]{2,1,0:T(8,128)S(1)}, f32[16,512]{1,0:T(8,128)S(1)},...) while((s32[]{:T(128)}, f32[2,16,512]{2,1,0:T(8,128)S(1)}, ...), condition=%wide.region_25.26_spmd, body=%wide.region_24.25_spmd.sunk | while | flops 676202 | bytes 2566949 | solution.py:93
  533.4 37.9 %while.83 = (s32[]{:T(128)}, f32[2,32,1024]{2,1,0:T(8,128)S(1)}, f32[32,1024]{1,0:T(8,128)S(1)}, f32[2,34,1026]{2,1,0:T(8,128)S(1)}, f32[32,1024]{1,0:T(8,128)S(...) while((s32[]{:T(128)}, f32[2,32,1024]{2,1,0:T(8,128)S(1)}, ...), condition=%wide.region_27.28_spmd, body=%wide.region_26.27_spmd.sunk | while | flops 2679466 | bytes 10048549 | solution.py:93
  (475 shorter events, 425.3 us)
Async XLA Ops:
  3.4 114.8 %collective-permute-start.28 = (f32[3,2,1024]{2,1,0:T(2,128)S(1)}, f32[3,2,1024]{2,1,0:T(2,128)S(1)}, u32[]{:S(2)}, u32[]{:S(2)}) collective-permute-start(f32[3,2,1024]{2,1,0:T(2,128)S(1)} %get-tuple-element.939), channel_id=1, source_target_pairs={{0,1},{1,2},{2,3},{3,4},{4,5},{5,6},{6,7},{8,9},{9,10},{10,11},{11... | collective-permute-start | bytes 73736 | tf_op jit(solution)/shard_map/ppermute | solution.py:21
  5.2 113.0 %collective-permute-start.29 = (f32[3,2,1024]{2,1,0:T(2,128)S(1)}, f32[3,2,1024]{2,1,0:T(2,128)S(1)}, u32[]{:S(2)}, u32[]{:S(2)}) collective-permute-start(f32[3,2,1024]{2,1,0:T(2,128)S(1)} %get-tuple-element.940), channel_id=1, source_target_pairs={{1,0},{2,1},{3,2},{4,3},{5,4},{6,5},{7,6},{9,8},{10,9},{11,10},{12... | collective-permute-start | bytes 73736 | tf_op jit(solution)/shard_map/ppermute | solution.py:23
  67.3 10.0 %collective-permute-start.48 = (f32[3,2,128]{2,1,0:T(2,128)S(1)}, f32[3,2,128]{2,1,0:T(2,128)S(1)}, u32[]{:S(2)}, u32[]{:S(2)}) collective-permute-start(f32[3,2,128]{2,1,0:T(2,128)S(1)} %get-tuple-element.1018), channel_id=1, source_target_pairs={{0,1},{1,2},{2,3},{3,4},{4,5},{5,6},{6,7},{8,9},{9,10},{10,11},{11... | collective-permute-start | bytes 9224 | tf_op jit(solution)/shard_map/ppermute | solution.py:21
  73.0 15.8 %collective-permute-start.40 = (f32[3,2,256]{2,1,0:T(2,128)S(1)}, f32[3,2,256]{2,1,0:T(2,128)S(1)}, u32[]{:S(2)}, u32[]{:S(2)}) collective-permute-start(f32[3,2,256]{2,1,0:T(2,128)S(1)} %get-tuple-element.1004), channel_id=1, source_target_pairs={{0,1},{1,2},{2,3},{3,4},{4,5},{5,6},{6,7},{8,9},{9,10},{10,11},{11... | collective-permute-start | bytes 18440 | tf_op jit(solution)/shard_map/ppermute | solution.py:21
  77.4 9.2 %collective-permute-start.50 = (f32[3,8,2]{2,1,0:T(8,128)S(1)}, f32[3,8,2]{2,1,0:T(8,128)S(1)}, u32[]{:S(2)}, u32[]{:S(2)}) collective-permute-start(f32[3,8,2]{2,1,0:T(8,128)S(1)} %get-tuple-element.1010), channel_id=1, source_target_pairs={{0,8},{8,16},{16,24},{24,32},{32,40},{40,48},{48,56},{56,64},{64,7... | collective-permute-start | bytes 584 | tf_op jit(solution)/shard_map/ppermute | solution.py:21
  90.4 13.6 %collective-permute-start.42 = (f32[3,12,2]{2,1,0:T(8,128)S(1)}, f32[3,12,2]{2,1,0:T(8,128)S(1)}, u32[]{:S(2)}, u32[]{:S(2)}) collective-permute-start(f32[3,12,2]{2,1,0:T(8,128)S(1)} %get-tuple-element.998), channel_id=1, source_target_pairs={{0,8},{8,16},{16,24},{24,32},{32,40},{40,48},{48,56},{56,64},{64,7... | collective-permute-start | bytes 872 | tf_op jit(solution)/shard_map/ppermute | solution.py:21
  93.0 12.3 %collective-permute-start.43 = (f32[3,12,2]{2,1,0:T(8,128)S(1)}, f32[3,12,2]{2,1,0:T(8,128)S(1)}, u32[]{:S(2)}, u32[]{:S(2)}) collective-permute-start(f32[3,12,2]{2,1,0:T(8,128)S(1)} %get-tuple-element.999), channel_id=1, source_target_pairs={{8,0},{16,8},{24,16},{32,24},{40,32},{48,40},{56,48},{64,56},{72,6... | collective-permute-start | bytes 872 | tf_op jit(solution)/shard_map/ppermute | solution.py:23
  107.2 9.9 %collective-permute-start.34 = (f32[3,20,2]{2,1,0:T(8,128)S(1)}, f32[3,20,2]{2,1,0:T(8,128)S(1)}, u32[]{:S(2)}, u32[]{:S(2)}) collective-permute-start(f32[3,20,2]{2,1,0:T(8,128)S(1)} %get-tuple-element.975), channel_id=1, source_target_pairs={{0,8},{8,16},{16,24},{24,32},{32,40},{40,48},{48,56},{56,64},{64,7... | collective-permute-start | bytes 1448 | tf_op jit(solution)/shard_map/ppermute | solution.py:21
  118.4 10.1 %collective-permute-start.30 = (f32[3,36,2]{2,1,0:T(8,128)S(1)}, f32[3,36,2]{2,1,0:T(8,128)S(1)}, u32[]{:S(2)}, u32[]{:S(2)}) collective-permute-start(f32[3,36,2]{2,1,0:T(8,128)S(1)} %get-tuple-element.938), channel_id=1, source_target_pairs={{0,8},{8,16},{16,24},{24,32},{32,40},{40,48},{48,56},{56,64},{64,7... | collective-permute-start | bytes 2600 | tf_op jit(solution)/shard_map/ppermute | solution.py:21
  120.3 9.9 %collective-permute-start.31 = (f32[3,36,2]{2,1,0:T(8,128)S(1)}, f32[3,36,2]{2,1,0:T(8,128)S(1)}, u32[]{:S(2)}, u32[]{:S(2)}) collective-permute-start(f32[3,36,2]{2,1,0:T(8,128)S(1)} %get-tuple-element.937), channel_id=1, source_target_pairs={{8,0},{16,8},{24,16},{32,24},{40,32},{48,40},{56,48},{64,56},{72,6... | collective-permute-start | bytes 2600 | tf_op jit(solution)/shard_map/ppermute | solution.py:23
  137.2 9.9 %collective-permute-start.14 = (f32[2,34,1]{2,1,0:T(8,128)S(1)}, f32[2,34,1]{2,1,0:T(8,128)S(1)}, u32[]{:S(2)}, u32[]{:S(2)}) collective-permute-start(f32[2,34,1]{2,1,0:T(8,128)S(1)} %get-tuple-element.1570), channel_id=1, source_target_pairs={{8,0},{16,8},{24,16},{32,24},{40,32},{48,40},{56,48},{64,56},{72,6... | collective-permute-start | bytes 824 | tf_op jit(solution)/shard_map/while/body/eval_jaxpr/ppermute | solution.py:23
  145.0 9.5 %collective-permute-start.15 = (f32[2,34,1]{2,1,0:T(8,128)S(1)}, f32[2,34,1]{2,1,0:T(8,128)S(1)}, u32[]{:S(2)}, u32[]{:S(2)}) collective-permute-start(f32[2,34,1]{2,1,0:T(8,128)S(1)} %get-tuple-element.1571), channel_id=1, source_target_pairs={{0,8},{8,16},{16,24},{24,32},{32,40},{40,48},{48,56},{56,64},{64,7... | collective-permute-start | bytes 824 | tf_op jit(solution)/shard_map/while/body/eval_jaxpr/ppermute | solution.py:21
  162.5 9.2 %collective-permute-start.15 = (f32[2,34,1]{2,1,0:T(8,128)S(1)}, f32[2,34,1]{2,1,0:T(8,128)S(1)}, u32[]{:S(2)}, u32[]{:S(2)}) collective-permute-start(f32[2,34,1]{2,1,0:T(8,128)S(1)} %get-tuple-element.1571), channel_id=1, source_target_pairs={{0,8},{8,16},{16,24},{24,32},{32,40},{40,48},{48,56},{56,64},{64,7... | collective-permute-start | bytes 824 | tf_op jit(solution)/shard_map/while/body/eval_jaxpr/ppermute | solution.py:21
  181.1 9.2 %collective-permute-start.39 = (f32[2,34,1]{2,1,0:T(8,128)S(1)}, f32[2,34,1]{2,1,0:T(8,128)S(1)}, u32[]{:S(2)}, u32[]{:S(2)}) collective-permute-start(f32[2,34,1]{2,1,0:T(8,128)S(1)} %get-tuple-element.955), channel_id=1, source_target_pairs={{0,8},{8,16},{16,24},{24,32},{32,40},{40,48},{48,56},{56,64},{64,7... | collective-permute-start | bytes 824 | tf_op jit(solution)/shard_map/ppermute | solution.py:21
  244.6 9.0 %collective-permute-start.19 = (f32[2,18,1]{2,1,0:T(8,128)S(1)}, f32[2,18,1]{2,1,0:T(8,128)S(1)}, u32[]{:S(2)}, u32[]{:S(2)}) collective-permute-start(f32[2,18,1]{2,1,0:T(8,128)S(1)} %get-tuple-element.1599), channel_id=1, source_target_pairs={{0,8},{8,16},{16,24},{24,32},{32,40},{40,48},{48,56},{56,64},{64,7... | collective-permute-start | bytes 440 | tf_op jit(solution)/shard_map/while/body/eval_jaxpr/ppermute | solution.py:21
  349.8 9.2 %collective-permute-start.26 = (f32[2,6,1]{2,1,0:T(8,128)S(1)}, f32[2,6,1]{2,1,0:T(8,128)S(1)}, u32[]{:S(2)}, u32[]{:S(2)}) collective-permute-start(f32[2,6,1]{2,1,0:T(8,128)S(1)} %get-tuple-element.1654), channel_id=1, source_target_pairs={{0,8},{8,16},{16,24},{24,32},{32,40},{40,48},{48,56},{56,64},{64,7... | collective-permute-start | bytes 152 | tf_op jit(solution)/shard_map/while/body/eval_jaxpr/ppermute | solution.py:21
  365.8 9.4 %collective-permute-start.26 = (f32[2,6,1]{2,1,0:T(8,128)S(1)}, f32[2,6,1]{2,1,0:T(8,128)S(1)}, u32[]{:S(2)}, u32[]{:S(2)}) collective-permute-start(f32[2,6,1]{2,1,0:T(8,128)S(1)} %get-tuple-element.1654), channel_id=1, source_target_pairs={{0,8},{8,16},{16,24},{24,32},{32,40},{40,48},{48,56},{56,64},{64,7... | collective-permute-start | bytes 152 | tf_op jit(solution)/shard_map/while/body/eval_jaxpr/ppermute | solution.py:21
  384.0 9.2 %collective-permute-start.26 = (f32[2,6,1]{2,1,0:T(8,128)S(1)}, f32[2,6,1]{2,1,0:T(8,128)S(1)}, u32[]{:S(2)}, u32[]{:S(2)}) collective-permute-start(f32[2,6,1]{2,1,0:T(8,128)S(1)} %get-tuple-element.1654), channel_id=1, source_target_pairs={{0,8},{8,16},{16,24},{24,32},{32,40},{40,48},{48,56},{56,64},{64,7... | collective-permute-start | bytes 152 | tf_op jit(solution)/shard_map/while/body/eval_jaxpr/ppermute | solution.py:21
  401.9 9.2 %collective-permute-start.26 = (f32[2,6,1]{2,1,0:T(8,128)S(1)}, f32[2,6,1]{2,1,0:T(8,128)S(1)}, u32[]{:S(2)}, u32[]{:S(2)}) collective-permute-start(f32[2,6,1]{2,1,0:T(8,128)S(1)} %get-tuple-element.1654), channel_id=1, source_target_pairs={{0,8},{8,16},{16,24},{24,32},{32,40},{40,48},{48,56},{56,64},{64,7... | collective-permute-start | bytes 152 | tf_op jit(solution)/shard_map/while/body/eval_jaxpr/ppermute | solution.py:21
  419.8 9.2 %collective-permute-start.26 = (f32[2,6,1]{2,1,0:T(8,128)S(1)}, f32[2,6,1]{2,1,0:T(8,128)S(1)}, u32[]{:S(2)}, u32[]{:S(2)}) collective-permute-start(f32[2,6,1]{2,1,0:T(8,128)S(1)} %get-tuple-element.1654), channel_id=1, source_target_pairs={{0,8},{8,16},{16,24},{24,32},{32,40},{40,48},{48,56},{56,64},{64,7... | collective-permute-start | bytes 152 | tf_op jit(solution)/shard_map/while/body/eval_jaxpr/ppermute | solution.py:21
  437.7 9.2 %collective-permute-start.26 = (f32[2,6,1]{2,1,0:T(8,128)S(1)}, f32[2,6,1]{2,1,0:T(8,128)S(1)}, u32[]{:S(2)}, u32[]{:S(2)}) collective-permute-start(f32[2,6,1]{2,1,0:T(8,128)S(1)} %get-tuple-element.1654), channel_id=1, source_target_pairs={{0,8},{8,16},{16,24},{24,32},{32,40},{40,48},{48,56},{56,64},{64,7... | collective-permute-start | bytes 152 | tf_op jit(solution)/shard_map/while/body/eval_jaxpr/ppermute | solution.py:21
  456.0 9.1 %collective-permute-start.2 = (f32[2,10,1]{2,1,0:T(8,128)S(1)}, f32[2,10,1]{2,1,0:T(8,128)S(1)}, u32[]{:S(2)}, u32[]{:S(2)}) collective-permute-start(f32[2,10,1]{2,1,0:T(8,128)S(1)} %get-tuple-element.1486), channel_id=1, source_target_pairs={{8,0},{16,8},{24,16},{32,24},{40,32},{48,40},{56,48},{64,56},{72,6... | collective-permute-start | bytes 248 | tf_op jit(solution)/shard_map/while/body/eval_jaxpr/ppermute | solution.py:23
  542.4 9.2 %collective-permute-start.11 = (f32[2,34,1]{2,1,0:T(8,128)S(1)}, f32[2,34,1]{2,1,0:T(8,128)S(1)}, u32[]{:S(2)}, u32[]{:S(2)}) collective-permute-start(f32[2,34,1]{2,1,0:T(8,128)S(1)} %get-tuple-element.1543), channel_id=1, source_target_pairs={{0,8},{8,16},{16,24},{24,32},{32,40},{40,48},{48,56},{56,64},{64,7... | collective-permute-start | bytes 824 | tf_op jit(solution)/shard_map/while/body/eval_jaxpr/ppermute | solution.py:21
  561.3 9.2 %collective-permute-start.11 = (f32[2,34,1]{2,1,0:T(8,128)S(1)}, f32[2,34,1]{2,1,0:T(8,128)S(1)}, u32[]{:S(2)}, u32[]{:S(2)}) collective-permute-start(f32[2,34,1]{2,1,0:T(8,128)S(1)} %get-tuple-element.1543), channel_id=1, source_target_pairs={{0,8},{8,16},{16,24},{24,32},{32,40},{40,48},{48,56},{56,64},{64,7... | collective-permute-start | bytes 824 | tf_op jit(solution)/shard_map/while/body/eval_jaxpr/ppermute | solution.py:21
  (96 other events, 873.6 us)
where the time goes:
time: 580 us; the launch traced here: 572 us
  starting transfers between devices  328 us (57%)
  waiting for transfers between devices  108 us (19%)
  local copies, waits for them, and re-layouts  80.1 us (14%)
  other arithmetic  52.7 us (9%)
    ppermute x50, starting transfers between devices, padded(): lax.ppermute(tail, axis, [(i, (i + 1) % count) for i in range(ends)])  184 us
    ppermute x50, starting transfers between devices, padded(): lax.ppermute(head, axis, [((i + 1) % count, i) for i in range(ends)])  144 us
    ppermute x50, waiting for transfers between devices, padded(): lax.ppermute(tail, axis, [(i, (i + 1) % count) for i in range(ends)])  93.8 us
    reshape x7, local copies, waits for them, and re-layouts, block_sum(): x.reshape(shape[:-2] + (shape[-2] // 2, 2, shape[-1] // 2, 2))  49.2 us
    reduce_sum x9, other arithmetic, block_sum(): x.reshape(shape[:-2] + (shape[-2] // 2, 2, shape[-1] // 2, 2))  25.5 us
    ppermute x50, waiting for transfers between devices, padded(): lax.ppermute(head, axis, [((i + 1) % count, i) for i in range(ends)])  14.1 us
    reshape x3, local copies, waits for them, and re-layouts, block_max(): x.reshape(shape[:-2] + (shape[-2] // 2, 2, shape[-1] // 2, 2))  13.6 us
  transfers between devices with their start and end apart: 100, of which 46 were waited for; matrix products, arithmetic and copies ran while one was open for 12% of the time, Pallas kernels for 0%

commit v1 on v0

v1 whole, which is shorter than its diff:
```python
import jax
import jax.numpy as jnp
from jax import lax
from jax.experimental import pallas as pl
from jax.experimental.pallas import tpu as pltpu
from jax.sharding import PartitionSpec as P

OMEGA = 0.6
KEEP = 1.0 - OMEGA
ROWS, COLS = 32, 1024
EDGE = 128
HALO = 16
WIDE = COLS + 2 * EDGE
PLANES = (8, 4, 2)
LANES = (1280, 640, 384)
LANES3 = 256
VMEM_LIMIT = 48 * 1024 * 1024


def vmem(count):
    return [pl.BlockSpec(memory_space=pltpu.VMEM)] * count


def params():
    return pltpu.CompilerParams(vmem_limit_bytes=VMEM_LIMIT)


def shape(*dims):
    return jax.ShapeDtypeStruct(dims, jnp.float32)


def from_left(x):
    return pltpu.roll(x, 1, axis=1)


def from_right(x):
    return pltpu.roll(x, x.shape[1] - 1, axis=1)


def from_above(x):
    return pltpu.roll(x, 1, axis=0)


def from_below(x):
    return pltpu.roll(x, x.shape[0] - 1, axis=0)


def tiles(x):
    return [x[:, i : i + 128] for i in range(0, x.shape[1], 128)]


def lane(kind):
    return lax.broadcasted_iota(jnp.int32, (8, 128), kind)


def pick(x, index):
    return jnp.take_along_axis(x, index, axis=1, mode="promise_in_bounds")


def halve_lanes(x, lanes):
    at = lane(1)
    index = 2 * (at % 64)
    parts = [pick(t + from_right(t), index) for t in tiles(x)]
    out = []
    for i in range(0, len(parts), 2):
        high = parts[i + 1] if i + 1 < len(parts) else jnp.zeros_like(parts[i])
        out.append(jnp.where(at < 64, parts[i], high))
    while len(out) * 128 < lanes:
        out.append(jnp.zeros_like(out[0]))
    return jnp.concatenate(out[: lanes // 128], axis=1)


def double_lanes(x, lanes):
    index = lane(1) // 2
    parts = tiles(x)
    return jnp.concatenate(
        [pick(parts[i // 2], index + 64 * (i % 2)) for i in range(lanes // 128)], axis=1
    )


def coefficients(eta, beta, eta_below, face_above):
    ice = eta > 0.0
    eta_right = from_right(eta)
    right = jnp.where(ice & (eta_right > 0.0), 0.5 * (eta + eta_right), 0.0)
    left = from_left(right)
    below = jnp.where(ice & (eta_below > 0.0), 0.5 * (eta + eta_below), 0.0)
    above = face_above(below)
    base = beta + jnp.where(ice, 0.0, 1.0)
    diag = base + ((right + left) + (below + above))
    return right, left, below, above, 0.05 * eta_right, 0.05 * from_left(eta), diag


def gather_terms(right, left, cross_right, cross_left, below, above, here, under, over, other_step, force):
    from_west = from_left(right * here + cross_right * other_step)
    from_east = from_right(left * here - cross_left * other_step)
    return (force + (from_west + from_east)) + (below * under + above * over)


class Level:
    def __init__(self, planes, refs):
        self.planes = planes
        self.right, self.left, self.cross_right, self.cross_left, self.below, self.scale, self.force, self.field = refs

    @staticmethod
    def shapes(level):
        planes, lanes = PLANES[level], LANES[level]
        one = [(planes, 8, lanes)] * 4 + [(planes + 1, 8, lanes), (planes, 8, lanes)]
        return one + [(2, planes, 8, lanes), (2, planes + 2, 8, lanes)]

    def wrap(self, field):
        for k in range(2):
            field[k, 0] = from_above(field[k, self.planes])
            field[k, self.planes + 1] = from_below(field[k, 1])

    def terms(self, p, field):
        out = []
        steps = [field[k, p + 2] - field[k, p] for k in range(2)]
        for k in range(2):
            out.append(
                gather_terms(
                    self.right[p],
                    self.left[p],
                    self.cross_right[p],
                    self.cross_left[p],
                    self.below[p + 1],
                    self.below[p],
                    field[k, p + 1],
                    field[k, p + 2],
                    field[k, p],
                    steps[1 - k],
                    self.force[k, p],
                )
            )
        return out

    def sweep(self, source, target):
        for p in range(self.planes):
            terms = self.terms(p, source)
            for k in range(2):
                target[k, p + 1] = KEEP * source[k, p + 1] + self.scale[p] * terms[k]

    def setup(self, eta, beta, diag):
        planes = self.planes
        for p in range(planes):
            here = eta[p]
            ice = here > 0.0
            next_eta = eta[p + 1] if p + 1 < planes else from_below(eta[0])
            self.below[p + 1] = jnp.where(ice & (next_eta > 0.0), 0.5 * (here + next_eta), 0.0)
        self.below[0] = from_above(self.below[planes])
        for p in range(planes):
            here = eta[p]
            ice = here > 0.0
            eta_right = from_right(here)
            right = jnp.where(ice & (eta_right > 0.0), 0.5 * (here + eta_right), 0.0)
            left = from_left(right)
            base = beta[p] + jnp.where(ice, 0.0, 1.0)
            total = base + ((right + left) + (self.below[p + 1] + self.below[p]))
            self.right[p] = right
            self.left[p] = left
            self.cross_right[p] = 0.05 * eta_right
            self.cross_left[p] = 0.05 * from_left(here)
            diag[p] = total
            self.scale[p] = OMEGA / total

    def first_sweeps(self, other):
        for k in range(2):
            for p in range(self.planes):
                other[k, p + 1] = self.scale[p] * self.force[k, p]
        self.wrap(other)
        self.sweep(other, self.field)
        self.wrap(self.field)

    def restrict(self, diag, target, lanes):
        for p in range(0, self.planes, 2):
            rest = [0.0, 0.0]
            for q in (p, p + 1):
                terms = self.terms(q, self.field)
                for k in range(2):
                    rest[k] = rest[k] + (terms[k] - diag[q] * self.field[k, q + 1])
            for k in range(2):
                target(k, p // 2, halve_lanes(rest[k], lanes))

    def last_sweeps(self, coarse, result, other):
        for k in range(2):
            for p in range(0, self.planes, 2):
                add = double_lanes(coarse(k, p // 2), self.field.shape[-1])
                result[k, p + 1] = self.field[k, p + 1] + add
                result[k, p + 2] = self.field[k, p + 2] + add
        self.wrap(result)
        self.sweep(result, other)
        self.wrap(other)
        self.sweep(other, result)


def halve_planes(source, target, planes, lanes, scale):
    for p in range(0, planes, 2):
        both = halve_lanes(source[p] + source[p + 1], lanes)
        target[p // 2] = scale * both if scale != 1.0 else both


def lookup_kernel(v_table, d_table, forcing, mask, v_class, d_class, send_even, send_odd, coef):
    at = lane(1)
    tables = []
    for table in (v_table, d_table):
        row = jnp.zeros((8, 128), jnp.float32)
        for i in range(16):
            row = jnp.where(at == i, table[i], row)
        tables.append(row)
    for r in range(0, ROWS, 8):
        for c in range(0, COLS, 128):
            part = (pl.ds(r, 8), pl.ds(c, 128))
            ice = mask[part].astype(jnp.float32)
            for k, classes in enumerate((v_class, d_class)):
                coef[(k,) + part] = pick(tables[k], classes[part]) * ice
    even = lax.axis_index("gx") % 2 == 0
    for k in range(2):
        for source, row in ((forcing, k), (coef, k + 2)):
            low = source[k, :, 0:EDGE]
            high = source[k, :, COLS - EDGE : COLS]
            send_even[row] = jnp.where(even, high, low)
            send_odd[row] = jnp.where(even, low, high)


def side_columns(get_even, get_odd):
    gx = lax.axis_index("gx")
    even = gx % 2 == 0
    a, b = get_even, get_odd
    left = jnp.where(gx == 0, 0.0, jnp.where(even, b, a))
    right = jnp.where(gx == lax.axis_size("gx") - 1, 0.0, jnp.where(even, a, b))
    return left, right


def rows_kernel(forcing, coef, got_even, got_odd, send_even, send_odd):
    even = lax.axis_index("gy") % 2 == 0
    for row in range(4):
        source = forcing if row < 2 else coef
        top = slice(0, HALO)
        bottom = slice(ROWS - HALO, ROWS)
        for part, flag in ((send_even, even), (send_odd, jnp.logical_not(even))):
            lows = side_columns(got_even[row, top], got_odd[row, top])
            highs = side_columns(got_even[row, bottom], got_odd[row, bottom])
            part[row, :, 0:EDGE] = jnp.where(flag, highs[0], lows[0])
            part[row, :, WIDE - EDGE : WIDE] = jnp.where(flag, highs[1], lows[1])
            part[row, :, EDGE : WIDE - EDGE] = jnp.where(flag, source[row % 2, bottom], source[row % 2, top])


def own_rows(a, b):
    upper = lax.broadcasted_iota(jnp.int32, a.shape, 0) < 4
    return jnp.where(upper, pltpu.roll(a, 6, axis=0), pltpu.roll(b, 2, axis=0))


def down_kernel(forcing, coef, got_even, got_odd, rows_even, rows_odd, *refs):
    levels = [Level(PLANES[i], refs[8 * i : 8 * i + 8]) for i in range(3)]
    near, far = refs[24:26]
    natural = refs[26]
    etas, betas, diags, others = (refs[27 + 3 * i : 30 + 3 * i] for i in range(4))
    gy = lax.axis_index("gy")
    even = gy % 2 == 0
    first = gy == 0
    last = gy == lax.axis_size("gy") - 1
    for row in range(4):
        source = forcing if row < 2 else coef
        sides = side_columns(got_even[row], got_odd[row])
        for i in range(WIDE // 128):
            cols = slice(128 * i, 128 * i + 128)
            a, b = rows_even[row, :, cols], rows_odd[row, :, cols]
            natural[i, 0:HALO] = jnp.where(first, 0.0, jnp.where(even, b, a))
            natural[i, HALO + ROWS :] = jnp.where(last, 0.0, jnp.where(even, a, b))
            if i == 0:
                own = sides[0]
            elif i == WIDE // 128 - 1:
                own = sides[1]
            else:
                own = source[row % 2, :, 128 * i - 128 : 128 * i]
            natural[i, HALO : HALO + ROWS] = own
            for p in range(8):
                plane = natural[i, pl.ds(p, 8, stride=8), :]
                if row < 2:
                    levels[0].force[row, p, :, cols] = plane
                else:
                    (etas, betas)[row - 2][0][p, :, cols] = plane
    for level in range(3):
        here = levels[level]
        here.setup(etas[level], betas[level], diags[level])
        here.first_sweeps(others[level])
        if level < 2:
            lanes = LANES[level + 1]
            halve_planes(etas[level], etas[level + 1], here.planes, lanes, 0.5)
            halve_planes(betas[level], betas[level + 1], here.planes, lanes, 1.0)

            def store(k, p, value, target=levels[level + 1].force):
                target[k, p] = value

            here.restrict(diags[level], store, lanes)
    found = [None, None]

    def keep(k, p, value):
        found[k] = value

    levels[2].restrict(diags[2], keep, LANES3)
    eta = 0.5 * halve_lanes(etas[2][0] + etas[2][1], LANES3)
    beta = halve_lanes(betas[2][0] + betas[2][1], LANES3)
    head = jnp.concatenate([own_rows(found[0], found[1]), own_rows(eta, beta)], axis=1)
    far[...] = head
    near[:, 0 : 2 * LANES3] = head
    at = 2 * LANES3
    for p in range(2):
        near[:, at : at + 384] = own_rows(levels[2].field[0, p + 1], levels[2].field[1, p + 1])
        near[:, at + 768 : at + 1152] = own_rows(levels[2].force[0, p], levels[2].force[1, p])
        at += 384


def up_kernel(far, near_even, near_odd, far_above, far_below, *refs):
    levels = [Level(PLANES[i], refs[8 * i : 8 * i + 8]) for i in range(3)]
    velocity, natural, late_force, late_field = refs[24:28]
    fields, others = refs[28:31], refs[31:34]
    gy = lax.axis_index("gy")
    count = lax.axis_size("gy")
    even = gy % 2 == 0

    def above(part):
        return jnp.where(gy == 0, 0.0, jnp.where(even, near_odd[:, part], near_even[:, part]))

    def below(part):
        return jnp.where(gy == count - 1, 0.0, jnp.where(even, near_even[:, part], near_odd[:, part]))

    def sublanes(like):
        return lax.broadcasted_iota(jnp.int32, like.shape, 0)

    def stacked(part):
        m2 = jnp.where(gy < 2, 0.0, far_above[:, part])
        p2 = jnp.where(gy > count - 3, 0.0, far_below[:, part])
        m1, p1, own = above(part), below(part), far[:, part]
        upper = sublanes(own) < 4

        def halves(x, y, second):
            if second:
                return jnp.where(upper, pltpu.roll(x, 4, axis=0), y)
            return jnp.where(upper, x, pltpu.roll(y, 4, axis=0))

        zero = jnp.zeros_like(own)
        return [
            jnp.concatenate([halves(m2, m1, s), halves(own, p1, s), halves(p2, zero, s)], axis=0)
            for s in (False, True)
        ]

    force = stacked(slice(0, LANES3))
    eta, beta = stacked(slice(LANES3, 2 * LANES3))
    right, left, under, over, cross_right, cross_left, diag = coefficients(eta, beta, from_below(eta), from_above)
    scale = OMEGA / diag
    field = [scale * force[0], scale * force[1]]
    for _ in range(5):
        downs = [from_below(x) for x in field]
        ups = [from_above(x) for x in field]
        steps = [downs[k] - ups[k] for k in range(2)]
        field = [
            KEEP * field[k]
            + scale
            * gather_terms(
                right, left, cross_right, cross_left, under, over, field[k], downs[k], ups[k], steps[1 - k], force[k]
            )
            for k in range(2)
        ]
    coarsest = []
    for k in range(2):
        a, b = pltpu.roll(field[k][0:8], 2, axis=0), pltpu.roll(field[k][8:16], 2, axis=0)
        coarsest.append(jnp.where(sublanes(a) < 2, a, b))
    at = 2 * LANES3
    for p in range(2):
        for target, own, start, shift in (
            (late_field, levels[2].field, at, 1),
            (late_force, levels[2].force, at + 768, 0),
        ):
            up, down = above(slice(start, start + 384)), below(slice(start, start + 384))
            for k in range(2):
                turn = 2 if k else 6
                a, b = pltpu.roll(up, turn, axis=0), pltpu.roll(down, turn, axis=0)
                sub = sublanes(a)
                target[k, p + shift] = jnp.where(sub < 2, a, jnp.where(sub < 6, own[k, p + shift], b))
        at += 384
    levels[2].force = late_force
    levels[2].field = late_field
    coarse = lambda k, p: coarsest[k]
    for level in (2, 1, 0):
        levels[level].last_sweeps(coarse, fields[level], others[level])
        coarse = lambda k, p, result=fields[level]: result[k, p + 1]
    for k in range(2):
        for i in range(COLS // 128):
            for p in range(8):
                part = fields[0][k, p + 1, :, 128 * i + EDGE : 128 * i + EDGE + 128]
                natural[i, pl.ds(p, 4, stride=8), :] = pltpu.roll(part, 6, axis=0)[0:4]
            velocity[k, :, 128 * i : 128 * i + 128] = natural[i]


def swap(x, axis, odd):
    count = lax.axis_size(axis)
    pairs = []
    for i in range(odd, count, 2):
        j = (i + 1) % count
        pairs += [(i, j), (j, i)]
    return lax.ppermute(x, axis, pairs)


def turn(x, axis, step):
    count = lax.axis_size(axis)
    return lax.ppermute(x, axis, [(i, (i + step) % count) for i in range(count)])


def local(forcing, ice_mask, viscosity_class, drag_class, viscosity_table, drag_table):
    smem = [pl.BlockSpec(memory_space=pltpu.SMEM)] * 2
    send_even, send_odd, coef = pl.pallas_call(
        lookup_kernel,
        out_shape=(shape(4, ROWS, EDGE), shape(4, ROWS, EDGE), shape(2, ROWS, COLS)),
        in_specs=smem + vmem(4),
        out_specs=vmem(3),
        compiler_params=params(),
        name="lookup",
    )(viscosity_table, drag_table, forcing, ice_mask, viscosity_class, drag_class)
    got_even = swap(send_even, "gx", 0)
    got_odd = swap(send_odd, "gx", 1)
    send_even, send_odd = pl.pallas_call(
        rows_kernel,
        out_shape=(shape(4, HALO, WIDE),) * 2,
        in_specs=vmem(4),
        out_specs=vmem(2),
        compiler_params=params(),
        name="rows",
    )(forcing, coef, got_even, got_odd)
    rows_even = swap(send_even, "gy", 0)
    rows_odd = swap(send_odd, "gy", 1)
    kept = [shape(*dims) for level in range(3) for dims in Level.shapes(level)]
    planes = [(PLANES[i], 8, LANES[i]) for i in range(3)]
    rims = [(2, PLANES[i] + 2, 8, LANES[i]) for i in range(3)]
    scratch = [pltpu.VMEM(dims, jnp.float32) for dims in [(WIDE // 128, 64, 128)] + planes * 3 + rims]
    near_lanes = 2 * LANES3 + 4 * LANES[2]
    *kept, near, far = pl.pallas_call(
        down_kernel,
        out_shape=tuple(kept) + (shape(8, near_lanes), shape(8, 2 * LANES3)),
        in_specs=vmem(6),
        out_specs=tuple(vmem(26)),
        scratch_shapes=scratch,
        compiler_params=params(),
        name="down",
    )(forcing, coef, got_even, got_odd, rows_even, rows_odd)
    near_even = swap(near, "gy", 0)
    near_odd = swap(near, "gy", 1)
    far_above = turn(far, "gy", 2)
    far_below = turn(far, "gy", -2)
    late = [(2, 2, 8, LANES[2]), (2, 4, 8, LANES[2])]
    scratch = [pltpu.VMEM(dims, jnp.float32) for dims in [(COLS // 128, ROWS, 128)] + late + rims + rims]
    return pl.pallas_call(
        up_kernel,
        out_shape=shape(2, ROWS, COLS),
        in_specs=vmem(29),
        out_specs=vmem(1)[0],
        scratch_shapes=scratch,
        compiler_params=params(),
        name="up",
    )(far, near_even, near_odd, far_above, far_below, *kept)


def solution(mesh):
    in_specs = (P(None, "gy", "gx"), P("gy", "gx"), P("gy", "gx"), P("gy", "gx"), P(), P())
    out_specs = P(None, "gy", "gx")
    return jax.shard_map(local, mesh=mesh, in_specs=in_specs, out_specs=out_specs, check_vma=False)
```

time: 580 us -> 40.9 us (0.07)
  the two profiles are of different devices: /device:TPU:128 before, /device:TPU:1 now
where the time goes in v1:
time: 40.9 us; the launch traced here: 40.7 us
  starting transfers between devices  17.8 us (44%)
  waiting for transfers between devices  9.59 us (23%)
  Pallas kernels  8.29 us (20%)
  local copies, waits for them, and re-layouts  4.97 us (12%)
    ppermute x6, starting transfers between devices, swap(): return lax.ppermute(x, axis, pairs)  16.4 us
    ppermute x6, waiting for transfers between devices, swap(): return lax.ppermute(x, axis, pairs)  7.25 us
    unnamed x14, local copies, waits for them, and re-layouts  4.97 us
    pallas_call x1, Pallas kernels, local(): pl.pallas_call(down_kernel, out_shape=tuple(kept) + (shape(8, near_lanes)...  3.99 us
    pallas_call x1, Pallas kernels, local(): pl.pallas_call(up_kernel, out_shape=shape(2, ROWS, COLS), in_specs=vmem(2...  3.45 us
    ppermute x2, waiting for transfers between devices, turn(): lax.ppermute(x, axis, [(i, (i + step) % count) for i in range(count)])  2.34 us
    ppermute x2, starting transfers between devices, turn(): lax.ppermute(x, axis, [(i, (i + step) % count) for i in range(count)])  1.47 us
  transfers between devices with their start and end apart: 8, of which 5 were waited for; matrix products, arithmetic and copies ran while one was open for 0% of the time, Pallas kernels for 0%

profile of v1, /device:TPU:1, one launch (start us, length us, event | category | flops | bytes accessed | tf_op | source)
XLA Modules:
  0.0 40.7 jit_solution(3270026247025632217)
XLA Ops:
  0.0 0.9 %copy-done = f32[2,32,1024]{2,1,0:T(8,128)S(1)} copy-done((f32[2,32,1024]{2,1,0:T(8,128)S(1)}, f32[2,32,1024]{2,1,0:T(8,128)}, u32[]{:S(2)}) %copy-start) | copy-done | bytes 262168
  1.0 0.9 %copy-done.2 = s32[32,1024]{1,0:T(8,128)S(1)} copy-done((s32[32,1024]{1,0:T(8,128)S(1)}, s32[32,1024]{1,0:T(8,128)}, u32[]{:S(2)}) %copy-start.2) | copy-done | bytes 131096
  1.9 0.9 %copy-done.3 = s32[32,1024]{1,0:T(8,128)S(1)} copy-done((s32[32,1024]{1,0:T(8,128)S(1)}, s32[32,1024]{1,0:T(8,128)}, u32[]{:S(2)}) %copy-start.3) | copy-done | bytes 131096
  2.8 0.9 %copy-done.4 = s32[32,1024]{1,0:T(8,128)S(1)} copy-done((s32[32,1024]{1,0:T(8,128)S(1)}, s32[32,1024]{1,0:T(8,128)}, u32[]{:S(2)}) %copy-start.4) | copy-done | bytes 131096
  3.7 0.7 %copy-done.5 = f32[16]{0:T(128)S(1)} copy-done((f32[16]{0:T(128)S(1)}, f32[16]{0:T(128)}, u32[]{:S(2)}) %copy-start.5) | copy-done | bytes 88
  4.3 0.7 %copy-done.6 = f32[16]{0:T(128)S(1)} copy-done((f32[16]{0:T(128)S(1)}, f32[16]{0:T(128)}, u32[]{:S(2)}) %copy-start.6) | copy-done | bytes 88
  5.0 0.8 %lookup.1 = (f32[4,32,128]{2,1,0:T(8,128)S(1)}, f32[4,32,128]{2,1,0:T(8,128)S(1)}, f32[2,32,1024]{2,1,0:T(8,128)S(1)}) custom-call(f32[16]{0:T(128)S(1)} %copy-done.5, f32[16]{0:T(128)S(1)} %copy-done.6, f32[2,32,1024]{2,1,0:T(8,128)S(1)} %copy-done, s32[32,1024]{1,0:T(8,128)S(1)} %copy-done.2, s32[32,1024]{1,0:T(8,128)S(1)} %copy-done.3, ...), custom_call_target="tpu_custom_call" | custom-call | tf_op jit(solution)/shard_map/lookup/pallas_call | solution.py:411
  5.8 2.2 %collective-permute-start = (f32[4,32,128]{2,1,0:T(8,128)S(1)}, f32[4,32,128]{2,1,0:T(8,128)S(1)}, u32[]{:S(2)}, u32[]{:S(2)}) collective-permute-start(f32[4,32,128]{2,1,0:T(8,128)S(1)} %get-tuple-element.37), channel_id=1, source_target_pairs={{0,8},{8,0},{16,24},{24,16},{32,40},{40,32},{48,56},{56,48},{64,72... | collective-permute-start | bytes 196616 | tf_op jit(solution)/shard_map/ppermute | solution.py:401
  8.0 7.2 %collective-permute-start.1 = (f32[4,32,128]{2,1,0:T(8,128)S(1)}, f32[4,32,128]{2,1,0:T(8,128)S(1)}, u32[]{:S(2)}, u32[]{:S(2)}) collective-permute-start(f32[4,32,128]{2,1,0:T(8,128)S(1)} %get-tuple-element.38), channel_id=1, source_target_pairs={{8,16},{16,8},{24,32},{32,24},{40,48},{48,40},{56,64},{64,56},{72,... | collective-permute-start | bytes 196616 | tf_op jit(solution)/shard_map/ppermute | solution.py:401
  15.2 1.6 %collective-permute-done.1.got_odd = f32[4,32,128]{2,1,0:T(8,128)S(1)} collective-permute-done((f32[4,32,128]{2,1,0:T(8,128)S(1)}, f32[4,32,128]{2,1,0:T(8,128)S(1)}, u32[]{:S(2)}, u32[]{:S(2)}) %collective-permute-start.1) | collective-permute-done | bytes 65568 | tf_op jit(solution)/shard_map/ppermute | solution.py:401
  16.8 0.1 rows.1
  16.9 1.9 %collective-permute-start.2 = (f32[4,16,1280]{2,1,0:T(8,128)S(1)}, f32[4,16,1280]{2,1,0:T(8,128)S(1)}, u32[]{:S(2)}, u32[]{:S(2)}) collective-permute-start(f32[4,16,1280]{2,1,0:T(8,128)S(1)} %get-tuple-element.39), channel_id=1, source_target_pairs={{0,1},{1,0},{2,3},{3,2},{4,5},{5,4},{6,7},{7,6},{8,9},{9,8},{10,11... | collective-permute-start | bytes 983048 | tf_op jit(solution)/shard_map/ppermute | solution.py:401
  18.8 1.2 %collective-permute-start.3 = (f32[4,16,1280]{2,1,0:T(8,128)S(1)}, f32[4,16,1280]{2,1,0:T(8,128)S(1)}, u32[]{:S(2)}, u32[]{:S(2)}) collective-permute-start(f32[4,16,1280]{2,1,0:T(8,128)S(1)} %get-tuple-element.40), channel_id=1, source_target_pairs={{1,2},{2,1},{3,4},{4,3},{5,6},{6,5},{7,0},{0,7},{9,10},{10,9},{11,... | collective-permute-start | bytes 983048 | tf_op jit(solution)/shard_map/ppermute | solution.py:401
  20.0 0.1 collective-permute-done.2.rows_even
  20.1 5.5 %collective-permute-done.3.rows_odd = f32[4,16,1280]{2,1,0:T(8,128)S(1)} collective-permute-done((f32[4,16,1280]{2,1,0:T(8,128)S(1)}, f32[4,16,1280]{2,1,0:T(8,128)S(1)}, u32[]{:S(2)}, u32[]{:S(2)}) %collective-permute-start.3) | collective-permute-done | bytes 327712 | tf_op jit(solution)/shard_map/ppermute | solution.py:401
  25.6 4.0 %down.1 = (f32[8,8,1280]{2,1,0:T(8,128)S(1)}, f32[8,8,1280]{2,1,0:T(8,128)S(1)}, f32[8,8,1280]{2,1,0:T(8,128)S(1)}, f32[8,8,1280]{2,1,0:T(8,128)S(1)}, f32[9,8,1...) custom-call(f32[2,32,1024]{2,1,0:T(8,128)S(1)} %copy-done.1, ...), custom_call_target="tpu_custom_call" | custom-call | tf_op jit(solution)/shard_map/down/pallas_call | solution.py:436
  29.6 1.0 %collective-permute-start.5 = (f32[8,2048]{1,0:T(8,128)S(1)}, f32[8,2048]{1,0:T(8,128)S(1)}, u32[]{:S(2)}, u32[]{:S(2)}) collective-permute-start(f32[8,2048]{1,0:T(8,128)S(1)} %get-tuple-element.42), channel_id=1, source_target_pairs={{1,2},{2,1},{3,4},{4,3},{5,6},{6,5},{7,0},{0,7},{9,10},{10,9},{11,... | collective-permute-start | bytes 196616 | tf_op jit(solution)/shard_map/ppermute | solution.py:401
  30.6 2.9 %collective-permute-start.4 = (f32[8,2048]{1,0:T(8,128)S(1)}, f32[8,2048]{1,0:T(8,128)S(1)}, u32[]{:S(2)}, u32[]{:S(2)}) collective-permute-start(f32[8,2048]{1,0:T(8,128)S(1)} %get-tuple-element.42), channel_id=1, source_target_pairs={{0,1},{1,0},{2,3},{3,2},{4,5},{5,4},{6,7},{7,6},{8,9},{9,8},{10,11... | collective-permute-start | bytes 196616 | tf_op jit(solution)/shard_map/ppermute | solution.py:401
  33.4 0.0 collective-permute-start.7
  33.5 1.5 %collective-permute-start.6 = (f32[8,512]{1,0:T(8,128)S(1)}, f32[8,512]{1,0:T(8,128)S(1)}, u32[]{:S(2)}, u32[]{:S(2)}) collective-permute-start(f32[8,512]{1,0:T(8,128)S(1)} %get-tuple-element.41.far), channel_id=1, source_target_pairs={{0,2},{1,3},{2,4},{3,5},{4,6},{5,7},{6,0},{7,1},{8,10},{9,11},{10,... | collective-permute-start | bytes 49160 | tf_op jit(solution)/shard_map/ppermute | solution.py:406
  34.9 1.1 %collective-permute-done.7.far_below = f32[8,512]{1,0:T(8,128)S(1)} collective-permute-done((f32[8,512]{1,0:T(8,128)S(1)}, f32[8,512]{1,0:T(8,128)S(1)}, u32[]{:S(2)}, u32[]{:S(2)}) %collective-permute-start.7) | collective-permute-done | bytes 16416 | tf_op jit(solution)/shard_map/ppermute | solution.py:406
  36.0 1.2 %collective-permute-done.6.far_above = f32[8,512]{1,0:T(8,128)S(1)} collective-permute-done((f32[8,512]{1,0:T(8,128)S(1)}, f32[8,512]{1,0:T(8,128)S(1)}, u32[]{:S(2)}, u32[]{:S(2)}) %collective-permute-start.6) | collective-permute-done | bytes 16416 | tf_op jit(solution)/shard_map/ppermute | solution.py:406
  37.3 0.0 collective-permute-done.5.near_odd
  37.3 3.4 %up.1 = f32[2,32,1024]{2,1,0:T(8,128)} custom-call(f32[8,512]{1,0:T(8,128)S(1)} %get-tuple-element.41.far, f32[8,2048]{1,0:T(8,128)S(1)} %collective-permute-done.4.near_even, f32[8,2048]{1,0:T(8,128)S(1)} %collective-permute-done.5.near_odd, f32[8,512]{1,0:T(8,128)S(1)} %collective-permute-done.6.far_above, f32[8,512]{1,0:T(8,128)S(1)} %collective-permute-done.7.far_below, ...), custom_call_target="tpu_custom_call" | custom-call | tf_op jit(solution)/shard_map/up/pallas_call | solution.py:451
  (10 shorter events, 0.0 us)
Async XLA Ops:
  0.0 0.9 %copy-start = (f32[2,32,1024]{2,1,0:T(8,128)S(1)}, f32[2,32,1024]{2,1,0:T(8,128)}, u32[]{:S(2)}) copy-start(f32[2,32,1024]{2,1,0:T(8,128)} %forcing.5) | copy-start | bytes 786436
  1.0 0.9 %copy-start.2 = (s32[32,1024]{1,0:T(8,128)S(1)}, s32[32,1024]{1,0:T(8,128)}, u32[]{:S(2)}) copy-start(s32[32,1024]{1,0:T(8,128)} %mask.1) | copy-start | bytes 393220
  1.9 0.9 %copy-start.3 = (s32[32,1024]{1,0:T(8,128)S(1)}, s32[32,1024]{1,0:T(8,128)}, u32[]{:S(2)}) copy-start(s32[32,1024]{1,0:T(8,128)} %v_class.1) | copy-start | bytes 393220
  2.8 0.9 %copy-start.4 = (s32[32,1024]{1,0:T(8,128)S(1)}, s32[32,1024]{1,0:T(8,128)}, u32[]{:S(2)}) copy-start(s32[32,1024]{1,0:T(8,128)} %d_class.1) | copy-start | bytes 393220
  3.7 0.7 %copy-start.5 = (f32[16]{0:T(128)S(1)}, f32[16]{0:T(128)}, u32[]{:S(2)}) copy-start(f32[16]{0:T(128)} %v_table.1) | copy-start | bytes 196
  4.3 0.7 %copy-start.6 = (f32[16]{0:T(128)S(1)}, f32[16]{0:T(128)}, u32[]{:S(2)}) copy-start(f32[16]{0:T(128)} %d_table.1) | copy-start | bytes 196
  5.0 11.8 %copy-start.1 = (f32[2,32,1024]{2,1,0:T(8,128)S(1)}, f32[2,32,1024]{2,1,0:T(8,128)}, u32[]{:S(2)}) copy-start(f32[2,32,1024]{2,1,0:T(8,128)} %forcing.5) | copy-start | bytes 786436
  5.8 9.4 %collective-permute-start = (f32[4,32,128]{2,1,0:T(8,128)S(1)}, f32[4,32,128]{2,1,0:T(8,128)S(1)}, u32[]{:S(2)}, u32[]{:S(2)}) collective-permute-start(f32[4,32,128]{2,1,0:T(8,128)S(1)} %get-tuple-element.37), channel_id=1, source_target_pairs={{0,8},{8,0},{16,24},{24,16},{32,40},{40,32},{48,56},{56,48},{64,72... | collective-permute-start | bytes 196616 | tf_op jit(solution)/shard_map/ppermute | solution.py:401
  8.0 8.8 %collective-permute-start.1 = (f32[4,32,128]{2,1,0:T(8,128)S(1)}, f32[4,32,128]{2,1,0:T(8,128)S(1)}, u32[]{:S(2)}, u32[]{:S(2)}) collective-permute-start(f32[4,32,128]{2,1,0:T(8,128)S(1)} %get-tuple-element.38), channel_id=1, source_target_pairs={{8,16},{16,8},{24,32},{32,24},{40,48},{48,40},{56,64},{64,56},{72,... | collective-permute-start | bytes 196616 | tf_op jit(solution)/shard_map/ppermute | solution.py:401
  16.9 3.2 %collective-permute-start.2 = (f32[4,16,1280]{2,1,0:T(8,128)S(1)}, f32[4,16,1280]{2,1,0:T(8,128)S(1)}, u32[]{:S(2)}, u32[]{:S(2)}) collective-permute-start(f32[4,16,1280]{2,1,0:T(8,128)S(1)} %get-tuple-element.39), channel_id=1, source_target_pairs={{0,1},{1,0},{2,3},{3,2},{4,5},{5,4},{6,7},{7,6},{8,9},{9,8},{10,11... | collective-permute-start | bytes 983048 | tf_op jit(solution)/shard_map/ppermute | solution.py:401
  18.8 6.8 %collective-permute-start.3 = (f32[4,16,1280]{2,1,0:T(8,128)S(1)}, f32[4,16,1280]{2,1,0:T(8,128)S(1)}, u32[]{:S(2)}, u32[]{:S(2)}) collective-permute-start(f32[4,16,1280]{2,1,0:T(8,128)S(1)} %get-tuple-element.40), channel_id=1, source_target_pairs={{1,2},{2,1},{3,4},{4,3},{5,6},{6,5},{7,0},{0,7},{9,10},{10,9},{11,... | collective-permute-start | bytes 983048 | tf_op jit(solution)/shard_map/ppermute | solution.py:401
  29.6 7.7 %collective-permute-start.5 = (f32[8,2048]{1,0:T(8,128)S(1)}, f32[8,2048]{1,0:T(8,128)S(1)}, u32[]{:S(2)}, u32[]{:S(2)}) collective-permute-start(f32[8,2048]{1,0:T(8,128)S(1)} %get-tuple-element.42), channel_id=1, source_target_pairs={{1,2},{2,1},{3,4},{4,3},{5,6},{6,5},{7,0},{0,7},{9,10},{10,9},{11,... | collective-permute-start | bytes 196616 | tf_op jit(solution)/shard_map/ppermute | solution.py:401
  30.6 6.7 %collective-permute-start.4 = (f32[8,2048]{1,0:T(8,128)S(1)}, f32[8,2048]{1,0:T(8,128)S(1)}, u32[]{:S(2)}, u32[]{:S(2)}) collective-permute-start(f32[8,2048]{1,0:T(8,128)S(1)} %get-tuple-element.42), channel_id=1, source_target_pairs={{0,1},{1,0},{2,3},{3,2},{4,5},{5,4},{6,7},{7,6},{8,9},{9,8},{10,11... | collective-permute-start | bytes 196616 | tf_op jit(solution)/shard_map/ppermute | solution.py:401
  33.4 2.6 %collective-permute-start.7 = (f32[8,512]{1,0:T(8,128)S(1)}, f32[8,512]{1,0:T(8,128)S(1)}, u32[]{:S(2)}, u32[]{:S(2)}) collective-permute-start(f32[8,512]{1,0:T(8,128)S(1)} %get-tuple-element.41.far), channel_id=1, source_target_pairs={{0,6},{1,7},{2,0},{3,1},{4,2},{5,3},{6,4},{7,5},{8,14},{9,15},{10,... | collective-permute-start | bytes 49160 | tf_op jit(solution)/shard_map/ppermute | solution.py:406
  33.5 3.8 %collective-permute-start.6 = (f32[8,512]{1,0:T(8,128)S(1)}, f32[8,512]{1,0:T(8,128)S(1)}, u32[]{:S(2)}, u32[]{:S(2)}) collective-permute-start(f32[8,512]{1,0:T(8,128)S(1)} %get-tuple-element.41.far), channel_id=1, source_target_pairs={{0,2},{1,3},{2,4},{3,5},{4,6},{5,7},{6,0},{7,1},{8,10},{9,11},{10,... | collective-permute-start | bytes 49160 | tf_op jit(solution)/shard_map/ppermute | solution.py:406

commit v2 on v1

--- a/solution.py
+++ b/solution.py
@@ -198,27 +198,73 @@
         target[p // 2] = scale * both if scale != 1.0 else both
 
 
-def lookup_kernel(v_table, d_table, forcing, mask, v_class, d_class, send_even, send_odd, coef):
+def look_up(tables, classes, ice):
     at = lane(1)
-    tables = []
-    for table in (v_table, d_table):
+    rows = []
+    for table in tables:
         row = jnp.zeros((8, 128), jnp.float32)
         for i in range(16):
             row = jnp.where(at == i, table[i], row)
-        tables.append(row)
+        rows.append(row)
+    return [pick(row, part) * ice for row, part in zip(rows, classes)]
+
+
+def start_all(pairs, sems):
+    copies = [pltpu.make_async_copy(a, b, sems.at[i]) for i, (a, b) in enumerate(pairs)]
+    for copy in copies:
+        copy.start()
+    return copies
+
+
+def edge_kernel(v_table, d_table, forcing, mask, v_class, d_class, send_even, send_odd, tables, force, ints, sems):
+    pairs = [(v_table, tables[0]), (d_table, tables[1])]
+    for side, start in enumerate((0, COLS - EDGE)):
+        cols = pl.ds(start, EDGE)
+        pairs.append((forcing.at[:, :, cols], force.at[side]))
+        for i, source in enumerate((mask, v_class, d_class)):
+            pairs.append((source.at[:, cols], ints.at[side, i]))
+    for copy in start_all(pairs, sems):
+        copy.wait()
+    even = lax.axis_index("gx") % 2 == 0
+    for r in range(0, ROWS, 8):
+        part = slice(r, r + 8)
+        sides = []
+        for side in range(2):
+            ice = ints[side, 0, part].astype(jnp.float32)
+            found = look_up(tables, [ints[side, 1, part], ints[side, 2, part]], ice)
+            sides.append([force[side, 0, part], force[side, 1, part]] + found)
+        for row in range(4):
+            send_even[row, part] = jnp.where(even, sides[1][row], sides[0][row])
+            send_odd[row, part] = jnp.where(even, sides[0][row], sides[1][row])
+
+
+def row_starts():
+    even = lax.axis_index("gy") % 2 == 0
+    first = pl.multiple_of(jnp.where(even, ROWS - HALO, 0), HALO)
+    return first, pl.multiple_of(ROWS - HALO - first, HALO)
+
+
+def lookup_kernel(v_table, d_table, forcing, mask, v_class, d_class, after, coef, send_even, send_odd, tables, ints, sems):
+    pairs = [(v_table, tables[0]), (d_table, tables[1])]
+    pairs += [(source, ints.at[i]) for i, source in enumerate((mask, v_class, d_class))]
+    starts = row_starts()
+    for start, target in zip(starts, (send_even, send_odd)):
+        pairs.append((forcing.at[:, pl.ds(start, HALO), :], target.at[0:2]))
+    copies = start_all(pairs, sems)
+    for copy in copies[:5]:
+        copy.wait()
     for r in range(0, ROWS, 8):
         for c in range(0, COLS, 128):
-            part = (pl.ds(r, 8), pl.ds(c, 128))
-            ice = mask[part].astype(jnp.float32)
-            for k, classes in enumerate((v_class, d_class)):
-                coef[(k,) + part] = pick(tables[k], classes[part]) * ice
-    even = lax.axis_index("gx") % 2 == 0
-    for k in range(2):
-        for source, row in ((forcing, k), (coef, k + 2)):
-            low = source[k, :, 0:EDGE]
-            high = source[k, :, COLS - EDGE : COLS]
-            send_even[row] = jnp.where(even, high, low)
-            send_odd[row] = jnp.where(even, low, high)
+            part = (slice(r, r + 8), slice(c, c + 128))
+            ice = ints[(0,) + part].astype(jnp.float32)
+            found = look_up(tables, [ints[(1,) + part], ints[(2,) + part]], ice)
+            for k in range(2):
+                coef[(k,) + part] = found[k]
+    for copy in copies[5:]:
+        copy.wait()
+    for start, target in zip(starts, (send_even, send_odd)):
+        for k in range(2):
+            target[2 + k] = coef[k, pl.ds(start, HALO), :]
 
 
 def side_columns(get_even, get_odd):
@@ -230,18 +276,13 @@
     return left, right
 
 
-def rows_kernel(forcing, coef, got_even, got_odd, send_even, send_odd):
-    even = lax.axis_index("gy") % 2 == 0
-    for row in range(4):
-        source = forcing if row < 2 else coef
-        top = slice(0, HALO)
-        bottom = slice(ROWS - HALO, ROWS)
-        for part, flag in ((send_even, even), (send_odd, jnp.logical_not(even))):
-            lows = side_columns(got_even[row, top], got_odd[row, top])
-            highs = side_columns(got_even[row, bottom], got_odd[row, bottom])
-            part[row, :, 0:EDGE] = jnp.where(flag, highs[0], lows[0])
-            part[row, :, WIDE - EDGE : WIDE] = jnp.where(flag, highs[1], lows[1])
-            part[row, :, EDGE : WIDE - EDGE] = jnp.where(flag, source[row % 2, bottom], source[row % 2, top])
+def corner_kernel(got_even, got_odd, send_even, send_odd):
+    for start, target in zip(row_starts(), (send_even, send_odd)):
+        rows = pl.ds(start, HALO)
+        for row in range(4):
+            left, right = side_columns(got_even[row, rows], got_odd[row, rows])
+            target[row, :, 0:EDGE] = left
+            target[row, :, EDGE : 2 * EDGE] = right
 
 
 def own_rows(a, b):
@@ -249,7 +290,7 @@
     return jnp.where(upper, pltpu.roll(a, 6, axis=0), pltpu.roll(b, 2, axis=0))
 
 
-def down_kernel(forcing, coef, got_even, got_odd, rows_even, rows_odd, *refs):
+def down_kernel(forcing, coef, got_even, got_odd, rows_even, rows_odd, corner_even, corner_odd, *refs):
     levels = [Level(PLANES[i], refs[8 * i : 8 * i + 8]) for i in range(3)]
     near, far = refs[24:26]
     natural = refs[26]
@@ -263,7 +304,12 @@
         sides = side_columns(got_even[row], got_odd[row])
         for i in range(WIDE // 128):
             cols = slice(128 * i, 128 * i + 128)
-            a, b = rows_even[row, :, cols], rows_odd[row, :, cols]
+            if 0 < i < WIDE // 128 - 1:
+                inner = slice(128 * i - 128, 128 * i)
+                a, b = rows_even[row, :, inner], rows_odd[row, :, inner]
+            else:
+                outer = slice(0, EDGE) if i == 0 else slice(EDGE, 2 * EDGE)
+                a, b = corner_even[row, :, outer], corner_odd[row, :, outer]
             natural[i, 0:HALO] = jnp.where(first, 0.0, jnp.where(even, b, a))
             natural[i, HALO + ROWS :] = jnp.where(last, 0.0, jnp.where(even, a, b))
             if i == 0:
@@ -407,27 +453,49 @@
 
 
 def local(forcing, ice_mask, viscosity_class, drag_class, viscosity_table, drag_table):
-    smem = [pl.BlockSpec(memory_space=pltpu.SMEM)] * 2
-    send_even, send_odd, coef = pl.pallas_call(
+    inputs = [
+        pltpu.with_memory_space_constraint(x, pltpu.HBM)
+        for x in (viscosity_table, drag_table, forcing, ice_mask, viscosity_class, drag_class)
+    ]
+    hbm = [pl.BlockSpec(memory_space=pltpu.HBM)] * 6
+    table = pltpu.SMEM((16,), jnp.float32)
+    send_even, send_odd = pl.pallas_call(
+        edge_kernel,
+        out_shape=(shape(4, ROWS, EDGE),) * 2,
+        in_specs=hbm,
+        out_specs=tuple(vmem(2)),
+        scratch_shapes=[
+            [table, table],
+            pltpu.VMEM((2, 2, ROWS, EDGE), jnp.float32),
+            pltpu.VMEM((2, 3, ROWS, EDGE), jnp.int32),
+            pltpu.SemaphoreType.DMA((10,)),
+        ],
+        compiler_params=params(),
+        name="edges",
+    )(*inputs)
+    got_even = swap(send_even, "gx", 0)
+    got_odd = swap(send_odd, "gx", 1)
+    coef, send_even, send_odd = pl.pallas_call(
         lookup_kernel,
-        out_shape=(shape(4, ROWS, EDGE), shape(4, ROWS, EDGE), shape(2, ROWS, COLS)),
-        in_specs=smem + vmem(4),
-        out_specs=vmem(3),
+        out_shape=(shape(2, ROWS, COLS), shape(4, HALO, COLS), shape(4, HALO, COLS)),
+        in_specs=hbm + [pl.BlockSpec(memory_space=pl.ANY)],
+        out_specs=tuple(vmem(3)),
+        scratch_shapes=[[table, table], pltpu.VMEM((3, ROWS, COLS), jnp.int32), pltpu.SemaphoreType.DMA((7,))],
         compiler_params=params(),
         name="lookup",
-    )(viscosity_table, drag_table, forcing, ice_mask, viscosity_class, drag_class)
-    got_even = swap(send_even, "gx", 0)
-    got_odd = swap(send_odd, "gx", 1)
-    send_even, send_odd = pl.pallas_call(
-        rows_kernel,
-        out_shape=(shape(4, HALO, WIDE),) * 2,
-        in_specs=vmem(4),
-        out_specs=vmem(2),
-        compiler_params=params(),
-        name="rows",
-    )(forcing, coef, got_even, got_odd)
+    )(*inputs, send_even)
     rows_even = swap(send_even, "gy", 0)
     rows_odd = swap(send_odd, "gy", 1)
+    send_even, send_odd = pl.pallas_call(
+        corner_kernel,
+        out_shape=(shape(4, HALO, 2 * EDGE),) * 2,
+        in_specs=vmem(2),
+        out_specs=tuple(vmem(2)),
+        compiler_params=params(),
+        name="corners",
+    )(got_even, got_odd)
+    corner_even = swap(send_even, "gy", 0)
+    corner_odd = swap(send_odd, "gy", 1)
     kept = [shape(*dims) for level in range(3) for dims in Level.shapes(level)]
     planes = [(PLANES[i], 8, LANES[i]) for i in range(3)]
     rims = [(2, PLANES[i] + 2, 8, LANES[i]) for i in range(3)]
@@ -436,12 +504,12 @@
     *kept, near, far = pl.pallas_call(
         down_kernel,
         out_shape=tuple(kept) + (shape(8, near_lanes), shape(8, 2 * LANES3)),
-        in_specs=vmem(6),
+        in_specs=vmem(8),
         out_specs=tuple(vmem(26)),
         scratch_shapes=scratch,
         compiler_params=params(),
         name="down",
-    )(forcing, coef, got_even, got_odd, rows_even, rows_odd)
+    )(forcing, coef, got_even, got_odd, rows_even, rows_odd, corner_even, corner_odd)
     near_even = swap(near, "gy", 0)
     near_odd = swap(near, "gy", 1)
     far_above = turn(far, "gy", 2)

time: 40.9 us -> 38.7 us (0.946)
  local copies, waits for them, and re-layouts: 4.97 us -> 0.01 us
  Pallas kernels: 8.29 us -> 9.95 us
  waiting for transfers between devices: 9.59 us -> 11.2 us
    unnamed x14 -> x2, local copies, waits for them, and re-layouts: 4.97 us -> 0.01 us
    pallas_call x2 -> x3, Pallas kernels: 0.85 us -> 2.47 us  [the longest x1 1.41 us: local(): pl.pallas_call(lookup_kernel, out_shape=(shape(2, ROWS, COLS), shape(4, H...]
    ppermute x2, waiting for transfers between devices: 2.34 us -> 3.8 us  [turn(): lax.ppermute(x, axis, [(i, (i + step) % count) for i in range(count)])]
    ppermute x6 -> x8, starting transfers between devices: 16.4 us -> 15.6 us  [swap(): return lax.ppermute(x, axis, pairs)]
    ppermute x6 -> x8, waiting for transfers between devices: 7.25 us -> 7.4 us  [swap(): return lax.ppermute(x, axis, pairs)]
  transfers between devices with their start and end apart: 8 -> 10, of which waited for: 5 -> 6; matrix products, arithmetic and copies ran while one was open for 0% -> 0% of each run, Pallas kernels for 0% -> 0%
where the time goes in v2:
time: 38.7 us; the launch traced here: 38.6 us
  starting transfers between devices  17.4 us (45%)
  waiting for transfers between devices  11.2 us (29%)
  Pallas kernels  9.95 us (26%)
    ppermute x8, starting transfers between devices, swap(): return lax.ppermute(x, axis, pairs)  15.6 us
    ppermute x8, waiting for transfers between devices, swap(): return lax.ppermute(x, axis, pairs)  7.4 us
    pallas_call x1, Pallas kernels, local(): pl.pallas_call(down_kernel, out_shape=tuple(kept) + (shape(8, near_lanes)...  4.01 us
    ppermute x2, waiting for transfers between devices, turn(): lax.ppermute(x, axis, [(i, (i + step) % count) for i in range(count)])  3.8 us
    pallas_call x1, Pallas kernels, local(): pl.pallas_call(up_kernel, out_shape=shape(2, ROWS, COLS), in_specs=vmem(2...  3.48 us
    ppermute x2, starting transfers between devices, turn(): lax.ppermute(x, axis, [(i, (i + step) % count) for i in range(count)])  1.72 us
    pallas_call x1, Pallas kernels, local(): pl.pallas_call(lookup_kernel, out_shape=(shape(2, ROWS, COLS), shape(4, H...  1.41 us
    pallas_call x1, Pallas kernels, local(): pl.pallas_call(edge_kernel, out_shape=(shape(4, ROWS, EDGE),) * 2, in_spe...  1.04 us
  transfers between devices with their start and end apart: 10, of which 6 were waited for; matrix products, arithmetic and copies ran while one was open for 0% of the time, Pallas kernels for 0%

profile of v2, /device:TPU:1, one launch (start us, length us, event | category | flops | bytes accessed | tf_op | source)
XLA Modules:
  0.0 38.6 jit_solution(12921261450365060062)
XLA Ops:
  0.0 1.0 %edges.1 = (f32[4,32,128]{2,1,0:T(8,128)S(1)}, f32[4,32,128]{2,1,0:T(8,128)S(1)}) custom-call(f32[16]{0:T(128)} %v_table.3, f32[16]{0:T(128)} %d_table.3, f32[2,32,1024]{2,1,0:T(8,128)} %forcing.5, s32[32,1024]{1,0:T(8,128)} %mask.3, s32[32,1024]{1,0:T(8,128)} %v_class.3, s32[32,1024]{1,0:T(8,128)} %d_class.3), custom_call_target="tpu_custom_call" | custom-call | tf_op jit(solution)/shard_map/edges/pallas_call | solution.py:462
  1.0 0.0 copy-start
  1.1 1.4 %lookup.1 = (f32[2,32,1024]{2,1,0:T(8,128)S(1)}, f32[4,16,1024]{2,1,0:T(8,128)S(1)}, f32[4,16,1024]{2,1,0:T(8,128)S(1)}) custom-call(f32[16]{0:T(128)} %v_table.3, f32[16]{0:T(128)} %d_table.3, f32[2,32,1024]{2,1,0:T(8,128)} %forcing.5, s32[32,1024]{1,0:T(8,128)} %mask.3, s32[32,1024]{1,0:T(8,128)} %v_class.3, s32[32,1024]{1,0:T(8,128)} %d_class.3, ...), custom_call_target="tpu_custom_call" | custom-call | tf_op jit(solution)/shard_map/lookup/pallas_call | solution.py:478
  2.5 3.3 %collective-permute-start.2 = (f32[4,16,1024]{2,1,0:T(8,128)S(1)}, f32[4,16,1024]{2,1,0:T(8,128)S(1)}, u32[]{:S(2)}, u32[]{:S(2)}) collective-permute-start(f32[4,16,1024]{2,1,0:T(8,128)S(1)} %get-tuple-element.41), channel_id=1, source_target_pairs={{0,1},{1,0},{2,3},{3,2},{4,5},{5,4},{6,7},{7,6},{8,9},{9,8},{10,11... | collective-permute-start | bytes 786440 | tf_op jit(solution)/shard_map/ppermute | solution.py:447
  5.8 0.0 collective-permute-start.3
  5.8 7.5 %collective-permute-start.1 = (f32[4,32,128]{2,1,0:T(8,128)S(1)}, f32[4,32,128]{2,1,0:T(8,128)S(1)}, u32[]{:S(2)}, u32[]{:S(2)}) collective-permute-start(f32[4,32,128]{2,1,0:T(8,128)S(1)} %get-tuple-element.40), channel_id=1, source_target_pairs={{8,16},{16,8},{24,32},{32,24},{40,48},{48,40},{56,64},{64,56},{72,... | collective-permute-start | bytes 196616 | tf_op jit(solution)/shard_map/ppermute | solution.py:447
  13.3 0.0 collective-permute-start
  13.3 1.6 %collective-permute-done.1.got_odd = f32[4,32,128]{2,1,0:T(8,128)S(1)} collective-permute-done((f32[4,32,128]{2,1,0:T(8,128)S(1)}, f32[4,32,128]{2,1,0:T(8,128)S(1)}, u32[]{:S(2)}, u32[]{:S(2)}) %collective-permute-start.1) | collective-permute-done | bytes 65568 | tf_op jit(solution)/shard_map/ppermute | solution.py:447
  15.0 1.8 %collective-permute-done.got_even = f32[4,32,128]{2,1,0:T(8,128)S(1)} collective-permute-done((f32[4,32,128]{2,1,0:T(8,128)S(1)}, f32[4,32,128]{2,1,0:T(8,128)S(1)}, u32[]{:S(2)}, u32[]{:S(2)}) %collective-permute-start) | collective-permute-done | bytes 65568 | tf_op jit(solution)/shard_map/ppermute | solution.py:447
  16.7 2.9 %collective-permute-start.4 = (f32[4,16,256]{2,1,0:T(8,128)S(1)}, f32[4,16,256]{2,1,0:T(8,128)S(1)}, u32[]{:S(2)}, u32[]{:S(2)}) collective-permute-start(f32[4,16,256]{2,1,0:T(8,128)S(1)} %get-tuple-element.43), channel_id=1, source_target_pairs={{0,1},{1,0},{2,3},{3,2},{4,5},{5,4},{6,7},{7,6},{8,9},{9,8},{10,11... | collective-permute-start | bytes 196616 | tf_op jit(solution)/shard_map/ppermute | solution.py:447
  19.6 0.0 collective-permute-start.5
  19.6 0.9 %collective-permute-done.4.corner_even = f32[4,16,256]{2,1,0:T(8,128)S(1)} collective-permute-done((f32[4,16,256]{2,1,0:T(8,128)S(1)}, f32[4,16,256]{2,1,0:T(8,128)S(1)}, u32[]{:S(2)}, u32[]{:S(2)}) %collective-permute-start.4) | collective-permute-done | bytes 65568 | tf_op jit(solution)/shard_map/ppermute | solution.py:447
  20.5 3.1 %collective-permute-done.5.corner_odd = f32[4,16,256]{2,1,0:T(8,128)S(1)} collective-permute-done((f32[4,16,256]{2,1,0:T(8,128)S(1)}, f32[4,16,256]{2,1,0:T(8,128)S(1)}, u32[]{:S(2)}, u32[]{:S(2)}) %collective-permute-start.5) | collective-permute-done | bytes 65568 | tf_op jit(solution)/shard_map/ppermute | solution.py:447
  23.6 0.0 collective-permute-done.2.rows_even
  23.6 0.0 collective-permute-done.3.rows_odd
  23.6 4.0 %down.1 = (f32[8,8,1280]{2,1,0:T(8,128)S(1)}, f32[8,8,1280]{2,1,0:T(8,128)S(1)}, f32[8,8,1280]{2,1,0:T(8,128)S(1)}, f32[8,8,1280]{2,1,0:T(8,128)S(1)}, f32[9,8,1...) custom-call(f32[2,32,1024]{2,1,0:T(8,128)S(1)} %copy-done, ...), custom_call_target="tpu_custom_call" | custom-call | tf_op jit(solution)/shard_map/down/pallas_call | solution.py:504
  27.6 0.1 collective-permute-start.7
  27.7 1.8 %collective-permute-start.6 = (f32[8,2048]{1,0:T(8,128)S(1)}, f32[8,2048]{1,0:T(8,128)S(1)}, u32[]{:S(2)}, u32[]{:S(2)}) collective-permute-start(f32[8,2048]{1,0:T(8,128)S(1)} %get-tuple-element.46), channel_id=1, source_target_pairs={{0,1},{1,0},{2,3},{3,2},{4,5},{5,4},{6,7},{7,6},{8,9},{9,8},{10,11... | collective-permute-start | bytes 196616 | tf_op jit(solution)/shard_map/ppermute | solution.py:447
  29.6 1.7 %collective-permute-start.9 = (f32[8,512]{1,0:T(8,128)S(1)}, f32[8,512]{1,0:T(8,128)S(1)}, u32[]{:S(2)}, u32[]{:S(2)}) collective-permute-start(f32[8,512]{1,0:T(8,128)S(1)} %get-tuple-element.45.far), channel_id=1, source_target_pairs={{0,6},{1,7},{2,0},{3,1},{4,2},{5,3},{6,4},{7,5},{8,14},{9,15},{10,... | collective-permute-start | bytes 49160 | tf_op jit(solution)/shard_map/ppermute | solution.py:452
  31.3 0.9 %collective-permute-done.9.far_below = f32[8,512]{1,0:T(8,128)S(1)} collective-permute-done((f32[8,512]{1,0:T(8,128)S(1)}, f32[8,512]{1,0:T(8,128)S(1)}, u32[]{:S(2)}, u32[]{:S(2)}) %collective-permute-start.9) | collective-permute-done | bytes 16416 | tf_op jit(solution)/shard_map/ppermute | solution.py:452
  32.2 2.9 %collective-permute-done.8.far_above = f32[8,512]{1,0:T(8,128)S(1)} collective-permute-done((f32[8,512]{1,0:T(8,128)S(1)}, f32[8,512]{1,0:T(8,128)S(1)}, u32[]{:S(2)}, u32[]{:S(2)}) %collective-permute-start.8) | collective-permute-done | bytes 16416 | tf_op jit(solution)/shard_map/ppermute | solution.py:452
  35.1 0.0 collective-permute-done.7.near_odd
  35.1 0.0 collective-permute-done.6.near_even
  35.1 3.5 %up.1 = f32[2,32,1024]{2,1,0:T(8,128)} custom-call(f32[8,512]{1,0:T(8,128)S(1)} %get-tuple-element.45.far, f32[8,2048]{1,0:T(8,128)S(1)} %collective-permute-done.6.near_even, f32[8,2048]{1,0:T(8,128)S(1)} %collective-permute-done.7.near_odd, f32[8,512]{1,0:T(8,128)S(1)} %collective-permute-done.8.far_above, f32[8,512]{1,0:T(8,128)S(1)} %collective-permute-done.9.far_below, ...), custom_call_target="tpu_custom_call" | custom-call | tf_op jit(solution)/shard_map/up/pallas_call | solution.py:519
  (3 shorter events, 0.0 us)
Async XLA Ops:
  1.0 22.6 %copy-start = (f32[2,32,1024]{2,1,0:T(8,128)S(1)}, f32[2,32,1024]{2,1,0:T(8,128)}, u32[]{:S(2)}) copy-start(f32[2,32,1024]{2,1,0:T(8,128)} %forcing.5) | copy-start | bytes 786436
  2.5 21.1 %collective-permute-start.2 = (f32[4,16,1024]{2,1,0:T(8,128)S(1)}, f32[4,16,1024]{2,1,0:T(8,128)S(1)}, u32[]{:S(2)}, u32[]{:S(2)}) collective-permute-start(f32[4,16,1024]{2,1,0:T(8,128)S(1)} %get-tuple-element.41), channel_id=1, source_target_pairs={{0,1},{1,0},{2,3},{3,2},{4,5},{5,4},{6,7},{7,6},{8,9},{9,8},{10,11... | collective-permute-start | bytes 786440 | tf_op jit(solution)/shard_map/ppermute | solution.py:447
  5.8 17.8 %collective-permute-start.3 = (f32[4,16,1024]{2,1,0:T(8,128)S(1)}, f32[4,16,1024]{2,1,0:T(8,128)S(1)}, u32[]{:S(2)}, u32[]{:S(2)}) collective-permute-start(f32[4,16,1024]{2,1,0:T(8,128)S(1)} %get-tuple-element.42), channel_id=1, source_target_pairs={{1,2},{2,1},{3,4},{4,3},{5,6},{6,5},{7,0},{0,7},{9,10},{10,9},{11,... | collective-permute-start | bytes 786440 | tf_op jit(solution)/shard_map/ppermute | solution.py:447
  5.8 9.1 %collective-permute-start.1 = (f32[4,32,128]{2,1,0:T(8,128)S(1)}, f32[4,32,128]{2,1,0:T(8,128)S(1)}, u32[]{:S(2)}, u32[]{:S(2)}) collective-permute-start(f32[4,32,128]{2,1,0:T(8,128)S(1)} %get-tuple-element.40), channel_id=1, source_target_pairs={{8,16},{16,8},{24,32},{32,24},{40,48},{48,40},{56,64},{64,56},{72,... | collective-permute-start | bytes 196616 | tf_op jit(solution)/shard_map/ppermute | solution.py:447
  13.3 3.4 %collective-permute-start = (f32[4,32,128]{2,1,0:T(8,128)S(1)}, f32[4,32,128]{2,1,0:T(8,128)S(1)}, u32[]{:S(2)}, u32[]{:S(2)}) collective-permute-start(f32[4,32,128]{2,1,0:T(8,128)S(1)} %get-tuple-element.38.after), channel_id=1, source_target_pairs={{0,8},{8,0},{16,24},{24,16},{32,40},{40,32},{48,56},{56,48},{64,72... | collective-permute-start | bytes 196616 | tf_op jit(solution)/shard_map/ppermute | solution.py:447
  16.7 3.8 %collective-permute-start.4 = (f32[4,16,256]{2,1,0:T(8,128)S(1)}, f32[4,16,256]{2,1,0:T(8,128)S(1)}, u32[]{:S(2)}, u32[]{:S(2)}) collective-permute-start(f32[4,16,256]{2,1,0:T(8,128)S(1)} %get-tuple-element.43), channel_id=1, source_target_pairs={{0,1},{1,0},{2,3},{3,2},{4,5},{5,4},{6,7},{7,6},{8,9},{9,8},{10,11... | collective-permute-start | bytes 196616 | tf_op jit(solution)/shard_map/ppermute | solution.py:447
  19.6 4.0 %collective-permute-start.5 = (f32[4,16,256]{2,1,0:T(8,128)S(1)}, f32[4,16,256]{2,1,0:T(8,128)S(1)}, u32[]{:S(2)}, u32[]{:S(2)}) collective-permute-start(f32[4,16,256]{2,1,0:T(8,128)S(1)} %get-tuple-element.44), channel_id=1, source_target_pairs={{1,2},{2,1},{3,4},{4,3},{5,6},{6,5},{7,0},{0,7},{9,10},{10,9},{11,... | collective-permute-start | bytes 196616 | tf_op jit(solution)/shard_map/ppermute | solution.py:447
  27.6 7.5 %collective-permute-start.7 = (f32[8,2048]{1,0:T(8,128)S(1)}, f32[8,2048]{1,0:T(8,128)S(1)}, u32[]{:S(2)}, u32[]{:S(2)}) collective-permute-start(f32[8,2048]{1,0:T(8,128)S(1)} %get-tuple-element.46), channel_id=1, source_target_pairs={{1,2},{2,1},{3,4},{4,3},{5,6},{6,5},{7,0},{0,7},{9,10},{10,9},{11,... | collective-permute-start | bytes 196616 | tf_op jit(solution)/shard_map/ppermute | solution.py:447
  27.7 7.4 %collective-permute-start.6 = (f32[8,2048]{1,0:T(8,128)S(1)}, f32[8,2048]{1,0:T(8,128)S(1)}, u32[]{:S(2)}, u32[]{:S(2)}) collective-permute-start(f32[8,2048]{1,0:T(8,128)S(1)} %get-tuple-element.46), channel_id=1, source_target_pairs={{0,1},{1,0},{2,3},{3,2},{4,5},{5,4},{6,7},{7,6},{8,9},{9,8},{10,11... | collective-permute-start | bytes 196616 | tf_op jit(solution)/shard_map/ppermute | solution.py:447
  29.6 2.6 %collective-permute-start.9 = (f32[8,512]{1,0:T(8,128)S(1)}, f32[8,512]{1,0:T(8,128)S(1)}, u32[]{:S(2)}, u32[]{:S(2)}) collective-permute-start(f32[8,512]{1,0:T(8,128)S(1)} %get-tuple-element.45.far), channel_id=1, source_target_pairs={{0,6},{1,7},{2,0},{3,1},{4,2},{5,3},{6,4},{7,5},{8,14},{9,15},{10,... | collective-permute-start | bytes 49160 | tf_op jit(solution)/shard_map/ppermute | solution.py:452
  31.3 3.8 %collective-permute-start.8 = (f32[8,512]{1,0:T(8,128)S(1)}, f32[8,512]{1,0:T(8,128)S(1)}, u32[]{:S(2)}, u32[]{:S(2)}) collective-permute-start(f32[8,512]{1,0:T(8,128)S(1)} %get-tuple-element.45.far), channel_id=1, source_target_pairs={{0,2},{1,3},{2,4},{3,5},{4,6},{5,7},{6,0},{7,1},{8,10},{9,11},{10,... | collective-permute-start | bytes 49160 | tf_op jit(solution)/shard_map/ppermute | solution.py:452

commit v3 on v2

--- a/solution.py
+++ b/solution.py
@@ -439,12 +439,18 @@
 
 
 def swap(x, axis, odd):
-    count = lax.axis_size(axis)
+    rows, cols = lax.axis_size("gy"), lax.axis_size("gx")
+    count, across = (rows, cols) if axis == "gy" else (cols, rows)
     pairs = []
-    for i in range(odd, count, 2):
-        j = (i + 1) % count
-        pairs += [(i, j), (j, i)]
-    return lax.ppermute(x, axis, pairs)
+    for j in range(across):
+        for i in range(odd, count - 1, 2):
+            pairs += [((i, j), (i + 1, j)), ((i + 1, j), (i, j))]
+        if odd and axis == "gy":
+            pairs += [((0, j), (count - 1, j)), ((count - 1, j), (0, j))]
+        elif odd:
+            pairs += [((i, j), (i, j ^ 1)) for i in (0, count - 1)]
+    place = (lambda i, j: j * rows + i) if axis == "gy" else (lambda i, j: i * rows + j)
+    return lax.ppermute(x, ("gx", "gy"), [(place(*a), place(*b)) for a, b in pairs])
 
 
 def turn(x, axis, step):
@@ -482,6 +488,7 @@
         out_specs=tuple(vmem(3)),
         scratch_shapes=[[table, table], pltpu.VMEM((3, ROWS, COLS), jnp.int32), pltpu.SemaphoreType.DMA((7,))],
         compiler_params=params(),
+        cost_estimate=pl.CostEstimate(flops=1 << 22, bytes_accessed=8 << 20, transcendentals=0),
         name="lookup",
     )(*inputs, send_even)
     rows_even = swap(send_even, "gy", 0)

time: 38.7 us -> 34.3 us (0.89)
  the two profiles are of different devices: /device:TPU:1 before, /device:TPU:128 now
where the time goes in v3:
time: 34.3 us; the launch traced here: 34 us
  waiting for transfers between devices  13.4 us (39%)
  starting transfers between devices  10.5 us (31%)
  Pallas kernels  9.95 us (29%)
    ppermute x8, waiting for transfers between devices, swap(): lax.ppermute(x, ('gx', 'gy'), [(place(*a), place(*b)) for a, b in pairs])  8.5 us
    ppermute x8, starting transfers between devices, swap(): lax.ppermute(x, ('gx', 'gy'), [(place(*a), place(*b)) for a, b in pairs])  8.04 us
    ppermute x2, waiting for transfers between devices, turn(): lax.ppermute(x, axis, [(i, (i + step) % count) for i in range(count)])  4.95 us
    pallas_call x1, Pallas kernels, local(): pl.pallas_call(down_kernel, out_shape=tuple(kept) + (shape(8, near_lanes)...  4.01 us
    pallas_call x1, Pallas kernels, local(): pl.pallas_call(up_kernel, out_shape=shape(2, ROWS, COLS), in_specs=vmem(2...  3.48 us
    ppermute x2, starting transfers between devices, turn(): lax.ppermute(x, axis, [(i, (i + step) % count) for i in range(count)])  2.51 us
    pallas_call x1, Pallas kernels, local(): pl.pallas_call(lookup_kernel, out_shape=(shape(2, ROWS, COLS), shape(4, H...  1.41 us
    pallas_call x1, Pallas kernels, local(): pl.pallas_call(edge_kernel, out_shape=(shape(4, ROWS, EDGE),) * 2, in_spe...  1.04 us
  transfers between devices with their start and end apart: 10, of which 5 were waited for; matrix products, arithmetic and copies ran while one was open for 0% of the time, Pallas kernels for 0%

profile of v3, /device:TPU:128, one launch (start us, length us, event | category | flops | bytes accessed | tf_op | source)
XLA Modules:
  0.0 34.0 jit_solution(12313509094935410348)
XLA Ops:
  0.0 1.0 %edges.1 = (f32[4,32,128]{2,1,0:T(8,128)S(1)}, f32[4,32,128]{2,1,0:T(8,128)S(1)}) custom-call(f32[16]{0:T(128)} %v_table.3, f32[16]{0:T(128)} %d_table.3, f32[2,32,1024]{2,1,0:T(8,128)} %forcing.5, s32[32,1024]{1,0:T(8,128)} %mask.3, s32[32,1024]{1,0:T(8,128)} %v_class.3, s32[32,1024]{1,0:T(8,128)} %d_class.3), custom_call_target="tpu_custom_call" | custom-call | tf_op jit(solution)/shard_map/edges/pallas_call | solution.py:468
  1.0 0.0 copy-start
  1.1 1.4 %lookup.1 = (f32[2,32,1024]{2,1,0:T(8,128)S(1)}, f32[4,16,1024]{2,1,0:T(8,128)S(1)}, f32[4,16,1024]{2,1,0:T(8,128)S(1)}) custom-call(f32[16]{0:T(128)} %v_table.3, f32[16]{0:T(128)} %d_table.3, f32[2,32,1024]{2,1,0:T(8,128)} %forcing.5, s32[32,1024]{1,0:T(8,128)} %mask.3, s32[32,1024]{1,0:T(8,128)} %v_class.3, s32[32,1024]{1,0:T(8,128)} %d_class.3, ...), custom_call_target="tpu_custom_call" | custom-call | flops 4194304 | bytes 8388608 | tf_op jit(solution)/shard_map/lookup/pallas_call | solution.py:484
  2.5 0.1 collective-permute-start.2
  2.6 2.9 %collective-permute-start.3 = (f32[4,16,1024]{2,1,0:T(8,128)S(1)}, f32[4,16,1024]{2,1,0:T(8,128)S(1)}, u32[]{:S(2)}, u32[]{:S(2)}) collective-permute-start(f32[4,16,1024]{2,1,0:T(8,128)S(1)} %get-tuple-element.42), channel_id=1, source_target_pairs={{1,2},{2,1},{3,4},{4,3},{5,6},{6,5},{0,7},{7,0},{9,10},{10,9},{11,... | collective-permute-start | bytes 786440 | tf_op jit(solution)/shard_map/ppermute | solution.py:453
  5.4 2.6 %collective-permute-start.1 = (f32[4,32,128]{2,1,0:T(8,128)S(1)}, f32[4,32,128]{2,1,0:T(8,128)S(1)}, u32[]{:S(2)}, u32[]{:S(2)}) collective-permute-start(f32[4,32,128]{2,1,0:T(8,128)S(1)} %get-tuple-element.40), channel_id=1, source_target_pairs={{8,16},{16,8},{24,32},{32,24},{40,48},{48,40},{56,64},{64,56},{72,... | collective-permute-start | bytes 196616 | tf_op jit(solution)/shard_map/ppermute | solution.py:453
  8.0 0.6 %collective-permute-start = (f32[4,32,128]{2,1,0:T(8,128)S(1)}, f32[4,32,128]{2,1,0:T(8,128)S(1)}, u32[]{:S(2)}, u32[]{:S(2)}) collective-permute-start(f32[4,32,128]{2,1,0:T(8,128)S(1)} %get-tuple-element.38.after), channel_id=1, source_target_pairs={{0,8},{8,0},{16,24},{24,16},{32,40},{40,32},{48,56},{56,48},{64,72... | collective-permute-start | bytes 196616 | tf_op jit(solution)/shard_map/ppermute | solution.py:453
  8.6 4.4 %collective-permute-done.1.got_odd = f32[4,32,128]{2,1,0:T(8,128)S(1)} collective-permute-done((f32[4,32,128]{2,1,0:T(8,128)S(1)}, f32[4,32,128]{2,1,0:T(8,128)S(1)}, u32[]{:S(2)}, u32[]{:S(2)}) %collective-permute-start.1) | collective-permute-done | bytes 65568 | tf_op jit(solution)/shard_map/ppermute | solution.py:453
  13.0 0.0 collective-permute-done.got_even
  13.1 0.1 collective-permute-start.4
  13.2 0.9 %collective-permute-start.5 = (f32[4,16,256]{2,1,0:T(8,128)S(1)}, f32[4,16,256]{2,1,0:T(8,128)S(1)}, u32[]{:S(2)}, u32[]{:S(2)}) collective-permute-start(f32[4,16,256]{2,1,0:T(8,128)S(1)} %get-tuple-element.44), channel_id=1, source_target_pairs={{1,2},{2,1},{3,4},{4,3},{5,6},{6,5},{0,7},{7,0},{9,10},{10,9},{11,... | collective-permute-start | bytes 196616 | tf_op jit(solution)/shard_map/ppermute | solution.py:453
  14.1 0.3 collective-permute-done.4.corner_even
  14.4 3.7 %collective-permute-done.5.corner_odd = f32[4,16,256]{2,1,0:T(8,128)S(1)} collective-permute-done((f32[4,16,256]{2,1,0:T(8,128)S(1)}, f32[4,16,256]{2,1,0:T(8,128)S(1)}, u32[]{:S(2)}, u32[]{:S(2)}) %collective-permute-start.5) | collective-permute-done | bytes 65568 | tf_op jit(solution)/shard_map/ppermute | solution.py:453
  18.1 0.0 collective-permute-done.2.rows_even
  18.1 0.0 collective-permute-done.3.rows_odd
  18.2 4.0 %down.1 = (f32[8,8,1280]{2,1,0:T(8,128)S(1)}, f32[8,8,1280]{2,1,0:T(8,128)S(1)}, f32[8,8,1280]{2,1,0:T(8,128)S(1)}, f32[8,8,1280]{2,1,0:T(8,128)S(1)}, f32[9,8,1...) custom-call(f32[2,32,1024]{2,1,0:T(8,128)S(1)} %copy-done, ...), custom_call_target="tpu_custom_call" | custom-call | tf_op jit(solution)/shard_map/down/pallas_call | solution.py:511
  22.2 0.9 %collective-permute-start.7 = (f32[8,2048]{1,0:T(8,128)S(1)}, f32[8,2048]{1,0:T(8,128)S(1)}, u32[]{:S(2)}, u32[]{:S(2)}) collective-permute-start(f32[8,2048]{1,0:T(8,128)S(1)} %get-tuple-element.46), channel_id=1, source_target_pairs={{1,2},{2,1},{3,4},{4,3},{5,6},{6,5},{0,7},{7,0},{9,10},{10,9},{11,... | collective-permute-start | bytes 196616 | tf_op jit(solution)/shard_map/ppermute | solution.py:453
  23.1 0.0 collective-permute-start.6
  23.1 2.5 %collective-permute-start.9 = (f32[8,512]{1,0:T(8,128)S(1)}, f32[8,512]{1,0:T(8,128)S(1)}, u32[]{:S(2)}, u32[]{:S(2)}) collective-permute-start(f32[8,512]{1,0:T(8,128)S(1)} %get-tuple-element.45.far), channel_id=1, source_target_pairs={{0,6},{1,7},{2,0},{3,1},{4,2},{5,3},{6,4},{7,5},{8,14},{9,15},{10,... | collective-permute-start | bytes 49160 | tf_op jit(solution)/shard_map/ppermute | solution.py:458
  25.6 0.0 collective-permute-start.8
  25.6 1.4 %collective-permute-done.9.far_below = f32[8,512]{1,0:T(8,128)S(1)} collective-permute-done((f32[8,512]{1,0:T(8,128)S(1)}, f32[8,512]{1,0:T(8,128)S(1)}, u32[]{:S(2)}, u32[]{:S(2)}) %collective-permute-start.9) | collective-permute-done | bytes 16416 | tf_op jit(solution)/shard_map/ppermute | solution.py:458
  27.0 3.5 %collective-permute-done.8.far_above = f32[8,512]{1,0:T(8,128)S(1)} collective-permute-done((f32[8,512]{1,0:T(8,128)S(1)}, f32[8,512]{1,0:T(8,128)S(1)}, u32[]{:S(2)}, u32[]{:S(2)}) %collective-permute-start.8) | collective-permute-done | bytes 16416 | tf_op jit(solution)/shard_map/ppermute | solution.py:458
  30.5 0.0 collective-permute-done.7.near_odd
  30.5 3.5 %up.1 = f32[2,32,1024]{2,1,0:T(8,128)} custom-call(f32[8,512]{1,0:T(8,128)S(1)} %get-tuple-element.45.far, f32[8,2048]{1,0:T(8,128)S(1)} %collective-permute-done.6.near_even, f32[8,2048]{1,0:T(8,128)S(1)} %collective-permute-done.7.near_odd, f32[8,512]{1,0:T(8,128)S(1)} %collective-permute-done.8.far_above, f32[8,512]{1,0:T(8,128)S(1)} %collective-permute-done.9.far_below, ...), custom_call_target="tpu_custom_call" | custom-call | tf_op jit(solution)/shard_map/up/pallas_call | solution.py:526
  (3 shorter events, 0.0 us)
Async XLA Ops:
  1.0 17.1 %copy-start = (f32[2,32,1024]{2,1,0:T(8,128)S(1)}, f32[2,32,1024]{2,1,0:T(8,128)}, u32[]{:S(2)}) copy-start(f32[2,32,1024]{2,1,0:T(8,128)} %forcing.5) | copy-start | bytes 786436
  2.5 15.7 %collective-permute-start.2 = (f32[4,16,1024]{2,1,0:T(8,128)S(1)}, f32[4,16,1024]{2,1,0:T(8,128)S(1)}, u32[]{:S(2)}, u32[]{:S(2)}) collective-permute-start(f32[4,16,1024]{2,1,0:T(8,128)S(1)} %get-tuple-element.41), channel_id=1, source_target_pairs={{0,1},{1,0},{2,3},{3,2},{4,5},{5,4},{6,7},{7,6},{8,9},{9,8},{10,11... | collective-permute-start | bytes 786440 | tf_op jit(solution)/shard_map/ppermute | solution.py:453
  2.6 15.6 %collective-permute-start.3 = (f32[4,16,1024]{2,1,0:T(8,128)S(1)}, f32[4,16,1024]{2,1,0:T(8,128)S(1)}, u32[]{:S(2)}, u32[]{:S(2)}) collective-permute-start(f32[4,16,1024]{2,1,0:T(8,128)S(1)} %get-tuple-element.42), channel_id=1, source_target_pairs={{1,2},{2,1},{3,4},{4,3},{5,6},{6,5},{0,7},{7,0},{9,10},{10,9},{11,... | collective-permute-start | bytes 786440 | tf_op jit(solution)/shard_map/ppermute | solution.py:453
  5.4 7.6 %collective-permute-start.1 = (f32[4,32,128]{2,1,0:T(8,128)S(1)}, f32[4,32,128]{2,1,0:T(8,128)S(1)}, u32[]{:S(2)}, u32[]{:S(2)}) collective-permute-start(f32[4,32,128]{2,1,0:T(8,128)S(1)} %get-tuple-element.40), channel_id=1, source_target_pairs={{8,16},{16,8},{24,32},{32,24},{40,48},{48,40},{56,64},{64,56},{72,... | collective-permute-start | bytes 196616 | tf_op jit(solution)/shard_map/ppermute | solution.py:453
  8.0 5.0 %collective-permute-start = (f32[4,32,128]{2,1,0:T(8,128)S(1)}, f32[4,32,128]{2,1,0:T(8,128)S(1)}, u32[]{:S(2)}, u32[]{:S(2)}) collective-permute-start(f32[4,32,128]{2,1,0:T(8,128)S(1)} %get-tuple-element.38.after), channel_id=1, source_target_pairs={{0,8},{8,0},{16,24},{24,16},{32,40},{40,32},{48,56},{56,48},{64,72... | collective-permute-start | bytes 196616 | tf_op jit(solution)/shard_map/ppermute | solution.py:453
  13.1 1.3 %collective-permute-start.4 = (f32[4,16,256]{2,1,0:T(8,128)S(1)}, f32[4,16,256]{2,1,0:T(8,128)S(1)}, u32[]{:S(2)}, u32[]{:S(2)}) collective-permute-start(f32[4,16,256]{2,1,0:T(8,128)S(1)} %get-tuple-element.43), channel_id=1, source_target_pairs={{0,1},{1,0},{2,3},{3,2},{4,5},{5,4},{6,7},{7,6},{8,9},{9,8},{10,11... | collective-permute-start | bytes 196616 | tf_op jit(solution)/shard_map/ppermute | solution.py:453
  13.2 5.0 %collective-permute-start.5 = (f32[4,16,256]{2,1,0:T(8,128)S(1)}, f32[4,16,256]{2,1,0:T(8,128)S(1)}, u32[]{:S(2)}, u32[]{:S(2)}) collective-permute-start(f32[4,16,256]{2,1,0:T(8,128)S(1)} %get-tuple-element.44), channel_id=1, source_target_pairs={{1,2},{2,1},{3,4},{4,3},{5,6},{6,5},{0,7},{7,0},{9,10},{10,9},{11,... | collective-permute-start | bytes 196616 | tf_op jit(solution)/shard_map/ppermute | solution.py:453
  22.2 8.4 %collective-permute-start.7 = (f32[8,2048]{1,0:T(8,128)S(1)}, f32[8,2048]{1,0:T(8,128)S(1)}, u32[]{:S(2)}, u32[]{:S(2)}) collective-permute-start(f32[8,2048]{1,0:T(8,128)S(1)} %get-tuple-element.46), channel_id=1, source_target_pairs={{1,2},{2,1},{3,4},{4,3},{5,6},{6,5},{0,7},{7,0},{9,10},{10,9},{11,... | collective-permute-start | bytes 196616 | tf_op jit(solution)/shard_map/ppermute | solution.py:453
  23.1 7.5 %collective-permute-start.6 = (f32[8,2048]{1,0:T(8,128)S(1)}, f32[8,2048]{1,0:T(8,128)S(1)}, u32[]{:S(2)}, u32[]{:S(2)}) collective-permute-start(f32[8,2048]{1,0:T(8,128)S(1)} %get-tuple-element.46), channel_id=1, source_target_pairs={{0,1},{1,0},{2,3},{3,2},{4,5},{5,4},{6,7},{7,6},{8,9},{9,8},{10,11... | collective-permute-start | bytes 196616 | tf_op jit(solution)/shard_map/ppermute | solution.py:453
  23.1 4.0 %collective-permute-start.9 = (f32[8,512]{1,0:T(8,128)S(1)}, f32[8,512]{1,0:T(8,128)S(1)}, u32[]{:S(2)}, u32[]{:S(2)}) collective-permute-start(f32[8,512]{1,0:T(8,128)S(1)} %get-tuple-element.45.far), channel_id=1, source_target_pairs={{0,6},{1,7},{2,0},{3,1},{4,2},{5,3},{6,4},{7,5},{8,14},{9,15},{10,... | collective-permute-start | bytes 49160 | tf_op jit(solution)/shard_map/ppermute | solution.py:458
  25.6 4.9 %collective-permute-start.8 = (f32[8,512]{1,0:T(8,128)S(1)}, f32[8,512]{1,0:T(8,128)S(1)}, u32[]{:S(2)}, u32[]{:S(2)}) collective-permute-start(f32[8,512]{1,0:T(8,128)S(1)} %get-tuple-element.45.far), channel_id=1, source_target_pairs={{0,2},{1,3},{2,4},{3,5},{4,6},{5,7},{6,0},{7,1},{8,10},{9,11},{10,... | collective-permute-start | bytes 49160 | tf_op jit(solution)/shard_map/ppermute | solution.py:458

commit v4 on v3

--- a/solution.py
+++ b/solution.py
@@ -216,39 +216,22 @@
     return copies
 
 
-def edge_kernel(v_table, d_table, forcing, mask, v_class, d_class, send_even, send_odd, tables, force, ints, sems):
-    pairs = [(v_table, tables[0]), (d_table, tables[1])]
-    for side, start in enumerate((0, COLS - EDGE)):
-        cols = pl.ds(start, EDGE)
-        pairs.append((forcing.at[:, :, cols], force.at[side]))
-        for i, source in enumerate((mask, v_class, d_class)):
-            pairs.append((source.at[:, cols], ints.at[side, i]))
-    for copy in start_all(pairs, sems):
-        copy.wait()
-    even = lax.axis_index("gx") % 2 == 0
-    for r in range(0, ROWS, 8):
-        part = slice(r, r + 8)
-        sides = []
-        for side in range(2):
-            ice = ints[side, 0, part].astype(jnp.float32)
-            found = look_up(tables, [ints[side, 1, part], ints[side, 2, part]], ice)
-            sides.append([force[side, 0, part], force[side, 1, part]] + found)
-        for row in range(4):
-            send_even[row, part] = jnp.where(even, sides[1][row], sides[0][row])
-            send_odd[row, part] = jnp.where(even, sides[0][row], sides[1][row])
-
-
-def row_starts():
-    even = lax.axis_index("gy") % 2 == 0
-    first = pl.multiple_of(jnp.where(even, ROWS - HALO, 0), HALO)
-    return first, pl.multiple_of(ROWS - HALO - first, HALO)
-
-
-def lookup_kernel(v_table, d_table, forcing, mask, v_class, d_class, after, coef, send_even, send_odd, tables, ints, sems):
+def halves_of(axis, size, part):
+    even = lax.axis_index(axis) % 2 == 0
+    first = pl.multiple_of(jnp.where(even, size - part, 0), part)
+    return first, pl.multiple_of(size - part - first, part)
+
+
+def lookup_kernel(v_table, d_table, forcing, mask, v_class, d_class, coef, *refs):
+    sides, rows = refs[0:2], refs[2:4]
+    tables, ints, sems = refs[4:]
     pairs = [(v_table, tables[0]), (d_table, tables[1])]
     pairs += [(source, ints.at[i]) for i, source in enumerate((mask, v_class, d_class))]
-    starts = row_starts()
-    for start, target in zip(starts, (send_even, send_odd)):
+    side_starts = halves_of("gx", COLS, EDGE)
+    row_starts = halves_of("gy", ROWS, HALO)
+    for start, target in zip(side_starts, sides):
+        pairs.append((forcing.at[:, :, pl.ds(start, EDGE)], target.at[0:2]))
+    for start, target in zip(row_starts, rows):
         pairs.append((forcing.at[:, pl.ds(start, HALO), :], target.at[0:2]))
     copies = start_all(pairs, sems)
     for copy in copies[:5]:
@@ -260,11 +243,13 @@
             found = look_up(tables, [ints[(1,) + part], ints[(2,) + part]], ice)
             for k in range(2):
                 coef[(k,) + part] = found[k]
+    for k in range(2):
+        for start, target in zip(side_starts, sides):
+            target[2 + k] = coef[k, :, pl.ds(start, EDGE)]
+        for start, target in zip(row_starts, rows):
+            target[2 + k] = coef[k, pl.ds(start, HALO), :]
     for copy in copies[5:]:
         copy.wait()
-    for start, target in zip(starts, (send_even, send_odd)):
-        for k in range(2):
-            target[2 + k] = coef[k, pl.ds(start, HALO), :]
 
 
 def side_columns(get_even, get_odd):
@@ -277,7 +262,7 @@
 
 
 def corner_kernel(got_even, got_odd, send_even, send_odd):
-    for start, target in zip(row_starts(), (send_even, send_odd)):
+    for start, target in zip(halves_of("gy", ROWS, HALO), (send_even, send_odd)):
         rows = pl.ds(start, HALO)
         for row in range(4):
             left, right = side_columns(got_even[row, rows], got_odd[row, rows])
@@ -465,34 +450,18 @@
     ]
     hbm = [pl.BlockSpec(memory_space=pltpu.HBM)] * 6
     table = pltpu.SMEM((16,), jnp.float32)
-    send_even, send_odd = pl.pallas_call(
-        edge_kernel,
-        out_shape=(shape(4, ROWS, EDGE),) * 2,
+    coef, side_even, side_odd, main_even, main_odd = pl.pallas_call(
+        lookup_kernel,
+        out_shape=(shape(2, ROWS, COLS),) + (shape(4, ROWS, EDGE),) * 2 + (shape(4, HALO, COLS),) * 2,
         in_specs=hbm,
-        out_specs=tuple(vmem(2)),
-        scratch_shapes=[
-            [table, table],
-            pltpu.VMEM((2, 2, ROWS, EDGE), jnp.float32),
-            pltpu.VMEM((2, 3, ROWS, EDGE), jnp.int32),
-            pltpu.SemaphoreType.DMA((10,)),
-        ],
+        out_specs=tuple(vmem(5)),
+        scratch_shapes=[[table, table], pltpu.VMEM((3, ROWS, COLS), jnp.int32), pltpu.SemaphoreType.DMA((9,))],
         compiler_params=params(),
-        name="edges",
+        name="lookup",
     )(*inputs)
-    got_even = swap(send_even, "gx", 0)
-    got_odd = swap(send_odd, "gx", 1)
-    coef, send_even, send_odd = pl.pallas_call(
-        lookup_kernel,
-        out_shape=(shape(2, ROWS, COLS), shape(4, HALO, COLS), shape(4, HALO, COLS)),
-        in_specs=hbm + [pl.BlockSpec(memory_space=pl.ANY)],
-        out_specs=tuple(vmem(3)),
-        scratch_shapes=[[table, table], pltpu.VMEM((3, ROWS, COLS), jnp.int32), pltpu.SemaphoreType.DMA((7,))],
-        compiler_params=params(),
-        cost_estimate=pl.CostEstimate(flops=1 << 22, bytes_accessed=8 << 20, transcendentals=0),
-        name="lookup",
-    )(*inputs, send_even)
-    rows_even = swap(send_even, "gy", 0)
-    rows_odd = swap(send_odd, "gy", 1)
+    got_even = swap(side_even, "gx", 0)
+    got_odd = swap(side_odd, "gx", 1)
+    rows_odd = swap(main_odd, "gy", 1)
     send_even, send_odd = pl.pallas_call(
         corner_kernel,
         out_shape=(shape(4, HALO, 2 * EDGE),) * 2,
@@ -501,6 +470,8 @@
         compiler_params=params(),
         name="corners",
     )(got_even, got_odd)
+    main_even, send_even = lax.optimization_barrier((main_even, send_even))
+    rows_even = swap(main_even, "gy", 0)
     corner_even = swap(send_even, "gy", 0)
     corner_odd = swap(send_odd, "gy", 1)
     kept = [shape(*dims) for level in range(3) for dims in Level.shapes(level)]

time: 34.3 us -> 32.2 us (0.939)
  waiting for transfers between devices: 13.4 us -> 10.5 us
  starting transfers between devices: 10.5 us -> 12.6 us
  Pallas kernels: 9.95 us -> 9 us
    ppermute x8, starting transfers between devices: 8.04 us -> 10.6 us  [swap(): lax.ppermute(x, ('gx', 'gy'), [(place(*a), place(*b)) for a, b in pairs])]
    ppermute x8, waiting for transfers between devices: 8.5 us -> 6.68 us  [swap(): lax.ppermute(x, ('gx', 'gy'), [(place(*a), place(*b)) for a, b in pairs])]
    ppermute x2, waiting for transfers between devices: 4.95 us -> 3.81 us  [turn(): lax.ppermute(x, axis, [(i, (i + step) % count) for i in range(count)])]
    pallas_call x2 -> x1, Pallas kernels: 2.45 us -> 1.5 us  [local(): pl.pallas_call(lookup_kernel, out_shape=(shape(2, ROWS, COLS),) + (shape(...]
    ppermute x2, starting transfers between devices: 2.51 us -> 2.03 us  [turn(): lax.ppermute(x, axis, [(i, (i + step) % count) for i in range(count)])]
  transfers between devices with their start and end apart: 10 -> 10, of which waited for: 5 -> 4; matrix products, arithmetic and copies ran while one was open for 0% -> 0% of each run, Pallas kernels for 0% -> 0%
where the time goes in v4:
time: 32.2 us; the launch traced here: 32.1 us
  starting transfers between devices  12.6 us (39%)
  waiting for transfers between devices  10.5 us (33%)
  Pallas kernels  9 us (28%)
    ppermute x8, starting transfers between devices, swap(): lax.ppermute(x, ('gx', 'gy'), [(place(*a), place(*b)) for a, b in pairs])  10.6 us
    ppermute x8, waiting for transfers between devices, swap(): lax.ppermute(x, ('gx', 'gy'), [(place(*a), place(*b)) for a, b in pairs])  6.68 us
    pallas_call x1, Pallas kernels, local(): pl.pallas_call(down_kernel, out_shape=tuple(kept) + (shape(8, near_lanes)...  4.01 us
    ppermute x2, waiting for transfers between devices, turn(): lax.ppermute(x, axis, [(i, (i + step) % count) for i in range(count)])  3.81 us
    pallas_call x1, Pallas kernels, local(): pl.pallas_call(up_kernel, out_shape=shape(2, ROWS, COLS), in_specs=vmem(2...  3.48 us
    ppermute x2, starting transfers between devices, turn(): lax.ppermute(x, axis, [(i, (i + step) % count) for i in range(count)])  2.03 us
    pallas_call x1, Pallas kernels, local(): pl.pallas_call(lookup_kernel, out_shape=(shape(2, ROWS, COLS),) + (shape(...  1.5 us
  transfers between devices with their start and end apart: 10, of which 4 were waited for; matrix products, arithmetic and copies ran while one was open for 0% of the time, Pallas kernels for 0%

profile of v4, /device:TPU:128, one launch (start us, length us, event | category | flops | bytes accessed | tf_op | source)
XLA Modules:
  0.0 32.1 jit_solution(2913548373552138503)
XLA Ops:
  0.0 1.5 %lookup.1 = (f32[2,32,1024]{2,1,0:T(8,128)S(1)}, f32[4,32,128]{2,1,0:T(8,128)S(1)}, f32[4,32,128]{2,1,0:T(8,128)S(1)}, f32[4,16,1024]{2,1,0:T(8,128)S(1)}, f32[4,16,1024]{2,1,0:T(8,128)S(1)}) custom-call(f32[16]{0:T(128)} %v_table.1, f32[16]{0:T(128)} %d_table.1, f32[2,32,1024]{2,1,0:T(8,128)} %forcing.3, s32[32,1024]{1,0:T(8,128)} %mask.1, ...), custom_call_target="tpu_custom_call" | custom-call | tf_op jit(solution)/shard_map/lookup/pallas_call | solution.py:453
  1.5 1.7 %collective-permute-start = (f32[4,32,128]{2,1,0:T(8,128)S(1)}, f32[4,32,128]{2,1,0:T(8,128)S(1)}, u32[]{:S(2)}, u32[]{:S(2)}) collective-permute-start(f32[4,32,128]{2,1,0:T(8,128)S(1)} %get-tuple-element.41), channel_id=1, source_target_pairs={{0,8},{8,0},{16,24},{24,16},{32,40},{40,32},{48,56},{56,48},{64,72... | collective-permute-start | bytes 196616 | tf_op jit(solution)/shard_map/ppermute | solution.py:438
  3.2 1.7 %collective-permute-start.1 = (f32[4,32,128]{2,1,0:T(8,128)S(1)}, f32[4,32,128]{2,1,0:T(8,128)S(1)}, u32[]{:S(2)}, u32[]{:S(2)}) collective-permute-start(f32[4,32,128]{2,1,0:T(8,128)S(1)} %get-tuple-element.42), channel_id=1, source_target_pairs={{8,16},{16,8},{24,32},{32,24},{40,48},{48,40},{56,64},{64,56},{72,... | collective-permute-start | bytes 196616 | tf_op jit(solution)/shard_map/ppermute | solution.py:438
  4.9 1.6 %collective-permute-start.3 = (f32[4,16,1024]{2,1,0:T(8,128)S(1)}, f32[4,16,1024]{2,1,0:T(8,128)S(1)}, u32[]{:S(2)}, u32[]{:S(2)}) collective-permute-start(f32[4,16,1024]{2,1,0:T(8,128)S(1)} %get-tuple-element.46), channel_id=1, source_target_pairs={{1,2},{2,1},{3,4},{4,3},{5,6},{6,5},{0,7},{7,0},{9,10},{10,9},{11,... | collective-permute-start | bytes 786440 | tf_op jit(solution)/shard_map/ppermute | solution.py:438
  6.5 0.0 collective-permute-done.got_even
  6.5 4.2 %collective-permute-done.1.got_odd = f32[4,32,128]{2,1,0:T(8,128)S(1)} collective-permute-done((f32[4,32,128]{2,1,0:T(8,128)S(1)}, f32[4,32,128]{2,1,0:T(8,128)S(1)}, u32[]{:S(2)}, u32[]{:S(2)}) %collective-permute-start.1) | collective-permute-done | bytes 65568 | tf_op jit(solution)/shard_map/ppermute | solution.py:438
  10.8 0.1 collective-permute-start.2
  10.9 0.5 %collective-permute-start.4 = (f32[4,16,256]{2,1,0:T(8,128)S(1)}, f32[4,16,256]{2,1,0:T(8,128)S(1)}, u32[]{:S(2)}, u32[]{:S(2)}) collective-permute-start(f32[4,16,256]{2,1,0:T(8,128)S(1)} %get-tuple-element.47), channel_id=1, source_target_pairs={{0,1},{1,0},{2,3},{3,2},{4,5},{5,4},{6,7},{7,6},{8,9},{9,8},{10,11... | collective-permute-start | bytes 196616 | tf_op jit(solution)/shard_map/ppermute | solution.py:438
  11.4 2.5 %collective-permute-start.5 = (f32[4,16,256]{2,1,0:T(8,128)S(1)}, f32[4,16,256]{2,1,0:T(8,128)S(1)}, u32[]{:S(2)}, u32[]{:S(2)}) collective-permute-start(f32[4,16,256]{2,1,0:T(8,128)S(1)} %get-tuple-element.48), channel_id=1, source_target_pairs={{1,2},{2,1},{3,4},{4,3},{5,6},{6,5},{0,7},{7,0},{9,10},{10,9},{11,... | collective-permute-start | bytes 196616 | tf_op jit(solution)/shard_map/ppermute | solution.py:438
  13.8 0.0 collective-permute-done.4.corner_even
  13.8 2.4 %collective-permute-done.5.corner_odd = f32[4,16,256]{2,1,0:T(8,128)S(1)} collective-permute-done((f32[4,16,256]{2,1,0:T(8,128)S(1)}, f32[4,16,256]{2,1,0:T(8,128)S(1)}, u32[]{:S(2)}, u32[]{:S(2)}) %collective-permute-start.5) | collective-permute-done | bytes 65568 | tf_op jit(solution)/shard_map/ppermute | solution.py:438
  16.3 0.0 collective-permute-done.3.rows_odd
  16.3 0.0 collective-permute-done.2.rows_even
  16.3 0.0 copy-done
  16.3 4.0 %down.1 = (f32[8,8,1280]{2,1,0:T(8,128)S(1)}, f32[8,8,1280]{2,1,0:T(8,128)S(1)}, f32[8,8,1280]{2,1,0:T(8,128)S(1)}, f32[8,8,1280]{2,1,0:T(8,128)S(1)}, f32[9,8,1...) custom-call(f32[2,32,1024]{2,1,0:T(8,128)S(1)} %copy-done, ...), custom_call_target="tpu_custom_call" | custom-call | tf_op jit(solution)/shard_map/down/pallas_call | solution.py:482
  20.3 2.5 %collective-permute-start.7 = (f32[8,2048]{1,0:T(8,128)S(1)}, f32[8,2048]{1,0:T(8,128)S(1)}, u32[]{:S(2)}, u32[]{:S(2)}) collective-permute-start(f32[8,2048]{1,0:T(8,128)S(1)} %get-tuple-element.50), channel_id=1, source_target_pairs={{1,2},{2,1},{3,4},{4,3},{5,6},{6,5},{0,7},{7,0},{9,10},{10,9},{11,... | collective-permute-start | bytes 196616 | tf_op jit(solution)/shard_map/ppermute | solution.py:438
  22.8 0.0 collective-permute-start.6
  22.8 0.9 %collective-permute-start.9 = (f32[8,512]{1,0:T(8,128)S(1)}, f32[8,512]{1,0:T(8,128)S(1)}, u32[]{:S(2)}, u32[]{:S(2)}) collective-permute-start(f32[8,512]{1,0:T(8,128)S(1)} %get-tuple-element.49.far), channel_id=1, source_target_pairs={{0,6},{1,7},{2,0},{3,1},{4,2},{5,3},{6,4},{7,5},{8,14},{9,15},{10,... | collective-permute-start | bytes 49160 | tf_op jit(solution)/shard_map/ppermute | solution.py:443
  23.7 1.1 %collective-permute-start.8 = (f32[8,512]{1,0:T(8,128)S(1)}, f32[8,512]{1,0:T(8,128)S(1)}, u32[]{:S(2)}, u32[]{:S(2)}) collective-permute-start(f32[8,512]{1,0:T(8,128)S(1)} %get-tuple-element.49.far), channel_id=1, source_target_pairs={{0,2},{1,3},{2,4},{3,5},{4,6},{5,7},{6,0},{7,1},{8,10},{9,11},{10,... | collective-permute-start | bytes 49160 | tf_op jit(solution)/shard_map/ppermute | solution.py:443
  24.9 1.7 %collective-permute-done.9.far_below = f32[8,512]{1,0:T(8,128)S(1)} collective-permute-done((f32[8,512]{1,0:T(8,128)S(1)}, f32[8,512]{1,0:T(8,128)S(1)}, u32[]{:S(2)}, u32[]{:S(2)}) %collective-permute-start.9) | collective-permute-done | bytes 16416 | tf_op jit(solution)/shard_map/ppermute | solution.py:443
  26.6 2.1 %collective-permute-done.8.far_above = f32[8,512]{1,0:T(8,128)S(1)} collective-permute-done((f32[8,512]{1,0:T(8,128)S(1)}, f32[8,512]{1,0:T(8,128)S(1)}, u32[]{:S(2)}, u32[]{:S(2)}) %collective-permute-start.8) | collective-permute-done | bytes 16416 | tf_op jit(solution)/shard_map/ppermute | solution.py:443
  28.7 0.0 collective-permute-done.7.near_odd
  28.7 0.0 collective-permute-done.6.near_even
  28.7 3.5 %up.1 = f32[2,32,1024]{2,1,0:T(8,128)} custom-call(f32[8,512]{1,0:T(8,128)S(1)} %get-tuple-element.49.far, f32[8,2048]{1,0:T(8,128)S(1)} %collective-permute-done.6.near_even, f32[8,2048]{1,0:T(8,128)S(1)} %collective-permute-done.7.near_odd, f32[8,512]{1,0:T(8,128)S(1)} %collective-permute-done.8.far_above, f32[8,512]{1,0:T(8,128)S(1)} %collective-permute-done.9.far_below, ...), custom_call_target="tpu_custom_call" | custom-call | tf_op jit(solution)/shard_map/up/pallas_call | solution.py:497
  (2 shorter events, 0.0 us)
Async XLA Ops:
  0.0 16.3 %copy-start = (f32[2,32,1024]{2,1,0:T(8,128)S(1)}, f32[2,32,1024]{2,1,0:T(8,128)}, u32[]{:S(2)}) copy-start(f32[2,32,1024]{2,1,0:T(8,128)} %forcing.3) | copy-start | bytes 786436
  1.5 5.0 %collective-permute-start = (f32[4,32,128]{2,1,0:T(8,128)S(1)}, f32[4,32,128]{2,1,0:T(8,128)S(1)}, u32[]{:S(2)}, u32[]{:S(2)}) collective-permute-start(f32[4,32,128]{2,1,0:T(8,128)S(1)} %get-tuple-element.41), channel_id=1, source_target_pairs={{0,8},{8,0},{16,24},{24,16},{32,40},{40,32},{48,56},{56,48},{64,72... | collective-permute-start | bytes 196616 | tf_op jit(solution)/shard_map/ppermute | solution.py:438
  3.2 7.6 %collective-permute-start.1 = (f32[4,32,128]{2,1,0:T(8,128)S(1)}, f32[4,32,128]{2,1,0:T(8,128)S(1)}, u32[]{:S(2)}, u32[]{:S(2)}) collective-permute-start(f32[4,32,128]{2,1,0:T(8,128)S(1)} %get-tuple-element.42), channel_id=1, source_target_pairs={{8,16},{16,8},{24,32},{32,24},{40,48},{48,40},{56,64},{64,56},{72,... | collective-permute-start | bytes 196616 | tf_op jit(solution)/shard_map/ppermute | solution.py:438
  4.9 11.4 %collective-permute-start.3 = (f32[4,16,1024]{2,1,0:T(8,128)S(1)}, f32[4,16,1024]{2,1,0:T(8,128)S(1)}, u32[]{:S(2)}, u32[]{:S(2)}) collective-permute-start(f32[4,16,1024]{2,1,0:T(8,128)S(1)} %get-tuple-element.46), channel_id=1, source_target_pairs={{1,2},{2,1},{3,4},{4,3},{5,6},{6,5},{0,7},{7,0},{9,10},{10,9},{11,... | collective-permute-start | bytes 786440 | tf_op jit(solution)/shard_map/ppermute | solution.py:438
  10.8 5.5 %collective-permute-start.2 = (f32[4,16,1024]{2,1,0:T(8,128)S(1)}, f32[4,16,1024]{2,1,0:T(8,128)S(1)}, u32[]{:S(2)}, u32[]{:S(2)}) collective-permute-start(f32[4,16,1024]{2,1,0:T(8,128)S(1)} %get-tuple-element.45), channel_id=1, source_target_pairs={{0,1},{1,0},{2,3},{3,2},{4,5},{5,4},{6,7},{7,6},{8,9},{9,8},{10,11... | collective-permute-start | bytes 786440 | tf_op jit(solution)/shard_map/ppermute | solution.py:438
  10.9 3.0 %collective-permute-start.4 = (f32[4,16,256]{2,1,0:T(8,128)S(1)}, f32[4,16,256]{2,1,0:T(8,128)S(1)}, u32[]{:S(2)}, u32[]{:S(2)}) collective-permute-start(f32[4,16,256]{2,1,0:T(8,128)S(1)} %get-tuple-element.47), channel_id=1, source_target_pairs={{0,1},{1,0},{2,3},{3,2},{4,5},{5,4},{6,7},{7,6},{8,9},{9,8},{10,11... | collective-permute-start | bytes 196616 | tf_op jit(solution)/shard_map/ppermute | solution.py:438
  11.4 4.9 %collective-permute-start.5 = (f32[4,16,256]{2,1,0:T(8,128)S(1)}, f32[4,16,256]{2,1,0:T(8,128)S(1)}, u32[]{:S(2)}, u32[]{:S(2)}) collective-permute-start(f32[4,16,256]{2,1,0:T(8,128)S(1)} %get-tuple-element.48), channel_id=1, source_target_pairs={{1,2},{2,1},{3,4},{4,3},{5,6},{6,5},{0,7},{7,0},{9,10},{10,9},{11,... | collective-permute-start | bytes 196616 | tf_op jit(solution)/shard_map/ppermute | solution.py:438
  20.3 8.4 %collective-permute-start.7 = (f32[8,2048]{1,0:T(8,128)S(1)}, f32[8,2048]{1,0:T(8,128)S(1)}, u32[]{:S(2)}, u32[]{:S(2)}) collective-permute-start(f32[8,2048]{1,0:T(8,128)S(1)} %get-tuple-element.50), channel_id=1, source_target_pairs={{1,2},{2,1},{3,4},{4,3},{5,6},{6,5},{0,7},{7,0},{9,10},{10,9},{11,... | collective-permute-start | bytes 196616 | tf_op jit(solution)/shard_map/ppermute | solution.py:438
  22.8 5.8 %collective-permute-start.6 = (f32[8,2048]{1,0:T(8,128)S(1)}, f32[8,2048]{1,0:T(8,128)S(1)}, u32[]{:S(2)}, u32[]{:S(2)}) collective-permute-start(f32[8,2048]{1,0:T(8,128)S(1)} %get-tuple-element.50), channel_id=1, source_target_pairs={{0,1},{1,0},{2,3},{3,2},{4,5},{5,4},{6,7},{7,6},{8,9},{9,8},{10,11... | collective-permute-start | bytes 196616 | tf_op jit(solution)/shard_map/ppermute | solution.py:438
  22.8 3.7 %collective-permute-start.9 = (f32[8,512]{1,0:T(8,128)S(1)}, f32[8,512]{1,0:T(8,128)S(1)}, u32[]{:S(2)}, u32[]{:S(2)}) collective-permute-start(f32[8,512]{1,0:T(8,128)S(1)} %get-tuple-element.49.far), channel_id=1, source_target_pairs={{0,6},{1,7},{2,0},{3,1},{4,2},{5,3},{6,4},{7,5},{8,14},{9,15},{10,... | collective-permute-start | bytes 49160 | tf_op jit(solution)/shard_map/ppermute | solution.py:443
  23.7 4.9 %collective-permute-start.8 = (f32[8,512]{1,0:T(8,128)S(1)}, f32[8,512]{1,0:T(8,128)S(1)}, u32[]{:S(2)}, u32[]{:S(2)}) collective-permute-start(f32[8,512]{1,0:T(8,128)S(1)} %get-tuple-element.49.far), channel_id=1, source_target_pairs={{0,2},{1,3},{2,4},{3,5},{4,6},{5,7},{6,0},{7,1},{8,10},{9,11},{10,... | collective-permute-start | bytes 49160 | tf_op jit(solution)/shard_map/ppermute | solution.py:443

commit v5 on v4

--- a/solution.py
+++ b/solution.py
@@ -10,11 +10,11 @@
 ROWS, COLS = 32, 1024
 EDGE = 128
 HALO = 16
-WIDE = COLS + 2 * EDGE
 PLANES = (8, 4, 2)
-LANES = (1280, 640, 384)
-LANES3 = 256
-VMEM_LIMIT = 48 * 1024 * 1024
+MAIN = (1024, 512, 256, 128)
+RIM = (512, 256, 128, 128)
+MERGED = (1152, 640, 384, 256)
+VMEM_LIMIT = 16 * 1024 * 1024
 
 
 def vmem(count):
@@ -57,25 +57,46 @@
     return jnp.take_along_axis(x, index, axis=1, mode="promise_in_bounds")
 
 
-def halve_lanes(x, lanes):
+def halve_lanes(x):
     at = lane(1)
-    index = 2 * (at % 64)
-    parts = [pick(t + from_right(t), index) for t in tiles(x)]
+    even = at % 2 == 0
+    index = jnp.where(at < 64, 2 * at, 2 * at - 127)
+    parts = tiles(x)
+    if len(parts) % 2:
+        parts.append(jnp.zeros_like(parts[0]))
     out = []
-    for i in range(0, len(parts), 2):
-        high = parts[i + 1] if i + 1 < len(parts) else jnp.zeros_like(parts[i])
-        out.append(jnp.where(at < 64, parts[i], high))
-    while len(out) * 128 < lanes:
-        out.append(jnp.zeros_like(out[0]))
-    return jnp.concatenate(out[: lanes // 128], axis=1)
+    for a, b in zip(parts[0::2], parts[1::2]):
+        out.append(pick(jnp.where(even, a, b), index) + pick(jnp.where(even, b, a), index ^ 1))
+    return jnp.concatenate(out, axis=1)
 
 
 def double_lanes(x, lanes):
-    index = lane(1) // 2
+    at = lane(1)
     parts = tiles(x)
-    return jnp.concatenate(
-        [pick(parts[i // 2], index + 64 * (i % 2)) for i in range(lanes // 128)], axis=1
-    )
+    count = lanes // 128 - 1
+    out = [pick(parts[i // 2], at // 2 + 64 * (i % 2)) for i in range(count)]
+    out.append(pick(parts[-1], jnp.where(at < 64, at // 2, at // 2 + 64)))
+    return jnp.concatenate(out, axis=1)
+
+
+def merge_tiles(level, main, rim):
+    at = lane(1)
+    if level == 0:
+        low, left, right, high = rim
+    else:
+        low = left = pltpu.roll(rim[0], (64, 96, 112)[level - 1], axis=1)
+        high = right = pltpu.roll(rim[-1], (64, 32, 80)[level - 1], axis=1)
+    out = list(main)
+    out[0] = jnp.where(at < 64 >> level, left, out[0])
+    out[-1] = jnp.where(at < 128 - (64 >> level), out[-1], right)
+    beside = jnp.where(at < 64, high, low)
+    if level > 1:
+        beside = jnp.where((at < EDGE >> level) | (at >= 128 - (EDGE >> level)), beside, 0.0)
+    return out + [beside]
+
+
+def merge(level, main, rim):
+    return jnp.concatenate(merge_tiles(level, tiles(main), tiles(rim)), axis=1)
 
 
 def coefficients(eta, beta, eta_below, face_above):
@@ -102,8 +123,8 @@
         self.right, self.left, self.cross_right, self.cross_left, self.below, self.scale, self.force, self.field = refs
 
     @staticmethod
-    def shapes(level):
-        planes, lanes = PLANES[level], LANES[level]
+    def shapes(level, widths):
+        planes, lanes = PLANES[level], widths[level]
         one = [(planes, 8, lanes)] * 4 + [(planes + 1, 8, lanes), (planes, 8, lanes)]
         return one + [(2, planes, 8, lanes), (2, planes + 2, 8, lanes)]
 
@@ -170,7 +191,7 @@
         self.sweep(other, self.field)
         self.wrap(self.field)
 
-    def restrict(self, diag, target, lanes):
+    def restrict(self, diag, target):
         for p in range(0, self.planes, 2):
             rest = [0.0, 0.0]
             for q in (p, p + 1):
@@ -178,7 +199,7 @@
                 for k in range(2):
                     rest[k] = rest[k] + (terms[k] - diag[q] * self.field[k, q + 1])
             for k in range(2):
-                target(k, p // 2, halve_lanes(rest[k], lanes))
+                target(k, p // 2, halve_lanes(rest[k]))
 
     def last_sweeps(self, coarse, result, other):
         for k in range(2):
@@ -192,9 +213,9 @@
         self.sweep(other, result)
 
 
-def halve_planes(source, target, planes, lanes, scale):
+def halve_planes(source, target, planes, scale):
     for p in range(0, planes, 2):
-        both = halve_lanes(source[p] + source[p + 1], lanes)
+        both = halve_lanes(source[p] + source[p + 1])
         target[p // 2] = scale * both if scale != 1.0 else both
 
 
@@ -275,74 +296,130 @@
     return jnp.where(upper, pltpu.roll(a, 6, axis=0), pltpu.roll(b, 2, axis=0))
 
 
-def down_kernel(forcing, coef, got_even, got_odd, rows_even, rows_odd, corner_even, corner_odd, *refs):
-    levels = [Level(PLANES[i], refs[8 * i : 8 * i + 8]) for i in range(3)]
-    near, far = refs[24:26]
-    natural = refs[26]
-    etas, betas, diags, others = (refs[27 + 3 * i : 30 + 3 * i] for i in range(4))
+def levels_of(refs):
+    return [Level(PLANES[i], refs[8 * i : 8 * i + 8]) for i in range(3)]
+
+
+def spread(above, own, below, natural, targets, cols):
     gy = lax.axis_index("gy")
     even = gy % 2 == 0
-    first = gy == 0
-    last = gy == lax.axis_size("gy") - 1
-    for row in range(4):
-        source = forcing if row < 2 else coef
-        sides = side_columns(got_even[row], got_odd[row])
-        for i in range(WIDE // 128):
-            cols = slice(128 * i, 128 * i + 128)
-            if 0 < i < WIDE // 128 - 1:
-                inner = slice(128 * i - 128, 128 * i)
-                a, b = rows_even[row, :, inner], rows_odd[row, :, inner]
-            else:
-                outer = slice(0, EDGE) if i == 0 else slice(EDGE, 2 * EDGE)
-                a, b = corner_even[row, :, outer], corner_odd[row, :, outer]
-            natural[i, 0:HALO] = jnp.where(first, 0.0, jnp.where(even, b, a))
-            natural[i, HALO + ROWS :] = jnp.where(last, 0.0, jnp.where(even, a, b))
-            if i == 0:
-                own = sides[0]
-            elif i == WIDE // 128 - 1:
-                own = sides[1]
-            else:
-                own = source[row % 2, :, 128 * i - 128 : 128 * i]
-            natural[i, HALO : HALO + ROWS] = own
-            for p in range(8):
-                plane = natural[i, pl.ds(p, 8, stride=8), :]
-                if row < 2:
-                    levels[0].force[row, p, :, cols] = plane
-                else:
-                    (etas, betas)[row - 2][0][p, :, cols] = plane
+    (above_even, above_odd), (below_even, below_odd) = above, below
+    natural[0:HALO] = jnp.where(gy == 0, 0.0, jnp.where(even, above_odd, above_even))
+    natural[HALO : HALO + ROWS] = own
+    natural[HALO + ROWS :] = jnp.where(gy == lax.axis_size("gy") - 1, 0.0, jnp.where(even, below_even, below_odd))
+    for p in range(8):
+        targets(p, cols, natural[pl.ds(p, 8, stride=8), :])
+
+
+def descend(levels, etas, betas, diags, others):
     for level in range(3):
         here = levels[level]
         here.setup(etas[level], betas[level], diags[level])
         here.first_sweeps(others[level])
         if level < 2:
-            lanes = LANES[level + 1]
-            halve_planes(etas[level], etas[level + 1], here.planes, lanes, 0.5)
-            halve_planes(betas[level], betas[level + 1], here.planes, lanes, 1.0)
+            halve_planes(etas[level], etas[level + 1], here.planes, 0.5)
+            halve_planes(betas[level], betas[level + 1], here.planes, 1.0)
 
             def store(k, p, value, target=levels[level + 1].force):
                 target[k, p] = value
 
-            here.restrict(diags[level], store, lanes)
+            here.restrict(diags[level], store)
     found = [None, None]
 
     def keep(k, p, value):
         found[k] = value
 
-    levels[2].restrict(diags[2], keep, LANES3)
-    eta = 0.5 * halve_lanes(etas[2][0] + etas[2][1], LANES3)
-    beta = halve_lanes(betas[2][0] + betas[2][1], LANES3)
-    head = jnp.concatenate([own_rows(found[0], found[1]), own_rows(eta, beta)], axis=1)
+    levels[2].restrict(diags[2], keep)
+    eta = 0.5 * halve_lanes(etas[2][0] + etas[2][1])
+    beta = halve_lanes(betas[2][0] + betas[2][1])
+    return found + [eta, beta]
+
+
+def plane_targets(row, levels, etas, betas):
+    def target(p, cols, plane):
+        if row < 2:
+            levels[0].force[row, p, :, cols] = plane
+        else:
+            (etas, betas)[row - 2][0][p, :, cols] = plane
+
+    return target
+
+
+def main_kernel(forcing, coef, rows_even, rows_odd, *refs):
+    levels = levels_of(refs)
+    top, natural = refs[24:26]
+    etas, betas, diags, others = (refs[26 + 3 * i : 29 + 3 * i] for i in range(4))
+    for row in range(4):
+        source = forcing if row < 2 else coef
+        target = plane_targets(row, levels, etas, betas)
+        for i in range(COLS // 128):
+            cols = slice(128 * i, 128 * i + 128)
+            halo = (rows_even[row, :, cols], rows_odd[row, :, cols])
+            spread(halo, source[row % 2, :, cols], halo, natural.at[(8 * row + i) % 2], target, cols)
+    for i, value in enumerate(descend(levels, etas, betas, diags, others)):
+        top[i] = value
+
+
+def rim_kernel(
+    forcing,
+    coef,
+    got_even,
+    got_odd,
+    rows_even,
+    rows_odd,
+    corner_even,
+    corner_odd,
+    top,
+    late_force,
+    late_field,
+    *refs,
+):
+    levels = levels_of(refs)
+    near, far, natural = refs[24:27]
+    etas, betas, diags, others = (refs[27 + 3 * i : 30 + 3 * i] for i in range(4))
+    for row in range(4):
+        source = forcing if row < 2 else coef
+        target = plane_targets(row, levels, etas, betas)
+        sides = side_columns(got_even[row], got_odd[row])
+        for i in range(4):
+            if i in (0, 3):
+                part = slice(0, EDGE) if i == 0 else slice(EDGE, 2 * EDGE)
+                halo = (corner_even[row, :, part], corner_odd[row, :, part])
+                own = sides[i // 3]
+            else:
+                part = slice(0, EDGE) if i == 1 else slice(COLS - EDGE, COLS)
+                halo = (rows_even[row, :, part], rows_odd[row, :, part])
+                own = source[row % 2, :, part]
+            spread(halo, own, halo, natural.at[i % 2], target, slice(128 * i, 128 * i + 128))
+    rim = descend(levels, etas, betas, diags, others)
+    both = [merge(3, top[i], rim[i]) for i in range(4)]
+    head = jnp.concatenate([own_rows(both[0], both[1]), own_rows(both[2], both[3])], axis=1)
     far[...] = head
-    near[:, 0 : 2 * LANES3] = head
-    at = 2 * LANES3
-    for p in range(2):
-        near[:, at : at + 384] = own_rows(levels[2].field[0, p + 1], levels[2].field[1, p + 1])
-        near[:, at + 768 : at + 1152] = own_rows(levels[2].force[0, p], levels[2].force[1, p])
-        at += 384
+    at = head.shape[1]
+    near[:, 0:at] = head
+    for source, rims, shift in ((late_field, levels[2].field, 1), (late_force, levels[2].force, 0)):
+        for p in range(2):
+            parts = [merge(2, source[k, p + shift], rims[k, p + shift]) for k in range(2)]
+            near[:, at : at + MERGED[2]] = own_rows(parts[0], parts[1])
+            at += MERGED[2]
+
+
+def merge_kernel(*refs):
+    for level in range(3):
+        for i in range(8):
+            main, rim, target = (refs[24 * j + 8 * level + i] for j in range(3))
+            planes = PLANES[level]
+            if i < 6:
+                for p in range(main.shape[0]):
+                    target[p] = merge(level, main[p], rim[p])
+            else:
+                for k in range(2):
+                    for p in range(i - 6, planes + i - 6):
+                        target[k, p] = merge(level, main[k, p], rim[k, p])
 
 
 def up_kernel(far, near_even, near_odd, far_above, far_below, *refs):
-    levels = [Level(PLANES[i], refs[8 * i : 8 * i + 8]) for i in range(3)]
+    levels = levels_of(refs)
     velocity, natural, late_force, late_field = refs[24:28]
     fields, others = refs[28:31], refs[31:34]
     gy = lax.axis_index("gy")
@@ -375,8 +452,8 @@
             for s in (False, True)
         ]
 
-    force = stacked(slice(0, LANES3))
-    eta, beta = stacked(slice(LANES3, 2 * LANES3))
+    force = stacked(slice(0, MERGED[3]))
+    eta, beta = stacked(slice(MERGED[3], 2 * MERGED[3]))
     right, left, under, over, cross_right, cross_left, diag = coefficients(eta, beta, from_below(eta), from_above)
     scale = OMEGA / diag
     field = [scale * force[0], scale * force[1]]
@@ -396,19 +473,17 @@
     for k in range(2):
         a, b = pltpu.roll(field[k][0:8], 2, axis=0), pltpu.roll(field[k][8:16], 2, axis=0)
         coarsest.append(jnp.where(sublanes(a) < 2, a, b))
-    at = 2 * LANES3
-    for p in range(2):
-        for target, own, start, shift in (
-            (late_field, levels[2].field, at, 1),
-            (late_force, levels[2].force, at + 768, 0),
-        ):
-            up, down = above(slice(start, start + 384)), below(slice(start, start + 384))
+    at = 2 * MERGED[3]
+    for target, own, shift in ((late_field, levels[2].field, 1), (late_force, levels[2].force, 0)):
+        for p in range(2):
+            part = slice(at, at + MERGED[2])
+            up, down = above(part), below(part)
             for k in range(2):
                 turn = 2 if k else 6
                 a, b = pltpu.roll(up, turn, axis=0), pltpu.roll(down, turn, axis=0)
                 sub = sublanes(a)
                 target[k, p + shift] = jnp.where(sub < 2, a, jnp.where(sub < 6, own[k, p + shift], b))
-        at += 384
+            at += MERGED[2]
     levels[2].force = late_force
     levels[2].field = late_field
     coarse = lambda k, p: coarsest[k]
@@ -418,7 +493,7 @@
     for k in range(2):
         for i in range(COLS // 128):
             for p in range(8):
-                part = fields[0][k, p + 1, :, 128 * i + EDGE : 128 * i + EDGE + 128]
+                part = fields[0][k, p + 1, :, 128 * i : 128 * i + 128]
                 natural[i, pl.ds(p, 4, stride=8), :] = pltpu.roll(part, 6, axis=0)[0:4]
             velocity[k, :, 128 * i : 128 * i + 128] = natural[i]
 
@@ -474,35 +549,60 @@
     rows_even = swap(main_even, "gy", 0)
     corner_even = swap(send_even, "gy", 0)
     corner_odd = swap(send_odd, "gy", 1)
-    kept = [shape(*dims) for level in range(3) for dims in Level.shapes(level)]
-    planes = [(PLANES[i], 8, LANES[i]) for i in range(3)]
-    rims = [(2, PLANES[i] + 2, 8, LANES[i]) for i in range(3)]
-    scratch = [pltpu.VMEM(dims, jnp.float32) for dims in [(WIDE // 128, 64, 128)] + planes * 3 + rims]
-    near_lanes = 2 * LANES3 + 4 * LANES[2]
-    *kept, near, far = pl.pallas_call(
-        down_kernel,
-        out_shape=tuple(kept) + (shape(8, near_lanes), shape(8, 2 * LANES3)),
-        in_specs=vmem(8),
+
+    def kept(widths):
+        return [dims for level in range(3) for dims in Level.shapes(level, widths)]
+
+    def scratch(dims):
+        return [pltpu.VMEM(one, jnp.float32) for one in dims]
+
+    def rims(widths):
+        return [(2, PLANES[i] + 2, 8, widths[i]) for i in range(3)]
+
+    def work(widths):
+        return scratch([(2, 64, 128)] + [(PLANES[i], 8, widths[i]) for i in range(3)] * 3 + rims(widths))
+
+    *main, top = pl.pallas_call(
+        main_kernel,
+        out_shape=tuple(shape(*dims) for dims in kept(MAIN) + [(4, 8, MAIN[3])]),
+        in_specs=vmem(4),
+        out_specs=tuple(vmem(25)),
+        scratch_shapes=work(MAIN),
+        compiler_params=params(),
+        name="main",
+    )(forcing, coef, rows_even, rows_odd)
+    near_lanes = 2 * MERGED[3] + 4 * MERGED[2]
+    *rim, near, far = pl.pallas_call(
+        rim_kernel,
+        out_shape=tuple(shape(*dims) for dims in kept(RIM) + [(8, near_lanes), (8, 2 * MERGED[3])]),
+        in_specs=vmem(11),
         out_specs=tuple(vmem(26)),
-        scratch_shapes=scratch,
+        scratch_shapes=work(RIM),
         compiler_params=params(),
-        name="down",
-    )(forcing, coef, got_even, got_odd, rows_even, rows_odd, corner_even, corner_odd)
+        name="rim",
+    )(forcing, coef, got_even, got_odd, rows_even, rows_odd, corner_even, corner_odd, top, main[22], main[23])
     near_even = swap(near, "gy", 0)
     near_odd = swap(near, "gy", 1)
     far_above = turn(far, "gy", 2)
     far_below = turn(far, "gy", -2)
-    late = [(2, 2, 8, LANES[2]), (2, 4, 8, LANES[2])]
-    scratch = [pltpu.VMEM(dims, jnp.float32) for dims in [(COLS // 128, ROWS, 128)] + late + rims + rims]
+    merged = pl.pallas_call(
+        merge_kernel,
+        out_shape=tuple(shape(*dims) for dims in kept(MERGED)),
+        in_specs=vmem(48),
+        out_specs=tuple(vmem(24)),
+        compiler_params=params(),
+        name="merge",
+    )(*main, *rim)
+    late = [(2, 2, 8, MERGED[2]), (2, 4, 8, MERGED[2])]
     return pl.pallas_call(
         up_kernel,
         out_shape=shape(2, ROWS, COLS),
         in_specs=vmem(29),
         out_specs=vmem(1)[0],
-        scratch_shapes=scratch,
+        scratch_shapes=scratch([(COLS // 128, ROWS, 128)] + late + rims(MERGED) + rims(MERGED)),
         compiler_params=params(),
         name="up",
-    )(far, near_even, near_odd, far_above, far_below, *kept)
+    )(far, near_even, near_odd, far_above, far_below, *merged)
 
 
 def solution(mesh):

time: 32.2 us -> 30.2 us (0.938)
  waiting for transfers between devices: 10.5 us -> 8.06 us
  Pallas kernels: 9 us -> 9.75 us
    ppermute x8, waiting for transfers between devices: 6.68 us -> 4.25 us  [swap(): lax.ppermute(x, ('gx', 'gy'), [(place(*a), place(*b)) for a, b in pairs])]
    pallas_call x1 -> x3, Pallas kernels: 4.01 us -> 4.77 us  [the longest x1 2.77 us: local(): pl.pallas_call(main_kernel, out_shape=tuple((shape(*dims) for dims in kep...]
    ppermute x8, starting transfers between devices: 10.6 us -> 10.2 us  [swap(): lax.ppermute(x, ('gx', 'gy'), [(place(*a), place(*b)) for a, b in pairs])]
  transfers between devices with their start and end apart: 10 -> 10, of which waited for: 4 -> 3; matrix products, arithmetic and copies ran while one was open for 0% -> 0% of each run, Pallas kernels for 0% -> 10%
where the time goes in v5:
time: 30.2 us; the launch traced here: 30.1 us
  starting transfers between devices  12.3 us (41%)
  Pallas kernels  9.75 us (32%)
  waiting for transfers between devices  8.06 us (27%)
    ppermute x8, starting transfers between devices, swap(): lax.ppermute(x, ('gx', 'gy'), [(place(*a), place(*b)) for a, b in pairs])  10.2 us
    ppermute x8, waiting for transfers between devices, swap(): lax.ppermute(x, ('gx', 'gy'), [(place(*a), place(*b)) for a, b in pairs])  4.25 us
    ppermute x2, waiting for transfers between devices, turn(): lax.ppermute(x, axis, [(i, (i + step) % count) for i in range(count)])  3.81 us
    pallas_call x1, Pallas kernels, local(): pl.pallas_call(up_kernel, out_shape=shape(2, ROWS, COLS), in_specs=vmem(2...  3.46 us
    pallas_call x1, Pallas kernels, local(): pl.pallas_call(main_kernel, out_shape=tuple((shape(*dims) for dims in kep...  2.77 us
    ppermute x2, starting transfers between devices, turn(): lax.ppermute(x, axis, [(i, (i + step) % count) for i in range(count)])  2.03 us
    pallas_call x1, Pallas kernels, local(): pl.pallas_call(rim_kernel, out_shape=tuple((shape(*dims) for dims in kept...  1.63 us
    pallas_call x1, Pallas kernels, local(): pl.pallas_call(lookup_kernel, out_shape=(shape(2, ROWS, COLS),) + (shape(...  1.5 us
  transfers between devices with their start and end apart: 10, of which 3 were waited for; matrix products, arithmetic and copies ran while one was open for 0% of the time, Pallas kernels for 10%

profile of v5, /device:TPU:128, one launch (start us, length us, event | category | flops | bytes accessed | tf_op | source)
XLA Modules:
  0.0 30.1 jit_solution(10759431625124654228)
XLA Ops:
  0.0 1.5 %lookup.1 = (f32[2,32,1024]{2,1,0:T(8,128)S(1)}, f32[4,32,128]{2,1,0:T(8,128)S(1)}, f32[4,32,128]{2,1,0:T(8,128)S(1)}, f32[4,16,1024]{2,1,0:T(8,128)S(1)}, f32[4,16,1024]{2,1,0:T(8,128)S(1)}) custom-call(f32[16]{0:T(128)} %v_table.1, f32[16]{0:T(128)} %d_table.1, f32[2,32,1024]{2,1,0:T(8,128)} %forcing.5, s32[32,1024]{1,0:T(8,128)} %mask.1, ...), custom_call_target="tpu_custom_call" | custom-call | tf_op jit(solution)/shard_map/lookup/pallas_call | solution.py:528
  1.5 1.7 %collective-permute-start = (f32[4,32,128]{2,1,0:T(8,128)S(1)}, f32[4,32,128]{2,1,0:T(8,128)S(1)}, u32[]{:S(2)}, u32[]{:S(2)}) collective-permute-start(f32[4,32,128]{2,1,0:T(8,128)S(1)} %get-tuple-element.90), channel_id=1, source_target_pairs={{0,8},{8,0},{16,24},{24,16},{32,40},{40,32},{48,56},{56,48},{64,72... | collective-permute-start | bytes 196616 | tf_op jit(solution)/shard_map/ppermute | solution.py:513
  3.2 1.7 %collective-permute-start.1 = (f32[4,32,128]{2,1,0:T(8,128)S(1)}, f32[4,32,128]{2,1,0:T(8,128)S(1)}, u32[]{:S(2)}, u32[]{:S(2)}) collective-permute-start(f32[4,32,128]{2,1,0:T(8,128)S(1)} %get-tuple-element.91), channel_id=1, source_target_pairs={{8,16},{16,8},{24,32},{32,24},{40,48},{48,40},{56,64},{64,56},{72,... | collective-permute-start | bytes 196616 | tf_op jit(solution)/shard_map/ppermute | solution.py:513
  4.9 1.6 %collective-permute-start.3 = (f32[4,16,1024]{2,1,0:T(8,128)S(1)}, f32[4,16,1024]{2,1,0:T(8,128)S(1)}, u32[]{:S(2)}, u32[]{:S(2)}) collective-permute-start(f32[4,16,1024]{2,1,0:T(8,128)S(1)} %get-tuple-element.95), channel_id=1, source_target_pairs={{1,2},{2,1},{3,4},{4,3},{5,6},{6,5},{0,7},{7,0},{9,10},{10,9},{11,... | collective-permute-start | bytes 786440 | tf_op jit(solution)/shard_map/ppermute | solution.py:513
  6.5 0.0 collective-permute-done.got_even
  6.5 4.2 %collective-permute-done.1.got_odd = f32[4,32,128]{2,1,0:T(8,128)S(1)} collective-permute-done((f32[4,32,128]{2,1,0:T(8,128)S(1)}, f32[4,32,128]{2,1,0:T(8,128)S(1)}, u32[]{:S(2)}, u32[]{:S(2)}) %collective-permute-start.1) | collective-permute-done | bytes 65568 | tf_op jit(solution)/shard_map/ppermute | solution.py:513
  10.8 0.1 collective-permute-start.2
  10.9 0.5 %collective-permute-start.4 = (f32[4,16,256]{2,1,0:T(8,128)S(1)}, f32[4,16,256]{2,1,0:T(8,128)S(1)}, u32[]{:S(2)}, u32[]{:S(2)}) collective-permute-start(f32[4,16,256]{2,1,0:T(8,128)S(1)} %get-tuple-element.96), channel_id=1, source_target_pairs={{0,1},{1,0},{2,3},{3,2},{4,5},{5,4},{6,7},{7,6},{8,9},{9,8},{10,11... | collective-permute-start | bytes 196616 | tf_op jit(solution)/shard_map/ppermute | solution.py:513
  11.4 2.5 %collective-permute-start.5 = (f32[4,16,256]{2,1,0:T(8,128)S(1)}, f32[4,16,256]{2,1,0:T(8,128)S(1)}, u32[]{:S(2)}, u32[]{:S(2)}) collective-permute-start(f32[4,16,256]{2,1,0:T(8,128)S(1)} %get-tuple-element.97), channel_id=1, source_target_pairs={{1,2},{2,1},{3,4},{4,3},{5,6},{6,5},{0,7},{7,0},{9,10},{10,9},{11,... | collective-permute-start | bytes 196616 | tf_op jit(solution)/shard_map/ppermute | solution.py:513
  13.8 0.0 collective-permute-done.3.rows_odd
  13.8 0.0 collective-permute-done.2.rows_even
  13.8 2.8 %main.1 = (f32[8,8,1024]{2,1,0:T(8,128)S(1)}, f32[8,8,1024]{2,1,0:T(8,128)S(1)}, f32[8,8,1024]{2,1,0:T(8,128)S(1)}, f32[8,8,1024]{2,1,0:T(8,128)S(1)}, f32[9,8,1...) custom-call(f32[2,32,1024]{2,1,0:T(8,128)S(1)} %copy-done, ...), custom_call_target="tpu_custom_call" | custom-call | tf_op jit(solution)/shard_map/main/pallas_call | solution.py:565
  16.6 0.0 collective-permute-done.4.corner_even
  16.6 0.0 collective-permute-done.5.corner_odd
  16.6 1.6 %rim.1 = (f32[8,8,512]{2,1,0:T(8,128)S(1)}, f32[8,8,512]{2,1,0:T(8,128)S(1)}, f32[8,8,512]{2,1,0:T(8,128)S(1)}, f32[8,8,512]{2,1,0:T(8,128)S(1)}, f32[9,8,512]{2...) custom-call(f32[2,32,1024]{2,1,0:T(8,128)S(1)} %copy-done, ...), custom_call_target="tpu_custom_call" | custom-call | tf_op jit(solution)/shard_map/rim/pallas_call | solution.py:575
  18.3 2.2 %collective-permute-start.7 = (f32[8,2048]{1,0:T(8,128)S(1)}, f32[8,2048]{1,0:T(8,128)S(1)}, u32[]{:S(2)}, u32[]{:S(2)}) collective-permute-start(f32[8,2048]{1,0:T(8,128)S(1)} %get-tuple-element.102), channel_id=1, source_target_pairs={{1,2},{2,1},{3,4},{4,3},{5,6},{6,5},{0,7},{7,0},{9,10},{10,9},{11,... | collective-permute-start | bytes 196616 | tf_op jit(solution)/shard_map/ppermute | solution.py:513
  20.4 1.3 %collective-permute-start.9 = (f32[8,512]{1,0:T(8,128)S(1)}, f32[8,512]{1,0:T(8,128)S(1)}, u32[]{:S(2)}, u32[]{:S(2)}) collective-permute-start(f32[8,512]{1,0:T(8,128)S(1)} %get-tuple-element.101.far), channel_id=1, source_target_pairs={{0,6},{1,7},{2,0},{3,1},{4,2},{5,3},{6,4},{7,5},{8,14},{9,15},{10,... | collective-permute-start | bytes 49160 | tf_op jit(solution)/shard_map/ppermute | solution.py:518
  21.7 0.7 %collective-permute-start.8 = (f32[8,512]{1,0:T(8,128)S(1)}, f32[8,512]{1,0:T(8,128)S(1)}, u32[]{:S(2)}, u32[]{:S(2)}) collective-permute-start(f32[8,512]{1,0:T(8,128)S(1)} %get-tuple-element.101.far), channel_id=1, source_target_pairs={{0,2},{1,3},{2,4},{3,5},{4,6},{5,7},{6,0},{7,1},{8,10},{9,11},{10,... | collective-permute-start | bytes 49160 | tf_op jit(solution)/shard_map/ppermute | solution.py:518
  22.5 0.4 %merge.1 = (f32[8,8,1152]{2,1,0:T(8,128)S(1)}, f32[8,8,1152]{2,1,0:T(8,128)S(1)}, f32[8,8,1152]{2,1,0:T(8,128)S(1)}, f32[8,8,1152]{2,1,0:T(8,128)S(1)}, f32[9,8,...) custom-call(f32[8,8,1024]{2,1,0:T(8,128)S(1)} %get-tuple-element.103, ...), custom_call_target="tpu_custom_call" | custom-call | tf_op jit(solution)/shard_map/merge/pallas_call | solution.py:588
  22.9 1.3 %collective-permute-done.9.far_below = f32[8,512]{1,0:T(8,128)S(1)} collective-permute-done((f32[8,512]{1,0:T(8,128)S(1)}, f32[8,512]{1,0:T(8,128)S(1)}, u32[]{:S(2)}, u32[]{:S(2)}) %collective-permute-start.9) | collective-permute-done | bytes 16416 | tf_op jit(solution)/shard_map/ppermute | solution.py:518
  24.2 2.5 %collective-permute-done.8.far_above = f32[8,512]{1,0:T(8,128)S(1)} collective-permute-done((f32[8,512]{1,0:T(8,128)S(1)}, f32[8,512]{1,0:T(8,128)S(1)}, u32[]{:S(2)}, u32[]{:S(2)}) %collective-permute-start.8) | collective-permute-done | bytes 16416 | tf_op jit(solution)/shard_map/ppermute | solution.py:518
  26.7 0.0 collective-permute-done.7.near_odd
  26.7 0.0 collective-permute-done.6.near_even
  26.7 3.5 %up.1 = f32[2,32,1024]{2,1,0:T(8,128)} custom-call(f32[8,512]{1,0:T(8,128)S(1)} %get-tuple-element.101.far, f32[8,2048]{1,0:T(8,128)S(1)} %collective-permute-done.6.near_even, f32[8,2048]{1,0:T(8,128)S(1)} %collective-permute-done.7.near_odd, f32[8,512]{1,0:T(8,128)S(1)} %collective-permute-done.8.far_above, f32[8,512]{1,0:T(8,128)S(1)} %collective-permute-done.9.far_below, ...), custom_call_target="tpu_custom_call" | custom-call | tf_op jit(solution)/shard_map/up/pallas_call | solution.py:597
  (4 shorter events, 0.0 us)
Async XLA Ops:
  0.0 13.8 %copy-start = (f32[2,32,1024]{2,1,0:T(8,128)S(1)}, f32[2,32,1024]{2,1,0:T(8,128)}, u32[]{:S(2)}) copy-start(f32[2,32,1024]{2,1,0:T(8,128)} %forcing.5) | copy-start | bytes 786436
  1.5 5.0 %collective-permute-start = (f32[4,32,128]{2,1,0:T(8,128)S(1)}, f32[4,32,128]{2,1,0:T(8,128)S(1)}, u32[]{:S(2)}, u32[]{:S(2)}) collective-permute-start(f32[4,32,128]{2,1,0:T(8,128)S(1)} %get-tuple-element.90), channel_id=1, source_target_pairs={{0,8},{8,0},{16,24},{24,16},{32,40},{40,32},{48,56},{56,48},{64,72... | collective-permute-start | bytes 196616 | tf_op jit(solution)/shard_map/ppermute | solution.py:513
  3.2 7.6 %collective-permute-start.1 = (f32[4,32,128]{2,1,0:T(8,128)S(1)}, f32[4,32,128]{2,1,0:T(8,128)S(1)}, u32[]{:S(2)}, u32[]{:S(2)}) collective-permute-start(f32[4,32,128]{2,1,0:T(8,128)S(1)} %get-tuple-element.91), channel_id=1, source_target_pairs={{8,16},{16,8},{24,32},{32,24},{40,48},{48,40},{56,64},{64,56},{72,... | collective-permute-start | bytes 196616 | tf_op jit(solution)/shard_map/ppermute | solution.py:513
  4.9 8.9 %collective-permute-start.3 = (f32[4,16,1024]{2,1,0:T(8,128)S(1)}, f32[4,16,1024]{2,1,0:T(8,128)S(1)}, u32[]{:S(2)}, u32[]{:S(2)}) collective-permute-start(f32[4,16,1024]{2,1,0:T(8,128)S(1)} %get-tuple-element.95), channel_id=1, source_target_pairs={{1,2},{2,1},{3,4},{4,3},{5,6},{6,5},{0,7},{7,0},{9,10},{10,9},{11,... | collective-permute-start | bytes 786440 | tf_op jit(solution)/shard_map/ppermute | solution.py:513
  10.8 3.1 %collective-permute-start.2 = (f32[4,16,1024]{2,1,0:T(8,128)S(1)}, f32[4,16,1024]{2,1,0:T(8,128)S(1)}, u32[]{:S(2)}, u32[]{:S(2)}) collective-permute-start(f32[4,16,1024]{2,1,0:T(8,128)S(1)} %get-tuple-element.94), channel_id=1, source_target_pairs={{0,1},{1,0},{2,3},{3,2},{4,5},{5,4},{6,7},{7,6},{8,9},{9,8},{10,11... | collective-permute-start | bytes 786440 | tf_op jit(solution)/shard_map/ppermute | solution.py:513
  10.9 5.7 %collective-permute-start.4 = (f32[4,16,256]{2,1,0:T(8,128)S(1)}, f32[4,16,256]{2,1,0:T(8,128)S(1)}, u32[]{:S(2)}, u32[]{:S(2)}) collective-permute-start(f32[4,16,256]{2,1,0:T(8,128)S(1)} %get-tuple-element.96), channel_id=1, source_target_pairs={{0,1},{1,0},{2,3},{3,2},{4,5},{5,4},{6,7},{7,6},{8,9},{9,8},{10,11... | collective-permute-start | bytes 196616 | tf_op jit(solution)/shard_map/ppermute | solution.py:513
  11.4 5.3 %collective-permute-start.5 = (f32[4,16,256]{2,1,0:T(8,128)S(1)}, f32[4,16,256]{2,1,0:T(8,128)S(1)}, u32[]{:S(2)}, u32[]{:S(2)}) collective-permute-start(f32[4,16,256]{2,1,0:T(8,128)S(1)} %get-tuple-element.97), channel_id=1, source_target_pairs={{1,2},{2,1},{3,4},{4,3},{5,6},{6,5},{0,7},{7,0},{9,10},{10,9},{11,... | collective-permute-start | bytes 196616 | tf_op jit(solution)/shard_map/ppermute | solution.py:513
  18.3 8.4 %collective-permute-start.7 = (f32[8,2048]{1,0:T(8,128)S(1)}, f32[8,2048]{1,0:T(8,128)S(1)}, u32[]{:S(2)}, u32[]{:S(2)}) collective-permute-start(f32[8,2048]{1,0:T(8,128)S(1)} %get-tuple-element.102), channel_id=1, source_target_pairs={{1,2},{2,1},{3,4},{4,3},{5,6},{6,5},{0,7},{7,0},{9,10},{10,9},{11,... | collective-permute-start | bytes 196616 | tf_op jit(solution)/shard_map/ppermute | solution.py:513
  20.4 6.2 %collective-permute-start.6 = (f32[8,2048]{1,0:T(8,128)S(1)}, f32[8,2048]{1,0:T(8,128)S(1)}, u32[]{:S(2)}, u32[]{:S(2)}) collective-permute-start(f32[8,2048]{1,0:T(8,128)S(1)} %get-tuple-element.102), channel_id=1, source_target_pairs={{0,1},{1,0},{2,3},{3,2},{4,5},{5,4},{6,7},{7,6},{8,9},{9,8},{10,11... | collective-permute-start | bytes 196616 | tf_op jit(solution)/shard_map/ppermute | solution.py:513
  20.4 3.7 %collective-permute-start.9 = (f32[8,512]{1,0:T(8,128)S(1)}, f32[8,512]{1,0:T(8,128)S(1)}, u32[]{:S(2)}, u32[]{:S(2)}) collective-permute-start(f32[8,512]{1,0:T(8,128)S(1)} %get-tuple-element.101.far), channel_id=1, source_target_pairs={{0,6},{1,7},{2,0},{3,1},{4,2},{5,3},{6,4},{7,5},{8,14},{9,15},{10,... | collective-permute-start | bytes 49160 | tf_op jit(solution)/shard_map/ppermute | solution.py:518
  21.7 5.0 %collective-permute-start.8 = (f32[8,512]{1,0:T(8,128)S(1)}, f32[8,512]{1,0:T(8,128)S(1)}, u32[]{:S(2)}, u32[]{:S(2)}) collective-permute-start(f32[8,512]{1,0:T(8,128)S(1)} %get-tuple-element.101.far), channel_id=1, source_target_pairs={{0,2},{1,3},{2,4},{3,5},{4,6},{5,7},{6,0},{7,1},{8,10},{9,11},{10,... | collective-permute-start | bytes 49160 | tf_op jit(solution)/shard_map/ppermute | solution.py:518

commit v6 on v5

--- a/solution.py
+++ b/solution.py
@@ -355,7 +355,7 @@
         for i in range(COLS // 128):
             cols = slice(128 * i, 128 * i + 128)
             halo = (rows_even[row, :, cols], rows_odd[row, :, cols])
-            spread(halo, source[row % 2, :, cols], halo, natural.at[(8 * row + i) % 2], target, cols)
+            spread(halo, source[row % 2, :, cols], halo, natural.at[8 * row + i], target, cols)
     for i, value in enumerate(descend(levels, etas, betas, diags, others)):
         top[i] = value
 
@@ -390,7 +390,7 @@
                 part = slice(0, EDGE) if i == 1 else slice(COLS - EDGE, COLS)
                 halo = (rows_even[row, :, part], rows_odd[row, :, part])
                 own = source[row % 2, :, part]
-            spread(halo, own, halo, natural.at[i % 2], target, slice(128 * i, 128 * i + 128))
+            spread(halo, own, halo, natural.at[4 * row + i], target, slice(128 * i, 128 * i + 128))
     rim = descend(levels, etas, betas, diags, others)
     both = [merge(3, top[i], rim[i]) for i in range(4)]
     head = jnp.concatenate([own_rows(both[0], both[1]), own_rows(both[2], both[3])], axis=1)
@@ -405,9 +405,38 @@
 
 
 def merge_kernel(*refs):
-    for level in range(3):
+    late = refs[48:]
+    mains, rims = levels_of(refs[:24]), levels_of(refs[24:48])
+
+    def joined(name, *index):
+        return merge(0, getattr(mains[0], name)[index], getattr(rims[0], name)[index])
+
+    names = ("right", "left", "cross_right", "cross_left", "scale")
+    for i, name in enumerate(names):
+        for p in range(8):
+            value = joined(name, p)
+            late[i][p] = own_rows(value, value)
+            if p in (0, 7):
+                late[8][i, p // 7] = value
+    for p in range(9):
+        value = joined("below", p)
+        late[5][p] = own_rows(value, value)
+        if p in (0, 1, 7, 8):
+            late[9][(0, 1, 7, 8).index(p)] = value
+    for p in range(8):
+        force = [joined("force", k, p) for k in range(2)]
+        field = [joined("field", k, p + 1) for k in range(2)]
+        late[6][p] = own_rows(force[0], force[1])
+        late[7][p] = own_rows(field[0], field[1])
+        for k in range(2):
+            if p in (0, 7):
+                late[10][k, p // 7] = force[k]
+            if p in (0, 1, 6, 7):
+                late[11][k, (0, 1, 6, 7).index(p)] = field[k]
+    for level in (1, 2):
         for i in range(8):
-            main, rim, target = (refs[24 * j + 8 * level + i] for j in range(3))
+            main, rim = (refs[24 * j + 8 * level + i] for j in range(2))
+            target = late[4 + 8 * level + i]
             planes = PLANES[level]
             if i < 6:
                 for p in range(main.shape[0]):
@@ -418,10 +447,99 @@
                         target[k, p] = merge(level, main[k, p], rim[k, p])
 
 
+def finest_up(refs, coarse, packed, next_packed, natural, velocity, sems):
+    right, left, cross_right, cross_left, scale, below, force, field = refs[:8]
+    edge_coef, edge_below, edge_force, edge_field = refs[8:]
+    wide = MERGED[0]
+    edges = [[None] * 8, [None] * 8]
+    for p in range(0, 8, 2):
+        adds = [double_lanes(coarse(k, p // 2), wide) for k in range(2)]
+        both = own_rows(adds[0], adds[1])
+        for q in (p, p + 1):
+            packed[q] = field[q] + both
+            if q in (0, 1, 6, 7):
+                for k in range(2):
+                    edges[k][q] = edge_field[k, (0, 1, 6, 7).index(q)] + adds[k]
+    found = {}
+    for i, p in enumerate((0, 7)):
+        under = [edges[k][1] if p == 0 else from_below(edges[k][0]) for k in range(2)]
+        over = [from_above(edges[k][7]) if p == 0 else edges[k][6] for k in range(2)]
+        for k in range(2):
+            terms = gather_terms(
+                edge_coef[0, i],
+                edge_coef[1, i],
+                edge_coef[2, i],
+                edge_coef[3, i],
+                edge_below[2 * i + 1],
+                edge_below[2 * i],
+                edges[k][p],
+                under[k],
+                over[k],
+                under[1 - k] - over[1 - k],
+                edge_force[k, i],
+            )
+            found[k, p] = KEEP * edges[k][p] + edge_coef[4, i] * terms
+    next_packed[1] = own_rows(found[0, 0], found[1, 0])
+    next_packed[8] = own_rows(found[0, 7], found[1, 7])
+    next_packed[0] = own_rows(from_above(found[0, 7]), from_above(found[1, 7]))
+    next_packed[9] = own_rows(from_below(found[0, 0]), from_below(found[1, 0]))
+
+    def sweep(p, above, here, under, first, count, part):
+        mid = slice(128, 128 + 128 * count)
+        low, high = slice(0, 128 + 128 * count), slice(128, 256 + 128 * count)
+        over, w, down = part(above), part(here), part(under)
+        step = pltpu.roll(down - over, 4, axis=0)
+        west = from_left((part(right[p]) * w + part(cross_right[p]) * step)[:, low])[:, 128:]
+        east = from_right((part(left[p]) * w - part(cross_left[p]) * step)[:, high])[:, : 128 * count]
+        cols = slice(128 * first, 128 * (first + count))
+        terms = (force[p][:, cols] + (west + east)) + (below[p + 1][:, cols] * down[:, mid] + below[p][:, cols] * over[:, mid])
+        return KEEP * w[:, mid] + scale[p][:, cols] * terms
+
+    for p in range(1, 7):
+        over, here, under = packed[p - 1], packed[p], packed[p + 1]
+        terms = gather_terms(
+            right[p],
+            left[p],
+            cross_right[p],
+            cross_left[p],
+            below[p + 1],
+            below[p],
+            here,
+            under,
+            over,
+            pltpu.roll(under - over, 4, axis=0),
+            force[p],
+        )
+        next_packed[p + 1] = KEEP * here + scale[p] * terms
+    copies = []
+    first = 0
+    for count in (4, 2, 2):
+
+        def part(x):
+            end = x[:, 128 * max(first - 1, 0) : 128 * (first + count + 1)]
+            return end if first else jnp.concatenate([x[:, wide - 128 :], end], axis=1)
+
+        for p in range(8):
+            done = sweep(p, next_packed[p], next_packed[p + 1], next_packed[p + 2], first, count, part)
+            for i in range(count):
+                tile = done[:, 128 * i : 128 * i + 128]
+                for k in range(2):
+                    natural[k, first + i, pl.ds(p, 4, stride=8), :] = tile[4 * k : 4 * k + 4]
+        for i in range(first, first + count):
+            for k in range(2):
+                target = velocity.at[k, :, pl.ds(128 * i, 128)]
+                copy = pltpu.make_async_copy(natural.at[k, i], target, sems.at[2 * i + k])
+                copy.start()
+                copies.append(copy)
+        first += count
+    for copy in copies:
+        copy.wait()
+
+
 def up_kernel(far, near_even, near_odd, far_above, far_below, *refs):
-    levels = levels_of(refs)
-    velocity, natural, late_force, late_field = refs[24:28]
-    fields, others = refs[28:31], refs[31:34]
+    levels = [None] + [Level(PLANES[i], refs[4 + 8 * i : 12 + 8 * i]) for i in (1, 2)]
+    velocity, natural, sems, packed, next_packed, late_force, late_field = refs[28:35]
+    fields, others = (None,) + refs[35:37], (None,) + refs[37:39]
     gy = lax.axis_index("gy")
     count = lax.axis_size("gy")
     even = gy % 2 == 0
@@ -487,15 +605,10 @@
     levels[2].force = late_force
     levels[2].field = late_field
     coarse = lambda k, p: coarsest[k]
-    for level in (2, 1, 0):
+    for level in (2, 1):
         levels[level].last_sweeps(coarse, fields[level], others[level])
         coarse = lambda k, p, result=fields[level]: result[k, p + 1]
-    for k in range(2):
-        for i in range(COLS // 128):
-            for p in range(8):
-                part = fields[0][k, p + 1, :, 128 * i : 128 * i + 128]
-                natural[i, pl.ds(p, 4, stride=8), :] = pltpu.roll(part, 6, axis=0)[0:4]
-            velocity[k, :, 128 * i : 128 * i + 128] = natural[i]
+    finest_up(refs[:12], coarse, packed, next_packed, natural, velocity, sems)
 
 
 def swap(x, axis, odd):
@@ -560,7 +673,7 @@
         return [(2, PLANES[i] + 2, 8, widths[i]) for i in range(3)]
 
     def work(widths):
-        return scratch([(2, 64, 128)] + [(PLANES[i], 8, widths[i]) for i in range(3)] * 3 + rims(widths))
+        return scratch([(32, 64, 128)] + [(PLANES[i], 8, widths[i]) for i in range(3)] * 3 + rims(widths))
 
     *main, top = pl.pallas_call(
         main_kernel,
@@ -585,21 +698,26 @@
     near_odd = swap(near, "gy", 1)
     far_above = turn(far, "gy", 2)
     far_below = turn(far, "gy", -2)
+    wide = MERGED[0]
+    finest = [(8, 8, wide)] * 5 + [(9, 8, wide)] + [(8, 8, wide)] * 2
+    finest += [(5, 2, 8, wide), (4, 8, wide), (2, 2, 8, wide), (2, 4, 8, wide)]
     merged = pl.pallas_call(
         merge_kernel,
-        out_shape=tuple(shape(*dims) for dims in kept(MERGED)),
+        out_shape=tuple(shape(*dims) for dims in finest + kept(MERGED)[8:]),
         in_specs=vmem(48),
-        out_specs=tuple(vmem(24)),
+        out_specs=tuple(vmem(28)),
         compiler_params=params(),
         name="merge",
     )(*main, *rim)
-    late = [(2, 2, 8, MERGED[2]), (2, 4, 8, MERGED[2])]
+    late = [(8, 8, wide), (10, 8, wide), (2, 2, 8, MERGED[2]), (2, 4, 8, MERGED[2])]
     return pl.pallas_call(
         up_kernel,
         out_shape=shape(2, ROWS, COLS),
-        in_specs=vmem(29),
-        out_specs=vmem(1)[0],
-        scratch_shapes=scratch([(COLS // 128, ROWS, 128)] + late + rims(MERGED) + rims(MERGED)),
+        in_specs=vmem(33),
+        out_specs=pl.BlockSpec(memory_space=pltpu.HBM),
+        scratch_shapes=scratch([(2, COLS // 128, ROWS, 128)])
+        + [pltpu.SemaphoreType.DMA((2 * COLS // 128,))]
+        + scratch(late + rims(MERGED)[1:] + rims(MERGED)[1:]),
         compiler_params=params(),
         name="up",
     )(far, near_even, near_odd, far_above, far_below, *merged)

time: 30.2 us -> 29.4 us (0.974)
  Pallas kernels: 9.75 us -> 9.05 us
    pallas_call x2, Pallas kernels: 3.84 us -> 3.44 us  [the longest x1 2.96 us: local(): pl.pallas_call(up_kernel, out_shape=shape(2, ROWS, COLS), in_specs=vmem(3...]
where the time goes in v6:
time: 29.4 us; the launch traced here: 29.3 us
  starting transfers between devices  12.4 us (42%)
  Pallas kernels  9.05 us (31%)
  waiting for transfers between devices  7.78 us (26%)
    ppermute x8, starting transfers between devices, swap(): lax.ppermute(x, ('gx', 'gy'), [(place(*a), place(*b)) for a, b in pairs])  10.4 us
    ppermute x8, waiting for transfers between devices, swap(): lax.ppermute(x, ('gx', 'gy'), [(place(*a), place(*b)) for a, b in pairs])  4.25 us
    ppermute x2, waiting for transfers between devices, turn(): lax.ppermute(x, axis, [(i, (i + step) % count) for i in range(count)])  3.53 us
    pallas_call x1, Pallas kernels, local(): pl.pallas_call(up_kernel, out_shape=shape(2, ROWS, COLS), in_specs=vmem(3...  2.96 us
    pallas_call x1, Pallas kernels, local(): pl.pallas_call(main_kernel, out_shape=tuple((shape(*dims) for dims in kep...  2.57 us
    ppermute x2, starting transfers between devices, turn(): lax.ppermute(x, axis, [(i, (i + step) % count) for i in range(count)])  2.03 us
    pallas_call x1, Pallas kernels, local(): pl.pallas_call(rim_kernel, out_shape=tuple((shape(*dims) for dims in kept...  1.53 us
    pallas_call x1, Pallas kernels, local(): pl.pallas_call(lookup_kernel, out_shape=(shape(2, ROWS, COLS),) + (shape(...  1.5 us
  transfers between devices with their start and end apart: 10, of which 3 were waited for; matrix products, arithmetic and copies ran while one was open for 0% of the time, Pallas kernels for 10%

profile of v6, /device:TPU:128, one launch (start us, length us, event | category | flops | bytes accessed | tf_op | source)
XLA Modules:
  0.0 29.3 jit_solution(10878591644878642237)
XLA Ops:
  0.0 1.5 %lookup.1 = (f32[2,32,1024]{2,1,0:T(8,128)S(1)}, f32[4,32,128]{2,1,0:T(8,128)S(1)}, f32[4,32,128]{2,1,0:T(8,128)S(1)}, f32[4,16,1024]{2,1,0:T(8,128)S(1)}, f32[4,16,1024]{2,1,0:T(8,128)S(1)}) custom-call(f32[16]{0:T(128)} %v_table.1, f32[16]{0:T(128)} %d_table.1, f32[2,32,1024]{2,1,0:T(8,128)} %forcing.5, s32[32,1024]{1,0:T(8,128)} %mask.1, ...), custom_call_target="tpu_custom_call" | custom-call | tf_op jit(solution)/shard_map/lookup/pallas_call | solution.py:641
  1.5 1.7 %collective-permute-start = (f32[4,32,128]{2,1,0:T(8,128)S(1)}, f32[4,32,128]{2,1,0:T(8,128)S(1)}, u32[]{:S(2)}, u32[]{:S(2)}) collective-permute-start(f32[4,32,128]{2,1,0:T(8,128)S(1)} %get-tuple-element.94), channel_id=1, source_target_pairs={{0,8},{8,0},{16,24},{24,16},{32,40},{40,32},{48,56},{56,48},{64,72... | collective-permute-start | bytes 196616 | tf_op jit(solution)/shard_map/ppermute | solution.py:626
  3.2 1.7 %collective-permute-start.1 = (f32[4,32,128]{2,1,0:T(8,128)S(1)}, f32[4,32,128]{2,1,0:T(8,128)S(1)}, u32[]{:S(2)}, u32[]{:S(2)}) collective-permute-start(f32[4,32,128]{2,1,0:T(8,128)S(1)} %get-tuple-element.95), channel_id=1, source_target_pairs={{8,16},{16,8},{24,32},{32,24},{40,48},{48,40},{56,64},{64,56},{72,... | collective-permute-start | bytes 196616 | tf_op jit(solution)/shard_map/ppermute | solution.py:626
  4.9 1.6 %collective-permute-start.3 = (f32[4,16,1024]{2,1,0:T(8,128)S(1)}, f32[4,16,1024]{2,1,0:T(8,128)S(1)}, u32[]{:S(2)}, u32[]{:S(2)}) collective-permute-start(f32[4,16,1024]{2,1,0:T(8,128)S(1)} %get-tuple-element.99), channel_id=1, source_target_pairs={{1,2},{2,1},{3,4},{4,3},{5,6},{6,5},{0,7},{7,0},{9,10},{10,9},{11,... | collective-permute-start | bytes 786440 | tf_op jit(solution)/shard_map/ppermute | solution.py:626
  6.5 0.0 collective-permute-done.got_even
  6.5 4.2 %collective-permute-done.1.got_odd = f32[4,32,128]{2,1,0:T(8,128)S(1)} collective-permute-done((f32[4,32,128]{2,1,0:T(8,128)S(1)}, f32[4,32,128]{2,1,0:T(8,128)S(1)}, u32[]{:S(2)}, u32[]{:S(2)}) %collective-permute-start.1) | collective-permute-done | bytes 65568 | tf_op jit(solution)/shard_map/ppermute | solution.py:626
  10.8 0.1 collective-permute-start.2
  10.9 0.5 %collective-permute-start.4 = (f32[4,16,256]{2,1,0:T(8,128)S(1)}, f32[4,16,256]{2,1,0:T(8,128)S(1)}, u32[]{:S(2)}, u32[]{:S(2)}) collective-permute-start(f32[4,16,256]{2,1,0:T(8,128)S(1)} %get-tuple-element.100), channel_id=1, source_target_pairs={{0,1},{1,0},{2,3},{3,2},{4,5},{5,4},{6,7},{7,6},{8,9},{9,8},{10,11... | collective-permute-start | bytes 196616 | tf_op jit(solution)/shard_map/ppermute | solution.py:626
  11.4 2.5 %collective-permute-start.5 = (f32[4,16,256]{2,1,0:T(8,128)S(1)}, f32[4,16,256]{2,1,0:T(8,128)S(1)}, u32[]{:S(2)}, u32[]{:S(2)}) collective-permute-start(f32[4,16,256]{2,1,0:T(8,128)S(1)} %get-tuple-element.101), channel_id=1, source_target_pairs={{1,2},{2,1},{3,4},{4,3},{5,6},{6,5},{0,7},{7,0},{9,10},{10,9},{11,... | collective-permute-start | bytes 196616 | tf_op jit(solution)/shard_map/ppermute | solution.py:626
  13.8 0.0 collective-permute-done.3.rows_odd
  13.8 0.0 collective-permute-done.2.rows_even
  13.8 2.6 %main.1 = (f32[8,8,1024]{2,1,0:T(8,128)S(1)}, f32[8,8,1024]{2,1,0:T(8,128)S(1)}, f32[8,8,1024]{2,1,0:T(8,128)S(1)}, f32[8,8,1024]{2,1,0:T(8,128)S(1)}, f32[9,8,1...) custom-call(f32[2,32,1024]{2,1,0:T(8,128)S(1)} %copy-done, ...), custom_call_target="tpu_custom_call" | custom-call | tf_op jit(solution)/shard_map/main/pallas_call | solution.py:678
  16.4 0.0 collective-permute-done.4.corner_even
  16.4 0.0 collective-permute-done.5.corner_odd
  16.4 1.5 %rim.1 = (f32[8,8,512]{2,1,0:T(8,128)S(1)}, f32[8,8,512]{2,1,0:T(8,128)S(1)}, f32[8,8,512]{2,1,0:T(8,128)S(1)}, f32[8,8,512]{2,1,0:T(8,128)S(1)}, f32[9,8,512]{2...) custom-call(f32[2,32,1024]{2,1,0:T(8,128)S(1)} %copy-done, ...), custom_call_target="tpu_custom_call" | custom-call | tf_op jit(solution)/shard_map/rim/pallas_call | solution.py:688
  18.0 2.4 %collective-permute-start.7 = (f32[8,2048]{1,0:T(8,128)S(1)}, f32[8,2048]{1,0:T(8,128)S(1)}, u32[]{:S(2)}, u32[]{:S(2)}) collective-permute-start(f32[8,2048]{1,0:T(8,128)S(1)} %get-tuple-element.106), channel_id=1, source_target_pairs={{1,2},{2,1},{3,4},{4,3},{5,6},{6,5},{0,7},{7,0},{9,10},{10,9},{11,... | collective-permute-start | bytes 196616 | tf_op jit(solution)/shard_map/ppermute | solution.py:626
  20.3 0.0 collective-permute-start.6
  20.3 1.1 %collective-permute-start.9 = (f32[8,512]{1,0:T(8,128)S(1)}, f32[8,512]{1,0:T(8,128)S(1)}, u32[]{:S(2)}, u32[]{:S(2)}) collective-permute-start(f32[8,512]{1,0:T(8,128)S(1)} %get-tuple-element.105.far), channel_id=1, source_target_pairs={{0,6},{1,7},{2,0},{3,1},{4,2},{5,3},{6,4},{7,5},{8,14},{9,15},{10,... | collective-permute-start | bytes 49160 | tf_op jit(solution)/shard_map/ppermute | solution.py:631
  21.4 0.9 %collective-permute-start.8 = (f32[8,512]{1,0:T(8,128)S(1)}, f32[8,512]{1,0:T(8,128)S(1)}, u32[]{:S(2)}, u32[]{:S(2)}) collective-permute-start(f32[8,512]{1,0:T(8,128)S(1)} %get-tuple-element.105.far), channel_id=1, source_target_pairs={{0,2},{1,3},{2,4},{3,5},{4,6},{5,7},{6,0},{7,1},{8,10},{9,11},{10,... | collective-permute-start | bytes 49160 | tf_op jit(solution)/shard_map/ppermute | solution.py:631
  22.4 0.5 %merge.1 = (f32[8,8,1152]{2,1,0:T(8,128)S(1)}, f32[8,8,1152]{2,1,0:T(8,128)S(1)}, f32[8,8,1152]{2,1,0:T(8,128)S(1)}, f32[8,8,1152]{2,1,0:T(8,128)S(1)}, f32[8,8,...) custom-call(f32[8,8,1024]{2,1,0:T(8,128)S(1)} %get-tuple-element.107, ...), custom_call_target="tpu_custom_call" | custom-call | tf_op jit(solution)/shard_map/merge/pallas_call | solution.py:704
  22.8 1.2 %collective-permute-done.9.far_below = f32[8,512]{1,0:T(8,128)S(1)} collective-permute-done((f32[8,512]{1,0:T(8,128)S(1)}, f32[8,512]{1,0:T(8,128)S(1)}, u32[]{:S(2)}, u32[]{:S(2)}) %collective-permute-start.9) | collective-permute-done | bytes 16416 | tf_op jit(solution)/shard_map/ppermute | solution.py:631
  24.1 2.3 %collective-permute-done.8.far_above = f32[8,512]{1,0:T(8,128)S(1)} collective-permute-done((f32[8,512]{1,0:T(8,128)S(1)}, f32[8,512]{1,0:T(8,128)S(1)}, u32[]{:S(2)}, u32[]{:S(2)}) %collective-permute-start.8) | collective-permute-done | bytes 16416 | tf_op jit(solution)/shard_map/ppermute | solution.py:631
  26.4 0.0 collective-permute-done.7.near_odd
  26.4 3.0 %up.1 = f32[2,32,1024]{2,1,0:T(8,128)} custom-call(f32[8,512]{1,0:T(8,128)S(1)} %get-tuple-element.105.far, f32[8,2048]{1,0:T(8,128)S(1)} %collective-permute-done.6.near_even, f32[8,2048]{1,0:T(8,128)S(1)} %collective-permute-done.7.near_odd, f32[8,512]{1,0:T(8,128)S(1)} %collective-permute-done.8.far_above, f32[8,512]{1,0:T(8,128)S(1)} %collective-permute-done.9.far_below, ...), custom_call_target="tpu_custom_call" | custom-call | tf_op jit(solution)/shard_map/up/pallas_call | solution.py:713
  (4 shorter events, 0.0 us)
Async XLA Ops:
  0.0 13.8 %copy-start = (f32[2,32,1024]{2,1,0:T(8,128)S(1)}, f32[2,32,1024]{2,1,0:T(8,128)}, u32[]{:S(2)}) copy-start(f32[2,32,1024]{2,1,0:T(8,128)} %forcing.5) | copy-start | bytes 786436
  1.5 5.0 %collective-permute-start = (f32[4,32,128]{2,1,0:T(8,128)S(1)}, f32[4,32,128]{2,1,0:T(8,128)S(1)}, u32[]{:S(2)}, u32[]{:S(2)}) collective-permute-start(f32[4,32,128]{2,1,0:T(8,128)S(1)} %get-tuple-element.94), channel_id=1, source_target_pairs={{0,8},{8,0},{16,24},{24,16},{32,40},{40,32},{48,56},{56,48},{64,72... | collective-permute-start | bytes 196616 | tf_op jit(solution)/shard_map/ppermute | solution.py:626
  3.2 7.6 %collective-permute-start.1 = (f32[4,32,128]{2,1,0:T(8,128)S(1)}, f32[4,32,128]{2,1,0:T(8,128)S(1)}, u32[]{:S(2)}, u32[]{:S(2)}) collective-permute-start(f32[4,32,128]{2,1,0:T(8,128)S(1)} %get-tuple-element.95), channel_id=1, source_target_pairs={{8,16},{16,8},{24,32},{32,24},{40,48},{48,40},{56,64},{64,56},{72,... | collective-permute-start | bytes 196616 | tf_op jit(solution)/shard_map/ppermute | solution.py:626
  4.9 8.9 %collective-permute-start.3 = (f32[4,16,1024]{2,1,0:T(8,128)S(1)}, f32[4,16,1024]{2,1,0:T(8,128)S(1)}, u32[]{:S(2)}, u32[]{:S(2)}) collective-permute-start(f32[4,16,1024]{2,1,0:T(8,128)S(1)} %get-tuple-element.99), channel_id=1, source_target_pairs={{1,2},{2,1},{3,4},{4,3},{5,6},{6,5},{0,7},{7,0},{9,10},{10,9},{11,... | collective-permute-start | bytes 786440 | tf_op jit(solution)/shard_map/ppermute | solution.py:626
  10.8 3.1 %collective-permute-start.2 = (f32[4,16,1024]{2,1,0:T(8,128)S(1)}, f32[4,16,1024]{2,1,0:T(8,128)S(1)}, u32[]{:S(2)}, u32[]{:S(2)}) collective-permute-start(f32[4,16,1024]{2,1,0:T(8,128)S(1)} %get-tuple-element.98), channel_id=1, source_target_pairs={{0,1},{1,0},{2,3},{3,2},{4,5},{5,4},{6,7},{7,6},{8,9},{9,8},{10,11... | collective-permute-start | bytes 786440 | tf_op jit(solution)/shard_map/ppermute | solution.py:626
  10.9 5.6 %collective-permute-start.4 = (f32[4,16,256]{2,1,0:T(8,128)S(1)}, f32[4,16,256]{2,1,0:T(8,128)S(1)}, u32[]{:S(2)}, u32[]{:S(2)}) collective-permute-start(f32[4,16,256]{2,1,0:T(8,128)S(1)} %get-tuple-element.100), channel_id=1, source_target_pairs={{0,1},{1,0},{2,3},{3,2},{4,5},{5,4},{6,7},{7,6},{8,9},{9,8},{10,11... | collective-permute-start | bytes 196616 | tf_op jit(solution)/shard_map/ppermute | solution.py:626
  11.4 5.1 %collective-permute-start.5 = (f32[4,16,256]{2,1,0:T(8,128)S(1)}, f32[4,16,256]{2,1,0:T(8,128)S(1)}, u32[]{:S(2)}, u32[]{:S(2)}) collective-permute-start(f32[4,16,256]{2,1,0:T(8,128)S(1)} %get-tuple-element.101), channel_id=1, source_target_pairs={{1,2},{2,1},{3,4},{4,3},{5,6},{6,5},{0,7},{7,0},{9,10},{10,9},{11,... | collective-permute-start | bytes 196616 | tf_op jit(solution)/shard_map/ppermute | solution.py:626
  18.0 8.4 %collective-permute-start.7 = (f32[8,2048]{1,0:T(8,128)S(1)}, f32[8,2048]{1,0:T(8,128)S(1)}, u32[]{:S(2)}, u32[]{:S(2)}) collective-permute-start(f32[8,2048]{1,0:T(8,128)S(1)} %get-tuple-element.106), channel_id=1, source_target_pairs={{1,2},{2,1},{3,4},{4,3},{5,6},{6,5},{0,7},{7,0},{9,10},{10,9},{11,... | collective-permute-start | bytes 196616 | tf_op jit(solution)/shard_map/ppermute | solution.py:626
  20.3 6.0 %collective-permute-start.6 = (f32[8,2048]{1,0:T(8,128)S(1)}, f32[8,2048]{1,0:T(8,128)S(1)}, u32[]{:S(2)}, u32[]{:S(2)}) collective-permute-start(f32[8,2048]{1,0:T(8,128)S(1)} %get-tuple-element.106), channel_id=1, source_target_pairs={{0,1},{1,0},{2,3},{3,2},{4,5},{5,4},{6,7},{7,6},{8,9},{9,8},{10,11... | collective-permute-start | bytes 196616 | tf_op jit(solution)/shard_map/ppermute | solution.py:626
  20.3 3.7 %collective-permute-start.9 = (f32[8,512]{1,0:T(8,128)S(1)}, f32[8,512]{1,0:T(8,128)S(1)}, u32[]{:S(2)}, u32[]{:S(2)}) collective-permute-start(f32[8,512]{1,0:T(8,128)S(1)} %get-tuple-element.105.far), channel_id=1, source_target_pairs={{0,6},{1,7},{2,0},{3,1},{4,2},{5,3},{6,4},{7,5},{8,14},{9,15},{10,... | collective-permute-start | bytes 49160 | tf_op jit(solution)/shard_map/ppermute | solution.py:631
  21.4 4.9 %collective-permute-start.8 = (f32[8,512]{1,0:T(8,128)S(1)}, f32[8,512]{1,0:T(8,128)S(1)}, u32[]{:S(2)}, u32[]{:S(2)}) collective-permute-start(f32[8,512]{1,0:T(8,128)S(1)} %get-tuple-element.105.far), channel_id=1, source_target_pairs={{0,2},{1,3},{2,4},{3,5},{4,6},{5,7},{6,0},{7,1},{8,10},{9,11},{10,... | collective-permute-start | bytes 49160 | tf_op jit(solution)/shard_map/ppermute | solution.py:631

commit v7 on v6

--- a/solution.py
+++ b/solution.py
@@ -282,7 +282,7 @@
     return left, right
 
 
-def corner_kernel(got_even, got_odd, send_even, send_odd):
+def corner_kernel(got_odd, got_even, send_even, send_odd):
     for start, target in zip(halves_of("gy", ROWS, HALO), (send_even, send_odd)):
         rows = pl.ds(start, HALO)
         for row in range(4):
@@ -363,12 +363,12 @@
 def rim_kernel(
     forcing,
     coef,
+    got_odd,
     got_even,
-    got_odd,
     rows_even,
     rows_odd,
+    corner_odd,
     corner_even,
-    corner_odd,
     top,
     late_force,
     late_field,
@@ -618,9 +618,7 @@
     for j in range(across):
         for i in range(odd, count - 1, 2):
             pairs += [((i, j), (i + 1, j)), ((i + 1, j), (i, j))]
-        if odd and axis == "gy":
-            pairs += [((0, j), (count - 1, j)), ((count - 1, j), (0, j))]
-        elif odd:
+        if odd:
             pairs += [((i, j), (i, j ^ 1)) for i in (0, count - 1)]
     place = (lambda i, j: j * rows + i) if axis == "gy" else (lambda i, j: i * rows + j)
     return lax.ppermute(x, ("gx", "gy"), [(place(*a), place(*b)) for a, b in pairs])
@@ -647,8 +645,8 @@
         compiler_params=params(),
         name="lookup",
     )(*inputs)
+    got_odd = swap(side_odd, "gx", 1)
     got_even = swap(side_even, "gx", 0)
-    got_odd = swap(side_odd, "gx", 1)
     rows_odd = swap(main_odd, "gy", 1)
     send_even, send_odd = pl.pallas_call(
         corner_kernel,
@@ -657,11 +655,11 @@
         out_specs=tuple(vmem(2)),
         compiler_params=params(),
         name="corners",
-    )(got_even, got_odd)
+    )(got_odd, got_even)
     main_even, send_even = lax.optimization_barrier((main_even, send_even))
+    corner_odd = swap(send_odd, "gy", 1)
+    corner_even = swap(send_even, "gy", 0)
     rows_even = swap(main_even, "gy", 0)
-    corner_even = swap(send_even, "gy", 0)
-    corner_odd = swap(send_odd, "gy", 1)
 
     def kept(widths):
         return [dims for level in range(3) for dims in Level.shapes(level, widths)]
@@ -693,7 +691,7 @@
         scratch_shapes=work(RIM),
         compiler_params=params(),
         name="rim",
-    )(forcing, coef, got_even, got_odd, rows_even, rows_odd, corner_even, corner_odd, top, main[22], main[23])
+    )(forcing, coef, got_odd, got_even, rows_even, rows_odd, corner_odd, corner_even, top, main[22], main[23])
     near_even = swap(near, "gy", 0)
     near_odd = swap(near, "gy", 1)
     far_above = turn(far, "gy", 2)

time: 29.4 us -> 27.4 us (0.932)
  the two profiles are of different devices: /device:TPU:128 before, /device:TPU:160 now
where the time goes in v7:
time: 27.4 us; the launch traced here: 27.3 us
  starting transfers between devices  9.6 us (35%)
  Pallas kernels  9.04 us (33%)
  waiting for transfers between devices  8.64 us (32%)
    ppermute x8, starting transfers between devices, swap(): lax.ppermute(x, ('gx', 'gy'), [(place(*a), place(*b)) for a, b in pairs])  7.58 us
    ppermute x8, waiting for transfers between devices, swap(): lax.ppermute(x, ('gx', 'gy'), [(place(*a), place(*b)) for a, b in pairs])  4.44 us
    ppermute x2, waiting for transfers between devices, turn(): lax.ppermute(x, axis, [(i, (i + step) % count) for i in range(count)])  4.2 us
    pallas_call x1, Pallas kernels, local(): pl.pallas_call(up_kernel, out_shape=shape(2, ROWS, COLS), in_specs=vmem(3...  2.96 us
    pallas_call x1, Pallas kernels, local(): pl.pallas_call(main_kernel, out_shape=tuple((shape(*dims) for dims in kep...  2.56 us
    ppermute x2, starting transfers between devices, turn(): lax.ppermute(x, axis, [(i, (i + step) % count) for i in range(count)])  2.03 us
    pallas_call x1, Pallas kernels, local(): pl.pallas_call(rim_kernel, out_shape=tuple((shape(*dims) for dims in kept...  1.53 us
    pallas_call x1, Pallas kernels, local(): pl.pallas_call(lookup_kernel, out_shape=(shape(2, ROWS, COLS),) + (shape(...  1.5 us
  transfers between devices with their start and end apart: 10, of which 5 were waited for; matrix products, arithmetic and copies ran while one was open for 0% of the time, Pallas kernels for 11%

profile of v7, /device:TPU:160, one launch (start us, length us, event | category | flops | bytes accessed | tf_op | source)
XLA Modules:
  0.0 27.3 jit_solution(10987751167972689256)
XLA Ops:
  0.0 1.5 %lookup.1 = (f32[2,32,1024]{2,1,0:T(8,128)S(1)}, f32[4,32,128]{2,1,0:T(8,128)S(1)}, f32[4,32,128]{2,1,0:T(8,128)S(1)}, f32[4,16,1024]{2,1,0:T(8,128)S(1)}, f32[4,16,1024]{2,1,0:T(8,128)S(1)}) custom-call(f32[16]{0:T(128)} %v_table.1, f32[16]{0:T(128)} %d_table.1, f32[2,32,1024]{2,1,0:T(8,128)} %forcing.5, s32[32,1024]{1,0:T(8,128)} %mask.1, ...), custom_call_target="tpu_custom_call" | custom-call | tf_op jit(solution)/shard_map/lookup/pallas_call | solution.py:639
  1.5 3.5 %collective-permute-start = (f32[4,32,128]{2,1,0:T(8,128)S(1)}, f32[4,32,128]{2,1,0:T(8,128)S(1)}, u32[]{:S(2)}, u32[]{:S(2)}) collective-permute-start(f32[4,32,128]{2,1,0:T(8,128)S(1)} %get-tuple-element.94), channel_id=1, source_target_pairs={{8,16},{16,8},{24,32},{32,24},{40,48},{48,40},{56,64},{64,56},{72,... | collective-permute-start | bytes 196616 | tf_op jit(solution)/shard_map/ppermute | solution.py:624
  5.1 0.0 collective-permute-start.1
  5.1 2.0 %collective-permute-start.3 = (f32[4,16,1024]{2,1,0:T(8,128)S(1)}, f32[4,16,1024]{2,1,0:T(8,128)S(1)}, u32[]{:S(2)}, u32[]{:S(2)}) collective-permute-start(f32[4,16,1024]{2,1,0:T(8,128)S(1)} %get-tuple-element.99), channel_id=1, source_target_pairs={{1,2},{2,1},{3,4},{4,3},{5,6},{6,5},{0,8},{7,15},{9,10},{10,9},{11... | collective-permute-start | bytes 786440 | tf_op jit(solution)/shard_map/ppermute | solution.py:624
  7.1 0.9 %collective-permute-done.got_odd = f32[4,32,128]{2,1,0:T(8,128)S(1)} collective-permute-done((f32[4,32,128]{2,1,0:T(8,128)S(1)}, f32[4,32,128]{2,1,0:T(8,128)S(1)}, u32[]{:S(2)}, u32[]{:S(2)}) %collective-permute-start) | collective-permute-done | bytes 65568 | tf_op jit(solution)/shard_map/ppermute | solution.py:624
  8.0 1.3 %collective-permute-done.1.got_even = f32[4,32,128]{2,1,0:T(8,128)S(1)} collective-permute-done((f32[4,32,128]{2,1,0:T(8,128)S(1)}, f32[4,32,128]{2,1,0:T(8,128)S(1)}, u32[]{:S(2)}, u32[]{:S(2)}) %collective-permute-start.1) | collective-permute-done | bytes 65568 | tf_op jit(solution)/shard_map/ppermute | solution.py:624
  9.3 0.1 collective-permute-start.2
  9.4 0.5 %collective-permute-start.5 = (f32[4,16,256]{2,1,0:T(8,128)S(1)}, f32[4,16,256]{2,1,0:T(8,128)S(1)}, u32[]{:S(2)}, u32[]{:S(2)}) collective-permute-start(f32[4,16,256]{2,1,0:T(8,128)S(1)} %get-tuple-element.101), channel_id=1, source_target_pairs={{0,1},{1,0},{2,3},{3,2},{4,5},{5,4},{6,7},{7,6},{8,9},{9,8},{10,11... | collective-permute-start | bytes 196616 | tf_op jit(solution)/shard_map/ppermute | solution.py:624
  9.9 0.0 collective-permute-start.4
  9.9 2.2 %collective-permute-done.3.rows_odd = f32[4,16,1024]{2,1,0:T(8,128)S(1)} collective-permute-done((f32[4,16,1024]{2,1,0:T(8,128)S(1)}, f32[4,16,1024]{2,1,0:T(8,128)S(1)}, u32[]{:S(2)}, u32[]{:S(2)}) %collective-permute-start.3) | collective-permute-done | bytes 262176 | tf_op jit(solution)/shard_map/ppermute | solution.py:624
  12.1 0.0 collective-permute-done.2.rows_even
  12.1 2.6 %main.1 = (f32[8,8,1024]{2,1,0:T(8,128)S(1)}, f32[8,8,1024]{2,1,0:T(8,128)S(1)}, f32[8,8,1024]{2,1,0:T(8,128)S(1)}, f32[8,8,1024]{2,1,0:T(8,128)S(1)}, f32[9,8,1...) custom-call(f32[2,32,1024]{2,1,0:T(8,128)S(1)} %copy-done, ...), custom_call_target="tpu_custom_call" | custom-call | tf_op jit(solution)/shard_map/main/pallas_call | solution.py:676
  14.7 0.0 collective-permute-done.5.corner_even
  14.7 0.0 collective-permute-done.4.corner_odd
  14.7 1.5 %rim.1 = (f32[8,8,512]{2,1,0:T(8,128)S(1)}, f32[8,8,512]{2,1,0:T(8,128)S(1)}, f32[8,8,512]{2,1,0:T(8,128)S(1)}, f32[8,8,512]{2,1,0:T(8,128)S(1)}, f32[9,8,512]{2...) custom-call(f32[2,32,1024]{2,1,0:T(8,128)S(1)} %copy-done, ...), custom_call_target="tpu_custom_call" | custom-call | tf_op jit(solution)/shard_map/rim/pallas_call | solution.py:686
  16.3 1.4 %collective-permute-start.7 = (f32[8,2048]{1,0:T(8,128)S(1)}, f32[8,2048]{1,0:T(8,128)S(1)}, u32[]{:S(2)}, u32[]{:S(2)}) collective-permute-start(f32[8,2048]{1,0:T(8,128)S(1)} %get-tuple-element.106), channel_id=1, source_target_pairs={{1,2},{2,1},{3,4},{4,3},{5,6},{6,5},{0,8},{7,15},{9,10},{10,9},{11... | collective-permute-start | bytes 196616 | tf_op jit(solution)/shard_map/ppermute | solution.py:624
  17.7 0.0 collective-permute-start.6
  17.7 1.8 %collective-permute-start.9 = (f32[8,512]{1,0:T(8,128)S(1)}, f32[8,512]{1,0:T(8,128)S(1)}, u32[]{:S(2)}, u32[]{:S(2)}) collective-permute-start(f32[8,512]{1,0:T(8,128)S(1)} %get-tuple-element.105.far), channel_id=1, source_target_pairs={{0,6},{1,7},{2,0},{3,1},{4,2},{5,3},{6,4},{7,5},{8,14},{9,15},{10,... | collective-permute-start | bytes 49160 | tf_op jit(solution)/shard_map/ppermute | solution.py:629
  19.4 0.3 collective-permute-start.8
  19.7 0.5 %merge.1 = (f32[8,8,1152]{2,1,0:T(8,128)S(1)}, f32[8,8,1152]{2,1,0:T(8,128)S(1)}, f32[8,8,1152]{2,1,0:T(8,128)S(1)}, f32[8,8,1152]{2,1,0:T(8,128)S(1)}, f32[8,8,...) custom-call(f32[8,8,1024]{2,1,0:T(8,128)S(1)} %get-tuple-element.107, ...), custom_call_target="tpu_custom_call" | custom-call | tf_op jit(solution)/shard_map/merge/pallas_call | solution.py:702
  20.2 1.2 %collective-permute-done.9.far_below = f32[8,512]{1,0:T(8,128)S(1)} collective-permute-done((f32[8,512]{1,0:T(8,128)S(1)}, f32[8,512]{1,0:T(8,128)S(1)}, u32[]{:S(2)}, u32[]{:S(2)}) %collective-permute-start.9) | collective-permute-done | bytes 16416 | tf_op jit(solution)/shard_map/ppermute | solution.py:629
  21.4 3.0 %collective-permute-done.8.far_above = f32[8,512]{1,0:T(8,128)S(1)} collective-permute-done((f32[8,512]{1,0:T(8,128)S(1)}, f32[8,512]{1,0:T(8,128)S(1)}, u32[]{:S(2)}, u32[]{:S(2)}) %collective-permute-start.8) | collective-permute-done | bytes 16416 | tf_op jit(solution)/shard_map/ppermute | solution.py:629
  24.4 0.0 collective-permute-done.7.near_odd
  24.4 3.0 %up.1 = f32[2,32,1024]{2,1,0:T(8,128)} custom-call(f32[8,512]{1,0:T(8,128)S(1)} %get-tuple-element.105.far, f32[8,2048]{1,0:T(8,128)S(1)} %collective-permute-done.6.near_even, f32[8,2048]{1,0:T(8,128)S(1)} %collective-permute-done.7.near_odd, f32[8,512]{1,0:T(8,128)S(1)} %collective-permute-done.8.far_above, f32[8,512]{1,0:T(8,128)S(1)} %collective-permute-done.9.far_below, ...), custom_call_target="tpu_custom_call" | custom-call | tf_op jit(solution)/shard_map/up/pallas_call | solution.py:711
  (4 shorter events, 0.0 us)
Async XLA Ops:
  0.0 12.1 %copy-start = (f32[2,32,1024]{2,1,0:T(8,128)S(1)}, f32[2,32,1024]{2,1,0:T(8,128)}, u32[]{:S(2)}) copy-start(f32[2,32,1024]{2,1,0:T(8,128)} %forcing.5) | copy-start | bytes 786436
  1.5 6.5 %collective-permute-start = (f32[4,32,128]{2,1,0:T(8,128)S(1)}, f32[4,32,128]{2,1,0:T(8,128)S(1)}, u32[]{:S(2)}, u32[]{:S(2)}) collective-permute-start(f32[4,32,128]{2,1,0:T(8,128)S(1)} %get-tuple-element.94), channel_id=1, source_target_pairs={{8,16},{16,8},{24,32},{32,24},{40,48},{48,40},{56,64},{64,56},{72,... | collective-permute-start | bytes 196616 | tf_op jit(solution)/shard_map/ppermute | solution.py:624
  5.1 4.3 %collective-permute-start.1 = (f32[4,32,128]{2,1,0:T(8,128)S(1)}, f32[4,32,128]{2,1,0:T(8,128)S(1)}, u32[]{:S(2)}, u32[]{:S(2)}) collective-permute-start(f32[4,32,128]{2,1,0:T(8,128)S(1)} %get-tuple-element.95), channel_id=1, source_target_pairs={{0,8},{8,0},{16,24},{24,16},{32,40},{40,32},{48,56},{56,48},{64,72... | collective-permute-start | bytes 196616 | tf_op jit(solution)/shard_map/ppermute | solution.py:624
  5.1 7.1 %collective-permute-start.3 = (f32[4,16,1024]{2,1,0:T(8,128)S(1)}, f32[4,16,1024]{2,1,0:T(8,128)S(1)}, u32[]{:S(2)}, u32[]{:S(2)}) collective-permute-start(f32[4,16,1024]{2,1,0:T(8,128)S(1)} %get-tuple-element.99), channel_id=1, source_target_pairs={{1,2},{2,1},{3,4},{4,3},{5,6},{6,5},{0,8},{7,15},{9,10},{10,9},{11... | collective-permute-start | bytes 786440 | tf_op jit(solution)/shard_map/ppermute | solution.py:624
  9.3 2.8 %collective-permute-start.2 = (f32[4,16,1024]{2,1,0:T(8,128)S(1)}, f32[4,16,1024]{2,1,0:T(8,128)S(1)}, u32[]{:S(2)}, u32[]{:S(2)}) collective-permute-start(f32[4,16,1024]{2,1,0:T(8,128)S(1)} %get-tuple-element.98), channel_id=1, source_target_pairs={{0,1},{1,0},{2,3},{3,2},{4,5},{5,4},{6,7},{7,6},{8,9},{9,8},{10,11... | collective-permute-start | bytes 786440 | tf_op jit(solution)/shard_map/ppermute | solution.py:624
  9.4 5.3 %collective-permute-start.5 = (f32[4,16,256]{2,1,0:T(8,128)S(1)}, f32[4,16,256]{2,1,0:T(8,128)S(1)}, u32[]{:S(2)}, u32[]{:S(2)}) collective-permute-start(f32[4,16,256]{2,1,0:T(8,128)S(1)} %get-tuple-element.101), channel_id=1, source_target_pairs={{0,1},{1,0},{2,3},{3,2},{4,5},{5,4},{6,7},{7,6},{8,9},{9,8},{10,11... | collective-permute-start | bytes 196616 | tf_op jit(solution)/shard_map/ppermute | solution.py:624
  9.9 4.8 %collective-permute-start.4 = (f32[4,16,256]{2,1,0:T(8,128)S(1)}, f32[4,16,256]{2,1,0:T(8,128)S(1)}, u32[]{:S(2)}, u32[]{:S(2)}) collective-permute-start(f32[4,16,256]{2,1,0:T(8,128)S(1)} %get-tuple-element.100), channel_id=1, source_target_pairs={{1,2},{2,1},{3,4},{4,3},{5,6},{6,5},{0,8},{7,15},{9,10},{10,9},{11... | collective-permute-start | bytes 196616 | tf_op jit(solution)/shard_map/ppermute | solution.py:624
  16.3 8.1 %collective-permute-start.7 = (f32[8,2048]{1,0:T(8,128)S(1)}, f32[8,2048]{1,0:T(8,128)S(1)}, u32[]{:S(2)}, u32[]{:S(2)}) collective-permute-start(f32[8,2048]{1,0:T(8,128)S(1)} %get-tuple-element.106), channel_id=1, source_target_pairs={{1,2},{2,1},{3,4},{4,3},{5,6},{6,5},{0,8},{7,15},{9,10},{10,9},{11... | collective-permute-start | bytes 196616 | tf_op jit(solution)/shard_map/ppermute | solution.py:624
  17.7 6.7 %collective-permute-start.6 = (f32[8,2048]{1,0:T(8,128)S(1)}, f32[8,2048]{1,0:T(8,128)S(1)}, u32[]{:S(2)}, u32[]{:S(2)}) collective-permute-start(f32[8,2048]{1,0:T(8,128)S(1)} %get-tuple-element.106), channel_id=1, source_target_pairs={{0,1},{1,0},{2,3},{3,2},{4,5},{5,4},{6,7},{7,6},{8,9},{9,8},{10,11... | collective-permute-start | bytes 196616 | tf_op jit(solution)/shard_map/ppermute | solution.py:624
  17.7 3.7 %collective-permute-start.9 = (f32[8,512]{1,0:T(8,128)S(1)}, f32[8,512]{1,0:T(8,128)S(1)}, u32[]{:S(2)}, u32[]{:S(2)}) collective-permute-start(f32[8,512]{1,0:T(8,128)S(1)} %get-tuple-element.105.far), channel_id=1, source_target_pairs={{0,6},{1,7},{2,0},{3,1},{4,2},{5,3},{6,4},{7,5},{8,14},{9,15},{10,... | collective-permute-start | bytes 49160 | tf_op jit(solution)/shard_map/ppermute | solution.py:629
  19.4 4.9 %collective-permute-start.8 = (f32[8,512]{1,0:T(8,128)S(1)}, f32[8,512]{1,0:T(8,128)S(1)}, u32[]{:S(2)}, u32[]{:S(2)}) collective-permute-start(f32[8,512]{1,0:T(8,128)S(1)} %get-tuple-element.105.far), channel_id=1, source_target_pairs={{0,2},{1,3},{2,4},{3,5},{4,6},{5,7},{6,0},{7,1},{8,10},{9,11},{10,... | collective-permute-start | bytes 49160 | tf_op jit(solution)/shard_map/ppermute | solution.py:629

commit v8 on v7

--- a/solution.py
+++ b/solution.py
@@ -536,7 +536,7 @@
         copy.wait()
 
 
-def up_kernel(far, near_even, near_odd, far_above, far_below, *refs):
+def up_kernel(far, near_even, near_odd, far_even, far_odd, *refs):
     levels = [None] + [Level(PLANES[i], refs[4 + 8 * i : 12 + 8 * i]) for i in (1, 2)]
     velocity, natural, sems, packed, next_packed, late_force, late_field = refs[28:35]
     fields, others = (None,) + refs[35:37], (None,) + refs[37:39]
@@ -554,8 +554,9 @@
         return lax.broadcasted_iota(jnp.int32, like.shape, 0)
 
     def stacked(part):
-        m2 = jnp.where(gy < 2, 0.0, far_above[:, part])
-        p2 = jnp.where(gy > count - 3, 0.0, far_below[:, part])
+        low = gy // 2 % 2 == 0
+        m2 = jnp.where(gy < 2, 0.0, jnp.where(low, far_odd[:, part], far_even[:, part]))
+        p2 = jnp.where(gy > count - 3, 0.0, jnp.where(low, far_even[:, part], far_odd[:, part]))
         m1, p1, own = above(part), below(part), far[:, part]
         upper = sublanes(own) < 4
 
@@ -624,9 +625,15 @@
     return lax.ppermute(x, ("gx", "gy"), [(place(*a), place(*b)) for a, b in pairs])
 
 
-def turn(x, axis, step):
-    count = lax.axis_size(axis)
-    return lax.ppermute(x, axis, [(i, (i + step) % count) for i in range(count)])
+def swap_far(x, odd):
+    count = lax.axis_size("gy")
+    pairs = []
+    for i in range(0, count - 2):
+        if i // 2 % 2 == odd:
+            pairs += [(i, i + 2), (i + 2, i)]
+    if odd:
+        pairs += [(i, i ^ 1) for i in (0, 1, count - 2, count - 1)]
+    return lax.ppermute(x, "gy", pairs)
 
 
 def local(forcing, ice_mask, viscosity_class, drag_class, viscosity_table, drag_table):
@@ -694,8 +701,8 @@
     )(forcing, coef, got_odd, got_even, rows_even, rows_odd, corner_odd, corner_even, top, main[22], main[23])
     near_even = swap(near, "gy", 0)
     near_odd = swap(near, "gy", 1)
-    far_above = turn(far, "gy", 2)
-    far_below = turn(far, "gy", -2)
+    far_even = swap_far(far, 0)
+    far_odd = swap_far(far, 1)
     wide = MERGED[0]
     finest = [(8, 8, wide)] * 5 + [(9, 8, wide)] + [(8, 8, wide)] * 2
     finest += [(5, 2, 8, wide), (4, 8, wide), (2, 2, 8, wide), (2, 4, 8, wide)]
@@ -718,7 +725,7 @@
         + scratch(late + rims(MERGED)[1:] + rims(MERGED)[1:]),
         compiler_params=params(),
         name="up",
-    )(far, near_even, near_odd, far_above, far_below, *merged)
+    )(far, near_even, near_odd, far_even, far_odd, *merged)
 
 
 def solution(mesh):

time: 27.4 us -> 25.6 us (0.934)
  the two profiles are of different devices: /device:TPU:160 before, /device:TPU:162 now
where the time goes in v8:
time: 25.6 us; the launch traced here: 25.5 us
  Pallas kernels  9.02 us (35%)
  waiting for transfers between devices  8.39 us (33%)
  starting transfers between devices  8.03 us (31%)
    ppermute x8, starting transfers between devices, swap(): lax.ppermute(x, ('gx', 'gy'), [(place(*a), place(*b)) for a, b in pairs])  6.07 us
    ppermute x8, waiting for transfers between devices, swap(): lax.ppermute(x, ('gx', 'gy'), [(place(*a), place(*b)) for a, b in pairs])  5.14 us
    ppermute x2, waiting for transfers between devices, swap_far(): return lax.ppermute(x, 'gy', pairs)  3.25 us
    pallas_call x1, Pallas kernels, local(): pl.pallas_call(up_kernel, out_shape=shape(2, ROWS, COLS), in_specs=vmem(3...  2.97 us
    pallas_call x1, Pallas kernels, local(): pl.pallas_call(main_kernel, out_shape=tuple((shape(*dims) for dims in kep...  2.56 us
    ppermute x2, starting transfers between devices, swap_far(): return lax.ppermute(x, 'gy', pairs)  1.96 us
    pallas_call x1, Pallas kernels, local(): pl.pallas_call(rim_kernel, out_shape=tuple((shape(*dims) for dims in kept...  1.5 us
    pallas_call x1, Pallas kernels, local(): pl.pallas_call(lookup_kernel, out_shape=(shape(2, ROWS, COLS),) + (shape(...  1.5 us
  transfers between devices with their start and end apart: 10, of which 7 were waited for; matrix products, arithmetic and copies ran while one was open for 0% of the time, Pallas kernels for 12%

profile of v8, /device:TPU:162, one launch (start us, length us, event | category | flops | bytes accessed | tf_op | source)
XLA Modules:
  0.0 25.5 jit_solution(12535107639223381500)
XLA Ops:
  0.0 1.5 %lookup.1 = (f32[2,32,1024]{2,1,0:T(8,128)S(1)}, f32[4,32,128]{2,1,0:T(8,128)S(1)}, f32[4,32,128]{2,1,0:T(8,128)S(1)}, f32[4,16,1024]{2,1,0:T(8,128)S(1)}, f32[4,16,1024]{2,1,0:T(8,128)S(1)}) custom-call(f32[16]{0:T(128)} %v_table.1, f32[16]{0:T(128)} %d_table.1, f32[2,32,1024]{2,1,0:T(8,128)} %forcing.5, s32[32,1024]{1,0:T(8,128)} %mask.1, ...), custom_call_target="tpu_custom_call" | custom-call | tf_op jit(solution)/shard_map/lookup/pallas_call | solution.py:646
  1.5 3.5 %collective-permute-start = (f32[4,32,128]{2,1,0:T(8,128)S(1)}, f32[4,32,128]{2,1,0:T(8,128)S(1)}, u32[]{:S(2)}, u32[]{:S(2)}) collective-permute-start(f32[4,32,128]{2,1,0:T(8,128)S(1)} %get-tuple-element.94), channel_id=1, source_target_pairs={{8,16},{16,8},{24,32},{32,24},{40,48},{48,40},{56,64},{64,56},{72,... | collective-permute-start | bytes 196616 | tf_op jit(solution)/shard_map/ppermute | solution.py:625
  5.1 0.0 collective-permute-start.1
  5.1 0.0 collective-permute-start.3
  5.1 2.9 %collective-permute-done.got_odd = f32[4,32,128]{2,1,0:T(8,128)S(1)} collective-permute-done((f32[4,32,128]{2,1,0:T(8,128)S(1)}, f32[4,32,128]{2,1,0:T(8,128)S(1)}, u32[]{:S(2)}, u32[]{:S(2)}) %collective-permute-start) | collective-permute-done | bytes 65568 | tf_op jit(solution)/shard_map/ppermute | solution.py:625
  8.0 1.3 %collective-permute-done.1.got_even = f32[4,32,128]{2,1,0:T(8,128)S(1)} collective-permute-done((f32[4,32,128]{2,1,0:T(8,128)S(1)}, f32[4,32,128]{2,1,0:T(8,128)S(1)}, u32[]{:S(2)}, u32[]{:S(2)}) %collective-permute-start.1) | collective-permute-done | bytes 65568 | tf_op jit(solution)/shard_map/ppermute | solution.py:625
  9.3 0.1 collective-permute-start.2
  9.4 0.5 %collective-permute-start.5 = (f32[4,16,256]{2,1,0:T(8,128)S(1)}, f32[4,16,256]{2,1,0:T(8,128)S(1)}, u32[]{:S(2)}, u32[]{:S(2)}) collective-permute-start(f32[4,16,256]{2,1,0:T(8,128)S(1)} %get-tuple-element.101), channel_id=1, source_target_pairs={{0,1},{1,0},{2,3},{3,2},{4,5},{5,4},{6,7},{7,6},{8,9},{9,8},{10,11... | collective-permute-start | bytes 196616 | tf_op jit(solution)/shard_map/ppermute | solution.py:625
  9.9 0.2 collective-permute-start.4
  10.2 0.7 %collective-permute-done.3.rows_odd = f32[4,16,1024]{2,1,0:T(8,128)S(1)} collective-permute-done((f32[4,16,1024]{2,1,0:T(8,128)S(1)}, f32[4,16,1024]{2,1,0:T(8,128)S(1)}, u32[]{:S(2)}, u32[]{:S(2)}) %collective-permute-start.3) | collective-permute-done | bytes 262176 | tf_op jit(solution)/shard_map/ppermute | solution.py:625
  10.9 0.1 collective-permute-done.2.rows_even
  11.0 2.6 %main.1 = (f32[8,8,1024]{2,1,0:T(8,128)S(1)}, f32[8,8,1024]{2,1,0:T(8,128)S(1)}, f32[8,8,1024]{2,1,0:T(8,128)S(1)}, f32[8,8,1024]{2,1,0:T(8,128)S(1)}, f32[9,8,1...) custom-call(f32[2,32,1024]{2,1,0:T(8,128)S(1)} %copy-done, ...), custom_call_target="tpu_custom_call" | custom-call | tf_op jit(solution)/shard_map/main/pallas_call | solution.py:683
  13.5 0.0 collective-permute-done.5.corner_even
  13.5 0.1 collective-permute-done.4.corner_odd
  13.6 1.5 %rim.1 = (f32[8,8,512]{2,1,0:T(8,128)S(1)}, f32[8,8,512]{2,1,0:T(8,128)S(1)}, f32[8,8,512]{2,1,0:T(8,128)S(1)}, f32[8,8,512]{2,1,0:T(8,128)S(1)}, f32[9,8,512]{2...) custom-call(f32[2,32,1024]{2,1,0:T(8,128)S(1)} %copy-done, ...), custom_call_target="tpu_custom_call" | custom-call | tf_op jit(solution)/shard_map/rim/pallas_call | solution.py:693
  15.1 0.8 %collective-permute-start.7 = (f32[8,2048]{1,0:T(8,128)S(1)}, f32[8,2048]{1,0:T(8,128)S(1)}, u32[]{:S(2)}, u32[]{:S(2)}) collective-permute-start(f32[8,2048]{1,0:T(8,128)S(1)} %get-tuple-element.106), channel_id=1, source_target_pairs={{1,2},{2,1},{3,4},{4,3},{5,6},{6,5},{0,8},{7,15},{9,10},{10,9},{11... | collective-permute-start | bytes 196616 | tf_op jit(solution)/shard_map/ppermute | solution.py:625
  15.9 0.9 %collective-permute-start.6 = (f32[8,2048]{1,0:T(8,128)S(1)}, f32[8,2048]{1,0:T(8,128)S(1)}, u32[]{:S(2)}, u32[]{:S(2)}) collective-permute-start(f32[8,2048]{1,0:T(8,128)S(1)} %get-tuple-element.106), channel_id=1, source_target_pairs={{0,1},{1,0},{2,3},{3,2},{4,5},{5,4},{6,7},{7,6},{8,9},{9,8},{10,11... | collective-permute-start | bytes 196616 | tf_op jit(solution)/shard_map/ppermute | solution.py:625
  16.8 2.0 %collective-permute-start.9 = (f32[8,512]{1,0:T(8,128)S(1)}, f32[8,512]{1,0:T(8,128)S(1)}, u32[]{:S(2)}, u32[]{:S(2)}) collective-permute-start(f32[8,512]{1,0:T(8,128)S(1)} %get-tuple-element.105.far), channel_id=1, source_target_pairs={{2,4},{4,2},{3,5},{5,3},{0,1},{1,0},{6,7},{7,6},{10,12},{12,10},{1... | collective-permute-start | bytes 49160 | tf_op jit(solution)/shard_map/ppermute | solution.py:636
  18.8 0.0 collective-permute-start.8
  18.8 0.5 %merge.1 = (f32[8,8,1152]{2,1,0:T(8,128)S(1)}, f32[8,8,1152]{2,1,0:T(8,128)S(1)}, f32[8,8,1152]{2,1,0:T(8,128)S(1)}, f32[8,8,1152]{2,1,0:T(8,128)S(1)}, f32[8,8,...) custom-call(f32[8,8,1024]{2,1,0:T(8,128)S(1)} %get-tuple-element.107, ...), custom_call_target="tpu_custom_call" | custom-call | tf_op jit(solution)/shard_map/merge/pallas_call | solution.py:709
  19.3 1.3 %collective-permute-done.9.far_odd = f32[8,512]{1,0:T(8,128)S(1)} collective-permute-done((f32[8,512]{1,0:T(8,128)S(1)}, f32[8,512]{1,0:T(8,128)S(1)}, u32[]{:S(2)}, u32[]{:S(2)}) %collective-permute-start.9) | collective-permute-done | bytes 16416 | tf_op jit(solution)/shard_map/ppermute | solution.py:636
  20.6 2.0 %collective-permute-done.8.far_even = f32[8,512]{1,0:T(8,128)S(1)} collective-permute-done((f32[8,512]{1,0:T(8,128)S(1)}, f32[8,512]{1,0:T(8,128)S(1)}, u32[]{:S(2)}, u32[]{:S(2)}) %collective-permute-start.8) | collective-permute-done | bytes 16416 | tf_op jit(solution)/shard_map/ppermute | solution.py:636
  22.5 0.0 collective-permute-done.7.near_odd
  22.5 3.0 %up.1 = f32[2,32,1024]{2,1,0:T(8,128)} custom-call(f32[8,512]{1,0:T(8,128)S(1)} %get-tuple-element.105.far, f32[8,2048]{1,0:T(8,128)S(1)} %collective-permute-done.6.near_even, f32[8,2048]{1,0:T(8,128)S(1)} %collective-permute-done.7.near_odd, f32[8,512]{1,0:T(8,128)S(1)} %collective-permute-done.8.far_even, f32[8,512]{1,0:T(8,128)S(1)} %collective-permute-done.9.far_odd, ...), custom_call_target="tpu_custom_call" | custom-call | tf_op jit(solution)/shard_map/up/pallas_call | solution.py:718
  (4 shorter events, 0.0 us)
Async XLA Ops:
  0.0 11.0 %copy-start = (f32[2,32,1024]{2,1,0:T(8,128)S(1)}, f32[2,32,1024]{2,1,0:T(8,128)}, u32[]{:S(2)}) copy-start(f32[2,32,1024]{2,1,0:T(8,128)} %forcing.5) | copy-start | bytes 786436
  1.5 6.5 %collective-permute-start = (f32[4,32,128]{2,1,0:T(8,128)S(1)}, f32[4,32,128]{2,1,0:T(8,128)S(1)}, u32[]{:S(2)}, u32[]{:S(2)}) collective-permute-start(f32[4,32,128]{2,1,0:T(8,128)S(1)} %get-tuple-element.94), channel_id=1, source_target_pairs={{8,16},{16,8},{24,32},{32,24},{40,48},{48,40},{56,64},{64,56},{72,... | collective-permute-start | bytes 196616 | tf_op jit(solution)/shard_map/ppermute | solution.py:625
  5.1 4.3 %collective-permute-start.1 = (f32[4,32,128]{2,1,0:T(8,128)S(1)}, f32[4,32,128]{2,1,0:T(8,128)S(1)}, u32[]{:S(2)}, u32[]{:S(2)}) collective-permute-start(f32[4,32,128]{2,1,0:T(8,128)S(1)} %get-tuple-element.95), channel_id=1, source_target_pairs={{0,8},{8,0},{16,24},{24,16},{32,40},{40,32},{48,56},{56,48},{64,72... | collective-permute-start | bytes 196616 | tf_op jit(solution)/shard_map/ppermute | solution.py:625
  5.1 5.8 %collective-permute-start.3 = (f32[4,16,1024]{2,1,0:T(8,128)S(1)}, f32[4,16,1024]{2,1,0:T(8,128)S(1)}, u32[]{:S(2)}, u32[]{:S(2)}) collective-permute-start(f32[4,16,1024]{2,1,0:T(8,128)S(1)} %get-tuple-element.99), channel_id=1, source_target_pairs={{1,2},{2,1},{3,4},{4,3},{5,6},{6,5},{0,8},{7,15},{9,10},{10,9},{11... | collective-permute-start | bytes 786440 | tf_op jit(solution)/shard_map/ppermute | solution.py:625
  9.3 1.6 %collective-permute-start.2 = (f32[4,16,1024]{2,1,0:T(8,128)S(1)}, f32[4,16,1024]{2,1,0:T(8,128)S(1)}, u32[]{:S(2)}, u32[]{:S(2)}) collective-permute-start(f32[4,16,1024]{2,1,0:T(8,128)S(1)} %get-tuple-element.98), channel_id=1, source_target_pairs={{0,1},{1,0},{2,3},{3,2},{4,5},{5,4},{6,7},{7,6},{8,9},{9,8},{10,11... | collective-permute-start | bytes 786440 | tf_op jit(solution)/shard_map/ppermute | solution.py:625
  9.4 4.1 %collective-permute-start.5 = (f32[4,16,256]{2,1,0:T(8,128)S(1)}, f32[4,16,256]{2,1,0:T(8,128)S(1)}, u32[]{:S(2)}, u32[]{:S(2)}) collective-permute-start(f32[4,16,256]{2,1,0:T(8,128)S(1)} %get-tuple-element.101), channel_id=1, source_target_pairs={{0,1},{1,0},{2,3},{3,2},{4,5},{5,4},{6,7},{7,6},{8,9},{9,8},{10,11... | collective-permute-start | bytes 196616 | tf_op jit(solution)/shard_map/ppermute | solution.py:625
  9.9 3.7 %collective-permute-start.4 = (f32[4,16,256]{2,1,0:T(8,128)S(1)}, f32[4,16,256]{2,1,0:T(8,128)S(1)}, u32[]{:S(2)}, u32[]{:S(2)}) collective-permute-start(f32[4,16,256]{2,1,0:T(8,128)S(1)} %get-tuple-element.100), channel_id=1, source_target_pairs={{1,2},{2,1},{3,4},{4,3},{5,6},{6,5},{0,8},{7,15},{9,10},{10,9},{11... | collective-permute-start | bytes 196616 | tf_op jit(solution)/shard_map/ppermute | solution.py:625
  15.1 7.4 %collective-permute-start.7 = (f32[8,2048]{1,0:T(8,128)S(1)}, f32[8,2048]{1,0:T(8,128)S(1)}, u32[]{:S(2)}, u32[]{:S(2)}) collective-permute-start(f32[8,2048]{1,0:T(8,128)S(1)} %get-tuple-element.106), channel_id=1, source_target_pairs={{1,2},{2,1},{3,4},{4,3},{5,6},{6,5},{0,8},{7,15},{9,10},{10,9},{11... | collective-permute-start | bytes 196616 | tf_op jit(solution)/shard_map/ppermute | solution.py:625
  15.9 6.6 %collective-permute-start.6 = (f32[8,2048]{1,0:T(8,128)S(1)}, f32[8,2048]{1,0:T(8,128)S(1)}, u32[]{:S(2)}, u32[]{:S(2)}) collective-permute-start(f32[8,2048]{1,0:T(8,128)S(1)} %get-tuple-element.106), channel_id=1, source_target_pairs={{0,1},{1,0},{2,3},{3,2},{4,5},{5,4},{6,7},{7,6},{8,9},{9,8},{10,11... | collective-permute-start | bytes 196616 | tf_op jit(solution)/shard_map/ppermute | solution.py:625
  16.8 3.7 %collective-permute-start.9 = (f32[8,512]{1,0:T(8,128)S(1)}, f32[8,512]{1,0:T(8,128)S(1)}, u32[]{:S(2)}, u32[]{:S(2)}) collective-permute-start(f32[8,512]{1,0:T(8,128)S(1)} %get-tuple-element.105.far), channel_id=1, source_target_pairs={{2,4},{4,2},{3,5},{5,3},{0,1},{1,0},{6,7},{7,6},{10,12},{12,10},{1... | collective-permute-start | bytes 49160 | tf_op jit(solution)/shard_map/ppermute | solution.py:636
  18.8 3.7 %collective-permute-start.8 = (f32[8,512]{1,0:T(8,128)S(1)}, f32[8,512]{1,0:T(8,128)S(1)}, u32[]{:S(2)}, u32[]{:S(2)}) collective-permute-start(f32[8,512]{1,0:T(8,128)S(1)} %get-tuple-element.105.far), channel_id=1, source_target_pairs={{0,2},{2,0},{1,3},{3,1},{4,6},{6,4},{5,7},{7,5},{8,10},{10,8},{9,1... | collective-permute-start | bytes 49160 | tf_op jit(solution)/shard_map/ppermute | solution.py:636

commit v9 on v8

--- a/solution.py
+++ b/solution.py
@@ -243,15 +243,47 @@
     return first, pl.multiple_of(size - part - first, part)
 
 
+def group(index):
+    return (lane(1) >= 8 * index) & (lane(1) < 8 * index + 8)
+
+
+def pack_side(parts, side):
+    near = lane(1) < 64
+    out = []
+    for pair in (0, 2):
+        for r in range(4):
+            x, y = parts[pair][r], parts[pair + 1][r]
+            x, y = (x, pltpu.roll(y, 64, axis=1)) if side == 0 else (pltpu.roll(x, 64, axis=1), y)
+            out.append(jnp.where(near, x, y))
+    rest = jnp.zeros_like(out[0])
+    for i in range(16):
+        start = 64 if side == 0 else 56
+        rest = jnp.where(group(i), pltpu.roll(parts[i // 4][i % 4], (8 * i - start) % 128, axis=1), rest)
+    return out + [rest]
+
+
+def unpack_side(tile, side):
+    out = []
+    near = lane(1) < 64 if side == 0 else lane(1) >= 64
+    start = 64 if side == 0 else 56
+    for row in range(4):
+        for r in range(4):
+            x = tile[4 * (row // 2) + r]
+            if row % 2 == (0 if side else 1):
+                x = pltpu.roll(x, 64, axis=1)
+            rest = pltpu.roll(tile[8], (start - 8 * (4 * row + r)) % 128, axis=1)
+            out.append(jnp.where(near, x, jnp.where(group(start // 8), rest, 0.0)))
+    return out
+
+
 def lookup_kernel(v_table, d_table, forcing, mask, v_class, d_class, coef, *refs):
     sides, rows = refs[0:2], refs[2:4]
-    tables, ints, sems = refs[4:]
+    tables, ints, edges, sems = refs[4:]
     pairs = [(v_table, tables[0]), (d_table, tables[1])]
     pairs += [(source, ints.at[i]) for i, source in enumerate((mask, v_class, d_class))]
-    side_starts = halves_of("gx", COLS, EDGE)
     row_starts = halves_of("gy", ROWS, HALO)
-    for start, target in zip(side_starts, sides):
-        pairs.append((forcing.at[:, :, pl.ds(start, EDGE)], target.at[0:2]))
+    for i, start in enumerate((0, COLS - EDGE)):
+        pairs.append((forcing.at[:, :, pl.ds(start, EDGE)], edges.at[i]))
     for start, target in zip(row_starts, rows):
         pairs.append((forcing.at[:, pl.ds(start, HALO), :], target.at[0:2]))
     copies = start_all(pairs, sems)
@@ -264,31 +296,43 @@
             found = look_up(tables, [ints[(1,) + part], ints[(2,) + part]], ice)
             for k in range(2):
                 coef[(k,) + part] = found[k]
+    for copy in copies[5:7]:
+        copy.wait()
+    even = lax.axis_index("gx") % 2 == 0
+    messages = []
+    for side, start in enumerate((0, COLS - EDGE)):
+        parts = [[edges[side, k, 8 * r : 8 * r + 8] for r in range(4)] for k in range(2)]
+        parts += [[coef[k, 8 * r : 8 * r + 8, start : start + EDGE] for r in range(4)] for k in range(2)]
+        messages.append(pack_side(parts, side))
+    for i in range(9):
+        low, high = messages[0][i], messages[1][i]
+        sides[0][8 * i : 8 * i + 8] = jnp.where(even, high, low)
+        sides[1][8 * i : 8 * i + 8] = jnp.where(even, low, high)
     for k in range(2):
-        for start, target in zip(side_starts, sides):
-            target[2 + k] = coef[k, :, pl.ds(start, EDGE)]
         for start, target in zip(row_starts, rows):
             target[2 + k] = coef[k, pl.ds(start, HALO), :]
-    for copy in copies[5:]:
+    for copy in copies[7:]:
         copy.wait()
 
 
-def side_columns(get_even, get_odd):
+def corner_kernel(got_odd, got_even, sides, send_even, send_odd):
     gx = lax.axis_index("gx")
     even = gx % 2 == 0
-    a, b = get_even, get_odd
-    left = jnp.where(gx == 0, 0.0, jnp.where(even, b, a))
-    right = jnp.where(gx == lax.axis_size("gx") - 1, 0.0, jnp.where(even, a, b))
-    return left, right
-
-
-def corner_kernel(got_odd, got_even, send_even, send_odd):
+    for side in range(2):
+        end = gx == (0 if side == 0 else lax.axis_size("gx") - 1)
+
+        def tile(i):
+            rows = slice(8 * i, 8 * i + 8)
+            a, b = got_even[rows], got_odd[rows]
+            return jnp.where(end, 0.0, jnp.where(even, b, a) if side == 0 else jnp.where(even, a, b))
+
+        parts = unpack_side([tile(i) for i in range(9)], 1 - side)
+        for i, part in enumerate(parts):
+            sides[side, i // 4, 8 * (i % 4) : 8 * (i % 4) + 8] = part
     for start, target in zip(halves_of("gy", ROWS, HALO), (send_even, send_odd)):
-        rows = pl.ds(start, HALO)
         for row in range(4):
-            left, right = side_columns(got_even[row, rows], got_odd[row, rows])
-            target[row, :, 0:EDGE] = left
-            target[row, :, EDGE : 2 * EDGE] = right
+            for side in range(2):
+                target[row, :, side * EDGE : (side + 1) * EDGE] = sides[side, row, pl.ds(start, HALO)]
 
 
 def own_rows(a, b):
@@ -363,8 +407,7 @@
 def rim_kernel(
     forcing,
     coef,
-    got_odd,
-    got_even,
+    sides,
     rows_even,
     rows_odd,
     corner_odd,
@@ -375,17 +418,16 @@
     *refs,
 ):
     levels = levels_of(refs)
-    near, far, natural = refs[24:27]
-    etas, betas, diags, others = (refs[27 + 3 * i : 30 + 3 * i] for i in range(4))
+    near_even, near_odd, far, natural = refs[24:28]
+    etas, betas, diags, others = (refs[28 + 3 * i : 31 + 3 * i] for i in range(4))
     for row in range(4):
         source = forcing if row < 2 else coef
         target = plane_targets(row, levels, etas, betas)
-        sides = side_columns(got_even[row], got_odd[row])
         for i in range(4):
             if i in (0, 3):
                 part = slice(0, EDGE) if i == 0 else slice(EDGE, 2 * EDGE)
                 halo = (corner_even[row, :, part], corner_odd[row, :, part])
-                own = sides[i // 3]
+                own = sides[i // 3, row]
             else:
                 part = slice(0, EDGE) if i == 1 else slice(COLS - EDGE, COLS)
                 halo = (rows_even[row, :, part], rows_odd[row, :, part])
@@ -396,12 +438,26 @@
     head = jnp.concatenate([own_rows(both[0], both[1]), own_rows(both[2], both[3])], axis=1)
     far[...] = head
     at = head.shape[1]
-    near[:, 0:at] = head
-    for source, rims, shift in ((late_field, levels[2].field, 1), (late_force, levels[2].force, 0)):
-        for p in range(2):
-            parts = [merge(2, source[k, p + shift], rims[k, p + shift]) for k in range(2)]
-            near[:, at : at + MERGED[2]] = own_rows(parts[0], parts[1])
-            at += MERGED[2]
+    w, f = (
+        [[merge(2, source[k, p + i], rims[k, p + i]) for p in range(2)] for k in range(2)]
+        for i, source, rims in ((1, late_field, levels[2].field), (0, late_force, levels[2].force))
+    )
+    messages = []
+    for picks in (
+        lambda k: [(w[k][0], 4), (w[k][0], 5), (w[k][1], 4), (f[k][1], 4)],
+        lambda k: [(w[k][0], 3), (w[k][1], 2), (w[k][1], 3), (f[k][0], 3)],
+    ):
+        rows = picks(0) + picks(1)
+        message = pltpu.roll(rows[0][0], 8 - rows[0][1], axis=0)
+        sub = lax.broadcasted_iota(jnp.int32, message.shape, 0)
+        for i, (x, g) in enumerate(rows):
+            if i:
+                message = jnp.where(sub == i, pltpu.roll(x, (i - g) % 8, axis=0) if i != g else x, message)
+        messages.append(message)
+    even = lax.axis_index("gy") % 2 == 0
+    for target, flag in ((near_even, even), (near_odd, jnp.logical_not(even))):
+        target[:, 0:at] = head
+        target[:, at:] = jnp.where(flag, messages[0], messages[1])
 
 
 def merge_kernel(*refs):
@@ -592,17 +648,20 @@
     for k in range(2):
         a, b = pltpu.roll(field[k][0:8], 2, axis=0), pltpu.roll(field[k][8:16], 2, axis=0)
         coarsest.append(jnp.where(sublanes(a) < 2, a, b))
-    at = 2 * MERGED[3]
-    for target, own, shift in ((late_field, levels[2].field, 1), (late_force, levels[2].force, 0)):
-        for p in range(2):
-            part = slice(at, at + MERGED[2])
-            up, down = above(part), below(part)
-            for k in range(2):
-                turn = 2 if k else 6
-                a, b = pltpu.roll(up, turn, axis=0), pltpu.roll(down, turn, axis=0)
-                sub = sublanes(a)
-                target[k, p + shift] = jnp.where(sub < 2, a, jnp.where(sub < 6, own[k, p + shift], b))
-            at += MERGED[2]
+    part = slice(2 * MERGED[3], 2 * MERGED[3] + MERGED[2])
+    up, down = above(part), below(part)
+    sub = sublanes(up)
+    own_field, own_force = levels[2].field, levels[2].force
+    for k in range(2):
+
+        def turned(x, by):
+            by = (by - 4 * k) % 8
+            return pltpu.roll(x, by, axis=0) if by else x
+
+        late_field[k, 1] = jnp.where(sub < 2, turned(up, 0), jnp.where(sub < 7, own_field[k, 1], turned(down, 7)))
+        late_field[k, 2] = jnp.where(sub < 1, turned(up, 6), jnp.where(sub < 6, own_field[k, 2], turned(down, 5)))
+        late_force[k, 0] = jnp.where(sub < 7, own_force[k, 0], turned(down, 4))
+        late_force[k, 1] = jnp.where(sub < 1, turned(up, 5), own_force[k, 1])
     levels[2].force = late_force
     levels[2].field = late_field
     coarse = lambda k, p: coarsest[k]
@@ -645,25 +704,25 @@
     table = pltpu.SMEM((16,), jnp.float32)
     coef, side_even, side_odd, main_even, main_odd = pl.pallas_call(
         lookup_kernel,
-        out_shape=(shape(2, ROWS, COLS),) + (shape(4, ROWS, EDGE),) * 2 + (shape(4, HALO, COLS),) * 2,
+        out_shape=(shape(2, ROWS, COLS),) + (shape(72, 128),) * 2 + (shape(4, HALO, COLS),) * 2,
         in_specs=hbm,
         out_specs=tuple(vmem(5)),
-        scratch_shapes=[[table, table], pltpu.VMEM((3, ROWS, COLS), jnp.int32), pltpu.SemaphoreType.DMA((9,))],
+        scratch_shapes=[[table, table], pltpu.VMEM((3, ROWS, COLS), jnp.int32)]
+        + [pltpu.VMEM((2, 2, ROWS, EDGE), jnp.float32), pltpu.SemaphoreType.DMA((9,))],
         compiler_params=params(),
         name="lookup",
     )(*inputs)
     got_odd = swap(side_odd, "gx", 1)
     got_even = swap(side_even, "gx", 0)
     rows_odd = swap(main_odd, "gy", 1)
-    send_even, send_odd = pl.pallas_call(
+    sides, send_even, send_odd = pl.pallas_call(
         corner_kernel,
-        out_shape=(shape(4, HALO, 2 * EDGE),) * 2,
+        out_shape=(shape(2, 4, ROWS, EDGE),) + (shape(4, HALO, 2 * EDGE),) * 2,
         in_specs=vmem(2),
-        out_specs=tuple(vmem(2)),
+        out_specs=tuple(vmem(3)),
         compiler_params=params(),
         name="corners",
     )(got_odd, got_even)
-    main_even, send_even = lax.optimization_barrier((main_even, send_even))
     corner_odd = swap(send_odd, "gy", 1)
     corner_even = swap(send_even, "gy", 0)
     rows_even = swap(main_even, "gy", 0)
@@ -689,18 +748,18 @@
         compiler_params=params(),
         name="main",
     )(forcing, coef, rows_even, rows_odd)
-    near_lanes = 2 * MERGED[3] + 4 * MERGED[2]
-    *rim, near, far = pl.pallas_call(
+    near_lanes = 2 * MERGED[3] + MERGED[2]
+    *rim, send_even, send_odd, far = pl.pallas_call(
         rim_kernel,
-        out_shape=tuple(shape(*dims) for dims in kept(RIM) + [(8, near_lanes), (8, 2 * MERGED[3])]),
-        in_specs=vmem(11),
-        out_specs=tuple(vmem(26)),
+        out_shape=tuple(shape(*dims) for dims in kept(RIM) + [(8, near_lanes)] * 2 + [(8, 2 * MERGED[3])]),
+        in_specs=vmem(10),
+        out_specs=tuple(vmem(27)),
         scratch_shapes=work(RIM),
         compiler_params=params(),
         name="rim",
-    )(forcing, coef, got_odd, got_even, rows_even, rows_odd, corner_odd, corner_even, top, main[22], main[23])
-    near_even = swap(near, "gy", 0)
-    near_odd = swap(near, "gy", 1)
+    )(forcing, coef, sides, rows_even, rows_odd, corner_odd, corner_even, top, main[22], main[23])
+    near_even = swap(send_even, "gy", 0)
+    near_odd = swap(send_odd, "gy", 1)
     far_even = swap_far(far, 0)
     far_odd = swap_far(far, 1)
     wide = MERGED[0]

time: 25.6 us -> 24.9 us (0.973)
  the two profiles are of different devices: /device:TPU:162 before, /device:TPU:2 now
where the time goes in v9:
time: 24.9 us
  starting transfers between devices  9.77 us (39%)
  Pallas kernels  9.2 us (37%)
  waiting for transfers between devices  5.82 us (23%)
    ppermute x8, starting transfers between devices, swap(): lax.ppermute(x, ('gx', 'gy'), [(place(*a), place(*b)) for a, b in pairs])  8.98 us
    ppermute x2, waiting for transfers between devices, swap_far(): return lax.ppermute(x, 'gy', pairs)  3.26 us
    pallas_call x1, Pallas kernels, local(): pl.pallas_call(up_kernel, out_shape=shape(2, ROWS, COLS), in_specs=vmem(3...  2.97 us
    pallas_call x1, Pallas kernels, local(): pl.pallas_call(main_kernel, out_shape=tuple((shape(*dims) for dims in kep...  2.58 us
    ppermute x8, waiting for transfers between devices, swap(): lax.ppermute(x, ('gx', 'gy'), [(place(*a), place(*b)) for a, b in pairs])  2.56 us
    pallas_call x1, Pallas kernels, local(): pl.pallas_call(lookup_kernel, out_shape=(shape(2, ROWS, COLS),) + (shape(...  1.55 us
    pallas_call x1, Pallas kernels, local(): pl.pallas_call(rim_kernel, out_shape=tuple((shape(*dims) for dims in kept...  1.49 us
    ppermute x2, starting transfers between devices, swap_far(): return lax.ppermute(x, 'gy', pairs)  0.79 us
  transfers between devices with their start and end apart: 10, of which 3 were waited for; matrix products, arithmetic and copies ran while one was open for 0% of the time, Pallas kernels for 13%

profile of v9, /device:TPU:2, one launch (start us, length us, event | category | flops | bytes accessed | tf_op | source)
XLA Modules:
  0.0 24.9 jit_solution(5522885569207517212)
XLA Ops:
  0.0 1.5 %lookup.1 = (f32[2,32,1024]{2,1,0:T(8,128)S(1)}, f32[72,128]{1,0:T(8,128)S(1)}, f32[72,128]{1,0:T(8,128)S(1)}, f32[4,16,1024]{2,1,0:T(8,128)S(1)}, f32[4,16,1024]{2,1,0:T(8,128)S(1)}) custom-call(f32[16]{0:T(128)} %v_table.1, f32[16]{0:T(128)} %d_table.1, f32[2,32,1024]{2,1,0:T(8,128)} %forcing.5, s32[32,1024]{1,0:T(8,128)} %mask.1, s32[32,1024]{1,0:T(8,128)} %v_class.1, ...), custom_call_target="tpu_custom_call" | custom-call | tf_op jit(solution)/shard_map/lookup/pallas_call | solution.py:705
  1.6 0.1 collective-permute-start.2
  1.7 2.4 %collective-permute-start.3 = (f32[4,16,1024]{2,1,0:T(8,128)S(1)}, f32[4,16,1024]{2,1,0:T(8,128)S(1)}, u32[]{:S(2)}, u32[]{:S(2)}) collective-permute-start(f32[4,16,1024]{2,1,0:T(8,128)S(1)} %get-tuple-element.98), channel_id=1, source_target_pairs={{1,2},{2,1},{3,4},{4,3},{5,6},{6,5},{0,8},{7,15},{9,10},{10,9},{11... | collective-permute-start | bytes 786440 | tf_op jit(solution)/shard_map/ppermute | solution.py:684
  4.0 0.0 collective-permute-start
  4.0 1.4 %collective-permute-start.1 = (f32[72,128]{1,0:T(8,128)S(1)}, f32[72,128]{1,0:T(8,128)S(1)}, u32[]{:S(2)}, u32[]{:S(2)}) collective-permute-start(f32[72,128]{1,0:T(8,128)S(1)} %get-tuple-element.95), channel_id=1, source_target_pairs={{0,8},{8,0},{16,24},{24,16},{32,40},{40,32},{48,56},{56,48},{64,72... | collective-permute-start | bytes 110600 | tf_op jit(solution)/shard_map/ppermute | solution.py:684
  5.4 0.0 collective-permute-done.got_odd
  5.5 2.5 %collective-permute-done.1.got_even = f32[72,128]{1,0:T(8,128)S(1)} collective-permute-done((f32[72,128]{1,0:T(8,128)S(1)}, f32[72,128]{1,0:T(8,128)S(1)}, u32[]{:S(2)}, u32[]{:S(2)}) %collective-permute-start.1) | collective-permute-done | bytes 36896 | tf_op jit(solution)/shard_map/ppermute | solution.py:684
  8.0 0.1 corners.1
  8.1 0.2 collective-permute-start.4
  8.3 1.1 %collective-permute-start.5 = (f32[4,16,256]{2,1,0:T(8,128)S(1)}, f32[4,16,256]{2,1,0:T(8,128)S(1)}, u32[]{:S(2)}, u32[]{:S(2)}) collective-permute-start(f32[4,16,256]{2,1,0:T(8,128)S(1)} %get-tuple-element.100), channel_id=1, source_target_pairs={{0,1},{1,0},{2,3},{3,2},{4,5},{5,4},{6,7},{7,6},{8,9},{9,8},{10,11... | collective-permute-start | bytes 196616 | tf_op jit(solution)/shard_map/ppermute | solution.py:684
  9.4 0.0 collective-permute-done.2.rows_even
  9.4 0.0 collective-permute-done.3.rows_odd
  9.4 2.6 %main.1 = (f32[8,8,1024]{2,1,0:T(8,128)S(1)}, f32[8,8,1024]{2,1,0:T(8,128)S(1)}, f32[8,8,1024]{2,1,0:T(8,128)S(1)}, f32[8,8,1024]{2,1,0:T(8,128)S(1)}, f32[9,8,1...) custom-call(f32[2,32,1024]{2,1,0:T(8,128)S(1)} %copy-done, ...), custom_call_target="tpu_custom_call" | custom-call | tf_op jit(solution)/shard_map/main/pallas_call | solution.py:742
  12.0 0.0 collective-permute-done.4.corner_odd
  12.0 0.0 collective-permute-done.5.corner_even
  12.0 1.5 %rim.1 = (f32[8,8,512]{2,1,0:T(8,128)S(1)}, f32[8,8,512]{2,1,0:T(8,128)S(1)}, f32[8,8,512]{2,1,0:T(8,128)S(1)}, f32[8,8,512]{2,1,0:T(8,128)S(1)}, f32[9,8,512]{2...) custom-call(f32[2,32,1024]{2,1,0:T(8,128)S(1)} %copy-done, ...), custom_call_target="tpu_custom_call" | custom-call | tf_op jit(solution)/shard_map/rim/pallas_call | solution.py:752
  13.5 0.1 collective-permute-start.6
  13.6 3.7 %collective-permute-start.7 = (f32[8,896]{1,0:T(8,128)S(1)}, f32[8,896]{1,0:T(8,128)S(1)}, u32[]{:S(2)}, u32[]{:S(2)}) collective-permute-start(f32[8,896]{1,0:T(8,128)S(1)} %get-tuple-element.106), channel_id=1, source_target_pairs={{1,2},{2,1},{3,4},{4,3},{5,6},{6,5},{0,8},{7,15},{9,10},{10,9},{11... | collective-permute-start | bytes 86024 | tf_op jit(solution)/shard_map/ppermute | solution.py:684
  17.4 0.8 %collective-permute-start.8 = (f32[8,512]{1,0:T(8,128)S(1)}, f32[8,512]{1,0:T(8,128)S(1)}, u32[]{:S(2)}, u32[]{:S(2)}) collective-permute-start(f32[8,512]{1,0:T(8,128)S(1)} %get-tuple-element.104.far), channel_id=1, source_target_pairs={{0,2},{2,0},{1,3},{3,1},{4,6},{6,4},{5,7},{7,5},{8,10},{10,8},{9,1... | collective-permute-start | bytes 49160 | tf_op jit(solution)/shard_map/ppermute | solution.py:695
  18.1 0.0 collective-permute-start.9
  18.1 0.5 %merge.1 = (f32[8,8,1152]{2,1,0:T(8,128)S(1)}, f32[8,8,1152]{2,1,0:T(8,128)S(1)}, f32[8,8,1152]{2,1,0:T(8,128)S(1)}, f32[8,8,1152]{2,1,0:T(8,128)S(1)}, f32[8,8,...) custom-call(f32[8,8,1024]{2,1,0:T(8,128)S(1)} %get-tuple-element.107, ...), custom_call_target="tpu_custom_call" | custom-call | tf_op jit(solution)/shard_map/merge/pallas_call | solution.py:768
  18.6 2.5 %collective-permute-done.8.far_even = f32[8,512]{1,0:T(8,128)S(1)} collective-permute-done((f32[8,512]{1,0:T(8,128)S(1)}, f32[8,512]{1,0:T(8,128)S(1)}, u32[]{:S(2)}, u32[]{:S(2)}) %collective-permute-start.8) | collective-permute-done | bytes 16416 | tf_op jit(solution)/shard_map/ppermute | solution.py:695
  21.1 0.8 %collective-permute-done.9.far_odd = f32[8,512]{1,0:T(8,128)S(1)} collective-permute-done((f32[8,512]{1,0:T(8,128)S(1)}, f32[8,512]{1,0:T(8,128)S(1)}, u32[]{:S(2)}, u32[]{:S(2)}) %collective-permute-start.9) | collective-permute-done | bytes 16416 | tf_op jit(solution)/shard_map/ppermute | solution.py:695
  21.9 3.0 %up.1 = f32[2,32,1024]{2,1,0:T(8,128)} custom-call(f32[8,512]{1,0:T(8,128)S(1)} %get-tuple-element.104.far, f32[8,896]{1,0:T(8,128)S(1)} %collective-permute-done.6.near_even, f32[8,896]{1,0:T(8,128)S(1)} %collective-permute-done.7.near_odd, f32[8,512]{1,0:T(8,128)S(1)} %collective-permute-done.8.far_even, f32[8,512]{1,0:T(8,128)S(1)} %collective-permute-done.9.far_odd, ...), custom_call_target="tpu_custom_call" | custom-call | tf_op jit(solution)/shard_map/up/pallas_call | solution.py:777
  (4 shorter events, 0.0 us)
Async XLA Ops:
  0.0 9.4 %copy-start = (f32[2,32,1024]{2,1,0:T(8,128)S(1)}, f32[2,32,1024]{2,1,0:T(8,128)}, u32[]{:S(2)}) copy-start(f32[2,32,1024]{2,1,0:T(8,128)} %forcing.5) | copy-start | bytes 786436
  1.6 7.9 %collective-permute-start.2 = (f32[4,16,1024]{2,1,0:T(8,128)S(1)}, f32[4,16,1024]{2,1,0:T(8,128)S(1)}, u32[]{:S(2)}, u32[]{:S(2)}) collective-permute-start(f32[4,16,1024]{2,1,0:T(8,128)S(1)} %get-tuple-element.97), channel_id=1, source_target_pairs={{0,1},{1,0},{2,3},{3,2},{4,5},{5,4},{6,7},{7,6},{8,9},{9,8},{10,11... | collective-permute-start | bytes 786440 | tf_op jit(solution)/shard_map/ppermute | solution.py:684
  1.7 7.8 %collective-permute-start.3 = (f32[4,16,1024]{2,1,0:T(8,128)S(1)}, f32[4,16,1024]{2,1,0:T(8,128)S(1)}, u32[]{:S(2)}, u32[]{:S(2)}) collective-permute-start(f32[4,16,1024]{2,1,0:T(8,128)S(1)} %get-tuple-element.98), channel_id=1, source_target_pairs={{1,2},{2,1},{3,4},{4,3},{5,6},{6,5},{0,8},{7,15},{9,10},{10,9},{11... | collective-permute-start | bytes 786440 | tf_op jit(solution)/shard_map/ppermute | solution.py:684
  4.0 1.4 %collective-permute-start = (f32[72,128]{1,0:T(8,128)S(1)}, f32[72,128]{1,0:T(8,128)S(1)}, u32[]{:S(2)}, u32[]{:S(2)}) collective-permute-start(f32[72,128]{1,0:T(8,128)S(1)} %get-tuple-element.94), channel_id=1, source_target_pairs={{8,16},{16,8},{24,32},{32,24},{40,48},{48,40},{56,64},{64,56},{72,... | collective-permute-start | bytes 110600 | tf_op jit(solution)/shard_map/ppermute | solution.py:684
  4.0 4.0 %collective-permute-start.1 = (f32[72,128]{1,0:T(8,128)S(1)}, f32[72,128]{1,0:T(8,128)S(1)}, u32[]{:S(2)}, u32[]{:S(2)}) collective-permute-start(f32[72,128]{1,0:T(8,128)S(1)} %get-tuple-element.95), channel_id=1, source_target_pairs={{0,8},{8,0},{16,24},{24,16},{32,40},{40,32},{48,56},{56,48},{64,72... | collective-permute-start | bytes 110600 | tf_op jit(solution)/shard_map/ppermute | solution.py:684
  8.1 3.9 %collective-permute-start.4 = (f32[4,16,256]{2,1,0:T(8,128)S(1)}, f32[4,16,256]{2,1,0:T(8,128)S(1)}, u32[]{:S(2)}, u32[]{:S(2)}) collective-permute-start(f32[4,16,256]{2,1,0:T(8,128)S(1)} %get-tuple-element.99), channel_id=1, source_target_pairs={{1,2},{2,1},{3,4},{4,3},{5,6},{6,5},{0,8},{7,15},{9,10},{10,9},{11... | collective-permute-start | bytes 196616 | tf_op jit(solution)/shard_map/ppermute | solution.py:684
  8.3 3.7 %collective-permute-start.5 = (f32[4,16,256]{2,1,0:T(8,128)S(1)}, f32[4,16,256]{2,1,0:T(8,128)S(1)}, u32[]{:S(2)}, u32[]{:S(2)}) collective-permute-start(f32[4,16,256]{2,1,0:T(8,128)S(1)} %get-tuple-element.100), channel_id=1, source_target_pairs={{0,1},{1,0},{2,3},{3,2},{4,5},{5,4},{6,7},{7,6},{8,9},{9,8},{10,11... | collective-permute-start | bytes 196616 | tf_op jit(solution)/shard_map/ppermute | solution.py:684
  13.5 8.4 %collective-permute-start.6 = (f32[8,896]{1,0:T(8,128)S(1)}, f32[8,896]{1,0:T(8,128)S(1)}, u32[]{:S(2)}, u32[]{:S(2)}) collective-permute-start(f32[8,896]{1,0:T(8,128)S(1)} %get-tuple-element.105), channel_id=1, source_target_pairs={{0,1},{1,0},{2,3},{3,2},{4,5},{5,4},{6,7},{7,6},{8,9},{9,8},{10,11... | collective-permute-start | bytes 86024 | tf_op jit(solution)/shard_map/ppermute | solution.py:684
  13.6 8.3 %collective-permute-start.7 = (f32[8,896]{1,0:T(8,128)S(1)}, f32[8,896]{1,0:T(8,128)S(1)}, u32[]{:S(2)}, u32[]{:S(2)}) collective-permute-start(f32[8,896]{1,0:T(8,128)S(1)} %get-tuple-element.106), channel_id=1, source_target_pairs={{1,2},{2,1},{3,4},{4,3},{5,6},{6,5},{0,8},{7,15},{9,10},{10,9},{11... | collective-permute-start | bytes 86024 | tf_op jit(solution)/shard_map/ppermute | solution.py:684
  17.4 3.7 %collective-permute-start.8 = (f32[8,512]{1,0:T(8,128)S(1)}, f32[8,512]{1,0:T(8,128)S(1)}, u32[]{:S(2)}, u32[]{:S(2)}) collective-permute-start(f32[8,512]{1,0:T(8,128)S(1)} %get-tuple-element.104.far), channel_id=1, source_target_pairs={{0,2},{2,0},{1,3},{3,1},{4,6},{6,4},{5,7},{7,5},{8,10},{10,8},{9,1... | collective-permute-start | bytes 49160 | tf_op jit(solution)/shard_map/ppermute | solution.py:695
  18.1 3.7 %collective-permute-start.9 = (f32[8,512]{1,0:T(8,128)S(1)}, f32[8,512]{1,0:T(8,128)S(1)}, u32[]{:S(2)}, u32[]{:S(2)}) collective-permute-start(f32[8,512]{1,0:T(8,128)S(1)} %get-tuple-element.104.far), channel_id=1, source_target_pairs={{2,4},{4,2},{3,5},{5,3},{0,1},{1,0},{6,7},{7,6},{10,12},{12,10},{1... | collective-permute-start | bytes 49160 | tf_op jit(solution)/shard_map/ppermute | solution.py:695

commit v10 on v9

--- a/solution.py
+++ b/solution.py
@@ -509,8 +509,9 @@
     wide = MERGED[0]
     edges = [[None] * 8, [None] * 8]
     for p in range(0, 8, 2):
-        adds = [double_lanes(coarse(k, p // 2), wide) for k in range(2)]
-        both = own_rows(adds[0], adds[1])
+        below_this = [coarse(k, p // 2) for k in range(2)]
+        both = double_lanes(own_rows(below_this[0], below_this[1]), wide)
+        adds = [double_lanes(x, wide) if p in (0, 6) else None for x in below_this]
         for q in (p, p + 1):
             packed[q] = field[q] + both
             if q in (0, 1, 6, 7):
@@ -569,7 +570,7 @@
         next_packed[p + 1] = KEEP * here + scale[p] * terms
     copies = []
     first = 0
-    for count in (4, 2, 2):
+    for count in (4, 3, 1):
 
         def part(x):
             end = x[:, 128 * max(first - 1, 0) : 128 * (first + count + 1)]
@@ -614,40 +615,61 @@
         m2 = jnp.where(gy < 2, 0.0, jnp.where(low, far_odd[:, part], far_even[:, part]))
         p2 = jnp.where(gy > count - 3, 0.0, jnp.where(low, far_even[:, part], far_odd[:, part]))
         m1, p1, own = above(part), below(part), far[:, part]
-        upper = sublanes(own) < 4
-
-        def halves(x, y, second):
-            if second:
-                return jnp.where(upper, pltpu.roll(x, 4, axis=0), y)
-            return jnp.where(upper, x, pltpu.roll(y, 4, axis=0))
-
-        zero = jnp.zeros_like(own)
-        return [
-            jnp.concatenate([halves(m2, m1, s), halves(own, p1, s), halves(p2, zero, s)], axis=0)
-            for s in (False, True)
-        ]
+        sub = sublanes(own)
+        out = []
+        for outer, inner in ((6, 2), (2, 6)):
+
+            def tile(x, y, z):
+                x, z = pltpu.roll(x, outer, axis=0), pltpu.roll(z, outer, axis=0)
+                return jnp.where(sub < 2, x, jnp.where(sub < 6, pltpu.roll(y, inner, axis=0), z))
+
+            if outer == 6:
+                ends = jnp.where(sub < 4, m2, pltpu.roll(p2, 4, axis=0))
+            else:
+                ends = jnp.where(sub < 4, pltpu.roll(m2, 4, axis=0), p2)
+            out.append((jnp.concatenate([tile(m2, m1, own), tile(own, p1, p2)], axis=0), ends))
+        return out
 
     force = stacked(slice(0, MERGED[3]))
-    eta, beta = stacked(slice(MERGED[3], 2 * MERGED[3]))
-    right, left, under, over, cross_right, cross_left, diag = coefficients(eta, beta, from_below(eta), from_above)
+    (eta, eta_ends), (beta, beta_ends) = stacked(slice(MERGED[3], 2 * MERGED[3]))
+    row = sublanes(eta)
+
+    def shifted_down(x, ends):
+        first = pltpu.roll(ends, 7, axis=0)
+        return jnp.where(row == 0, jnp.concatenate([first, first], axis=0), from_above(x))
+
+    def shifted_up(x, ends):
+        last = pltpu.roll(ends, 1, axis=0)
+        return jnp.where(row == 15, jnp.concatenate([last, last], axis=0), from_below(x))
+
+    ends = coefficients(eta_ends, beta_ends, from_below(eta_ends), from_above)
+    right, left, under, over, cross_right, cross_left, diag = coefficients(
+        eta, beta, shifted_up(eta, eta_ends), lambda x: shifted_down(x, ends[2])
+    )
     scale = OMEGA / diag
-    field = [scale * force[0], scale * force[1]]
-    for _ in range(5):
-        downs = [from_below(x) for x in field]
-        ups = [from_above(x) for x in field]
+    scale_ends = OMEGA / ends[6]
+    field = [scale * force[k][0] for k in range(2)]
+    for step in range(5):
+        if step == 0:
+            field_ends = [scale_ends * force[k][1] for k in range(2)]
+            downs = [shifted_up(field[k], field_ends[k]) for k in range(2)]
+            ups = [shifted_down(field[k], field_ends[k]) for k in range(2)]
+        else:
+            downs = [from_below(x) for x in field]
+            ups = [from_above(x) for x in field]
         steps = [downs[k] - ups[k] for k in range(2)]
         field = [
             KEEP * field[k]
             + scale
             * gather_terms(
-                right, left, cross_right, cross_left, under, over, field[k], downs[k], ups[k], steps[1 - k], force[k]
+                right, left, cross_right, cross_left, under, over, field[k], downs[k], ups[k], steps[1 - k], force[k][0]
             )
             for k in range(2)
         ]
     coarsest = []
     for k in range(2):
-        a, b = pltpu.roll(field[k][0:8], 2, axis=0), pltpu.roll(field[k][8:16], 2, axis=0)
-        coarsest.append(jnp.where(sublanes(a) < 2, a, b))
+        a, b = pltpu.roll(field[k][0:8], 4, axis=0), pltpu.roll(field[k][8:16], 4, axis=0)
+        coarsest.append(jnp.where(sublanes(a) < 4, a, b))
     part = slice(2 * MERGED[3], 2 * MERGED[3] + MERGED[2])
     up, down = above(part), below(part)
     sub = sublanes(up)

time: 24.9 us -> 24.9 us (level)
  no operation moved by 1% of the time
where the time goes in v10:
time: 24.9 us; the launch traced here: 24.8 us
  starting transfers between devices  9.77 us (39%)
  Pallas kernels  9.14 us (37%)
  waiting for transfers between devices  5.82 us (23%)
    ppermute x8, starting transfers between devices, swap(): lax.ppermute(x, ('gx', 'gy'), [(place(*a), place(*b)) for a, b in pairs])  8.98 us
    ppermute x2, waiting for transfers between devices, swap_far(): return lax.ppermute(x, 'gy', pairs)  3.26 us
    pallas_call x1, Pallas kernels, local(): pl.pallas_call(up_kernel, out_shape=shape(2, ROWS, COLS), in_specs=vmem(3...  2.92 us
    pallas_call x1, Pallas kernels, local(): pl.pallas_call(main_kernel, out_shape=tuple((shape(*dims) for dims in kep...  2.58 us
    ppermute x8, waiting for transfers between devices, swap(): lax.ppermute(x, ('gx', 'gy'), [(place(*a), place(*b)) for a, b in pairs])  2.56 us
    pallas_call x1, Pallas kernels, local(): pl.pallas_call(lookup_kernel, out_shape=(shape(2, ROWS, COLS),) + (shape(...  1.55 us
    pallas_call x1, Pallas kernels, local(): pl.pallas_call(rim_kernel, out_shape=tuple((shape(*dims) for dims in kept...  1.49 us
    ppermute x2, starting transfers between devices, swap_far(): return lax.ppermute(x, 'gy', pairs)  0.79 us
  transfers between devices with their start and end apart: 10, of which 3 were waited for; matrix products, arithmetic and copies ran while one was open for 0% of the time, Pallas kernels for 13%

profile of v10, /device:TPU:2, one launch (start us, length us, event | category | flops | bytes accessed | tf_op | source)
XLA Modules:
  0.0 24.8 jit_solution(17179210978995617309)
XLA Ops:
  0.0 1.5 %lookup.1 = (f32[2,32,1024]{2,1,0:T(8,128)S(1)}, f32[72,128]{1,0:T(8,128)S(1)}, f32[72,128]{1,0:T(8,128)S(1)}, f32[4,16,1024]{2,1,0:T(8,128)S(1)}, f32[4,16,1024]{2,1,0:T(8,128)S(1)}) custom-call(f32[16]{0:T(128)} %v_table.1, f32[16]{0:T(128)} %d_table.1, f32[2,32,1024]{2,1,0:T(8,128)} %forcing.5, s32[32,1024]{1,0:T(8,128)} %mask.1, s32[32,1024]{1,0:T(8,128)} %v_class.1, ...), custom_call_target="tpu_custom_call" | custom-call | tf_op jit(solution)/shard_map/lookup/pallas_call | solution.py:727
  1.6 0.1 collective-permute-start.2
  1.7 2.4 %collective-permute-start.3 = (f32[4,16,1024]{2,1,0:T(8,128)S(1)}, f32[4,16,1024]{2,1,0:T(8,128)S(1)}, u32[]{:S(2)}, u32[]{:S(2)}) collective-permute-start(f32[4,16,1024]{2,1,0:T(8,128)S(1)} %get-tuple-element.98), channel_id=1, source_target_pairs={{1,2},{2,1},{3,4},{4,3},{5,6},{6,5},{0,8},{7,15},{9,10},{10,9},{11... | collective-permute-start | bytes 786440 | tf_op jit(solution)/shard_map/ppermute | solution.py:706
  4.0 0.0 collective-permute-start
  4.0 1.4 %collective-permute-start.1 = (f32[72,128]{1,0:T(8,128)S(1)}, f32[72,128]{1,0:T(8,128)S(1)}, u32[]{:S(2)}, u32[]{:S(2)}) collective-permute-start(f32[72,128]{1,0:T(8,128)S(1)} %get-tuple-element.95), channel_id=1, source_target_pairs={{0,8},{8,0},{16,24},{24,16},{32,40},{40,32},{48,56},{56,48},{64,72... | collective-permute-start | bytes 110600 | tf_op jit(solution)/shard_map/ppermute | solution.py:706
  5.4 0.0 collective-permute-done.got_odd
  5.5 2.5 %collective-permute-done.1.got_even = f32[72,128]{1,0:T(8,128)S(1)} collective-permute-done((f32[72,128]{1,0:T(8,128)S(1)}, f32[72,128]{1,0:T(8,128)S(1)}, u32[]{:S(2)}, u32[]{:S(2)}) %collective-permute-start.1) | collective-permute-done | bytes 36896 | tf_op jit(solution)/shard_map/ppermute | solution.py:706
  8.0 0.1 corners.1
  8.1 0.2 collective-permute-start.4
  8.3 1.1 %collective-permute-start.5 = (f32[4,16,256]{2,1,0:T(8,128)S(1)}, f32[4,16,256]{2,1,0:T(8,128)S(1)}, u32[]{:S(2)}, u32[]{:S(2)}) collective-permute-start(f32[4,16,256]{2,1,0:T(8,128)S(1)} %get-tuple-element.100), channel_id=1, source_target_pairs={{0,1},{1,0},{2,3},{3,2},{4,5},{5,4},{6,7},{7,6},{8,9},{9,8},{10,11... | collective-permute-start | bytes 196616 | tf_op jit(solution)/shard_map/ppermute | solution.py:706
  9.4 0.0 collective-permute-done.2.rows_even
  9.4 0.0 collective-permute-done.3.rows_odd
  9.4 2.6 %main.1 = (f32[8,8,1024]{2,1,0:T(8,128)S(1)}, f32[8,8,1024]{2,1,0:T(8,128)S(1)}, f32[8,8,1024]{2,1,0:T(8,128)S(1)}, f32[8,8,1024]{2,1,0:T(8,128)S(1)}, f32[9,8,1...) custom-call(f32[2,32,1024]{2,1,0:T(8,128)S(1)} %copy-done, ...), custom_call_target="tpu_custom_call" | custom-call | tf_op jit(solution)/shard_map/main/pallas_call | solution.py:764
  12.0 0.0 collective-permute-done.4.corner_odd
  12.0 0.0 collective-permute-done.5.corner_even
  12.0 1.5 %rim.1 = (f32[8,8,512]{2,1,0:T(8,128)S(1)}, f32[8,8,512]{2,1,0:T(8,128)S(1)}, f32[8,8,512]{2,1,0:T(8,128)S(1)}, f32[8,8,512]{2,1,0:T(8,128)S(1)}, f32[9,8,512]{2...) custom-call(f32[2,32,1024]{2,1,0:T(8,128)S(1)} %copy-done, ...), custom_call_target="tpu_custom_call" | custom-call | tf_op jit(solution)/shard_map/rim/pallas_call | solution.py:774
  13.5 0.1 collective-permute-start.6
  13.6 3.7 %collective-permute-start.7 = (f32[8,896]{1,0:T(8,128)S(1)}, f32[8,896]{1,0:T(8,128)S(1)}, u32[]{:S(2)}, u32[]{:S(2)}) collective-permute-start(f32[8,896]{1,0:T(8,128)S(1)} %get-tuple-element.106), channel_id=1, source_target_pairs={{1,2},{2,1},{3,4},{4,3},{5,6},{6,5},{0,8},{7,15},{9,10},{10,9},{11... | collective-permute-start | bytes 86024 | tf_op jit(solution)/shard_map/ppermute | solution.py:706
  17.4 0.8 %collective-permute-start.8 = (f32[8,512]{1,0:T(8,128)S(1)}, f32[8,512]{1,0:T(8,128)S(1)}, u32[]{:S(2)}, u32[]{:S(2)}) collective-permute-start(f32[8,512]{1,0:T(8,128)S(1)} %get-tuple-element.104.far), channel_id=1, source_target_pairs={{0,2},{2,0},{1,3},{3,1},{4,6},{6,4},{5,7},{7,5},{8,10},{10,8},{9,1... | collective-permute-start | bytes 49160 | tf_op jit(solution)/shard_map/ppermute | solution.py:717
  18.1 0.0 collective-permute-start.9
  18.1 0.5 %merge.1 = (f32[8,8,1152]{2,1,0:T(8,128)S(1)}, f32[8,8,1152]{2,1,0:T(8,128)S(1)}, f32[8,8,1152]{2,1,0:T(8,128)S(1)}, f32[8,8,1152]{2,1,0:T(8,128)S(1)}, f32[8,8,...) custom-call(f32[8,8,1024]{2,1,0:T(8,128)S(1)} %get-tuple-element.107, ...), custom_call_target="tpu_custom_call" | custom-call | tf_op jit(solution)/shard_map/merge/pallas_call | solution.py:790
  18.6 2.5 %collective-permute-done.8.far_even = f32[8,512]{1,0:T(8,128)S(1)} collective-permute-done((f32[8,512]{1,0:T(8,128)S(1)}, f32[8,512]{1,0:T(8,128)S(1)}, u32[]{:S(2)}, u32[]{:S(2)}) %collective-permute-start.8) | collective-permute-done | bytes 16416 | tf_op jit(solution)/shard_map/ppermute | solution.py:717
  21.1 0.8 %collective-permute-done.9.far_odd = f32[8,512]{1,0:T(8,128)S(1)} collective-permute-done((f32[8,512]{1,0:T(8,128)S(1)}, f32[8,512]{1,0:T(8,128)S(1)}, u32[]{:S(2)}, u32[]{:S(2)}) %collective-permute-start.9) | collective-permute-done | bytes 16416 | tf_op jit(solution)/shard_map/ppermute | solution.py:717
  21.9 2.9 %up.1 = f32[2,32,1024]{2,1,0:T(8,128)} custom-call(f32[8,512]{1,0:T(8,128)S(1)} %get-tuple-element.104.far, f32[8,896]{1,0:T(8,128)S(1)} %collective-permute-done.6.near_even, f32[8,896]{1,0:T(8,128)S(1)} %collective-permute-done.7.near_odd, f32[8,512]{1,0:T(8,128)S(1)} %collective-permute-done.8.far_even, f32[8,512]{1,0:T(8,128)S(1)} %collective-permute-done.9.far_odd, ...), custom_call_target="tpu_custom_call" | custom-call | tf_op jit(solution)/shard_map/up/pallas_call | solution.py:799
  (4 shorter events, 0.0 us)
Async XLA Ops:
  0.0 9.4 %copy-start = (f32[2,32,1024]{2,1,0:T(8,128)S(1)}, f32[2,32,1024]{2,1,0:T(8,128)}, u32[]{:S(2)}) copy-start(f32[2,32,1024]{2,1,0:T(8,128)} %forcing.5) | copy-start | bytes 786436
  1.6 7.9 %collective-permute-start.2 = (f32[4,16,1024]{2,1,0:T(8,128)S(1)}, f32[4,16,1024]{2,1,0:T(8,128)S(1)}, u32[]{:S(2)}, u32[]{:S(2)}) collective-permute-start(f32[4,16,1024]{2,1,0:T(8,128)S(1)} %get-tuple-element.97), channel_id=1, source_target_pairs={{0,1},{1,0},{2,3},{3,2},{4,5},{5,4},{6,7},{7,6},{8,9},{9,8},{10,11... | collective-permute-start | bytes 786440 | tf_op jit(solution)/shard_map/ppermute | solution.py:706
  1.7 7.8 %collective-permute-start.3 = (f32[4,16,1024]{2,1,0:T(8,128)S(1)}, f32[4,16,1024]{2,1,0:T(8,128)S(1)}, u32[]{:S(2)}, u32[]{:S(2)}) collective-permute-start(f32[4,16,1024]{2,1,0:T(8,128)S(1)} %get-tuple-element.98), channel_id=1, source_target_pairs={{1,2},{2,1},{3,4},{4,3},{5,6},{6,5},{0,8},{7,15},{9,10},{10,9},{11... | collective-permute-start | bytes 786440 | tf_op jit(solution)/shard_map/ppermute | solution.py:706
  4.0 1.4 %collective-permute-start = (f32[72,128]{1,0:T(8,128)S(1)}, f32[72,128]{1,0:T(8,128)S(1)}, u32[]{:S(2)}, u32[]{:S(2)}) collective-permute-start(f32[72,128]{1,0:T(8,128)S(1)} %get-tuple-element.94), channel_id=1, source_target_pairs={{8,16},{16,8},{24,32},{32,24},{40,48},{48,40},{56,64},{64,56},{72,... | collective-permute-start | bytes 110600 | tf_op jit(solution)/shard_map/ppermute | solution.py:706
  4.0 4.0 %collective-permute-start.1 = (f32[72,128]{1,0:T(8,128)S(1)}, f32[72,128]{1,0:T(8,128)S(1)}, u32[]{:S(2)}, u32[]{:S(2)}) collective-permute-start(f32[72,128]{1,0:T(8,128)S(1)} %get-tuple-element.95), channel_id=1, source_target_pairs={{0,8},{8,0},{16,24},{24,16},{32,40},{40,32},{48,56},{56,48},{64,72... | collective-permute-start | bytes 110600 | tf_op jit(solution)/shard_map/ppermute | solution.py:706
  8.1 3.9 %collective-permute-start.4 = (f32[4,16,256]{2,1,0:T(8,128)S(1)}, f32[4,16,256]{2,1,0:T(8,128)S(1)}, u32[]{:S(2)}, u32[]{:S(2)}) collective-permute-start(f32[4,16,256]{2,1,0:T(8,128)S(1)} %get-tuple-element.99), channel_id=1, source_target_pairs={{1,2},{2,1},{3,4},{4,3},{5,6},{6,5},{0,8},{7,15},{9,10},{10,9},{11... | collective-permute-start | bytes 196616 | tf_op jit(solution)/shard_map/ppermute | solution.py:706
  8.3 3.7 %collective-permute-start.5 = (f32[4,16,256]{2,1,0:T(8,128)S(1)}, f32[4,16,256]{2,1,0:T(8,128)S(1)}, u32[]{:S(2)}, u32[]{:S(2)}) collective-permute-start(f32[4,16,256]{2,1,0:T(8,128)S(1)} %get-tuple-element.100), channel_id=1, source_target_pairs={{0,1},{1,0},{2,3},{3,2},{4,5},{5,4},{6,7},{7,6},{8,9},{9,8},{10,11... | collective-permute-start | bytes 196616 | tf_op jit(solution)/shard_map/ppermute | solution.py:706
  13.5 8.4 %collective-permute-start.6 = (f32[8,896]{1,0:T(8,128)S(1)}, f32[8,896]{1,0:T(8,128)S(1)}, u32[]{:S(2)}, u32[]{:S(2)}) collective-permute-start(f32[8,896]{1,0:T(8,128)S(1)} %get-tuple-element.105), channel_id=1, source_target_pairs={{0,1},{1,0},{2,3},{3,2},{4,5},{5,4},{6,7},{7,6},{8,9},{9,8},{10,11... | collective-permute-start | bytes 86024 | tf_op jit(solution)/shard_map/ppermute | solution.py:706
  13.6 8.3 %collective-permute-start.7 = (f32[8,896]{1,0:T(8,128)S(1)}, f32[8,896]{1,0:T(8,128)S(1)}, u32[]{:S(2)}, u32[]{:S(2)}) collective-permute-start(f32[8,896]{1,0:T(8,128)S(1)} %get-tuple-element.106), channel_id=1, source_target_pairs={{1,2},{2,1},{3,4},{4,3},{5,6},{6,5},{0,8},{7,15},{9,10},{10,9},{11... | collective-permute-start | bytes 86024 | tf_op jit(solution)/shard_map/ppermute | solution.py:706
  17.4 3.7 %collective-permute-start.8 = (f32[8,512]{1,0:T(8,128)S(1)}, f32[8,512]{1,0:T(8,128)S(1)}, u32[]{:S(2)}, u32[]{:S(2)}) collective-permute-start(f32[8,512]{1,0:T(8,128)S(1)} %get-tuple-element.104.far), channel_id=1, source_target_pairs={{0,2},{2,0},{1,3},{3,1},{4,6},{6,4},{5,7},{7,5},{8,10},{10,8},{9,1... | collective-permute-start | bytes 49160 | tf_op jit(solution)/shard_map/ppermute | solution.py:717
  18.1 3.7 %collective-permute-start.9 = (f32[8,512]{1,0:T(8,128)S(1)}, f32[8,512]{1,0:T(8,128)S(1)}, u32[]{:S(2)}, u32[]{:S(2)}) collective-permute-start(f32[8,512]{1,0:T(8,128)S(1)} %get-tuple-element.104.far), channel_id=1, source_target_pairs={{2,4},{4,2},{3,5},{5,3},{0,1},{1,0},{6,7},{7,6},{10,12},{12,10},{1... | collective-permute-start | bytes 49160 | tf_op jit(solution)/shard_map/ppermute | solution.py:717

commit v11 on v10

--- a/solution.py
+++ b/solution.py
@@ -350,7 +350,7 @@
     (above_even, above_odd), (below_even, below_odd) = above, below
     natural[0:HALO] = jnp.where(gy == 0, 0.0, jnp.where(even, above_odd, above_even))
     natural[HALO : HALO + ROWS] = own
-    natural[HALO + ROWS :] = jnp.where(gy == lax.axis_size("gy") - 1, 0.0, jnp.where(even, below_even, below_odd))
+    natural[HALO + ROWS : 2 * HALO + ROWS] = jnp.where(gy == lax.axis_size("gy") - 1, 0.0, jnp.where(even, below_even, below_odd))
     for p in range(8):
         targets(p, cols, natural[pl.ds(p, 8, stride=8), :])
 
@@ -585,7 +585,7 @@
         for i in range(first, first + count):
             for k in range(2):
                 target = velocity.at[k, :, pl.ds(128 * i, 128)]
-                copy = pltpu.make_async_copy(natural.at[k, i], target, sems.at[2 * i + k])
+                copy = pltpu.make_async_copy(natural.at[k, i, pl.ds(0, ROWS)], target, sems.at[2 * i + k])
                 copy.start()
                 copies.append(copy)
         first += count
@@ -593,7 +593,7 @@
         copy.wait()
 
 
-def up_kernel(far, near_even, near_odd, far_even, far_odd, *refs):
+def up_kernel(far, near_odd, far_even, far_odd, near_even, *refs):
     levels = [None] + [Level(PLANES[i], refs[4 + 8 * i : 12 + 8 * i]) for i in (1, 2)]
     velocity, natural, sems, packed, next_packed, late_force, late_field = refs[28:35]
     fields, others = (None,) + refs[35:37], (None,) + refs[37:39]
@@ -759,7 +759,7 @@
         return [(2, PLANES[i] + 2, 8, widths[i]) for i in range(3)]
 
     def work(widths):
-        return scratch([(32, 64, 128)] + [(PLANES[i], 8, widths[i]) for i in range(3)] * 3 + rims(widths))
+        return scratch([(32, 72, 128)] + [(PLANES[i], 8, widths[i]) for i in range(3)] * 3 + rims(widths))
 
     *main, top = pl.pallas_call(
         main_kernel,
@@ -801,12 +801,12 @@
         out_shape=shape(2, ROWS, COLS),
         in_specs=vmem(33),
         out_specs=pl.BlockSpec(memory_space=pltpu.HBM),
-        scratch_shapes=scratch([(2, COLS // 128, ROWS, 128)])
+        scratch_shapes=scratch([(2, COLS // 128, ROWS + 8, 128)])
         + [pltpu.SemaphoreType.DMA((2 * COLS // 128,))]
         + scratch(late + rims(MERGED)[1:] + rims(MERGED)[1:]),
         compiler_params=params(),
         name="up",
-    )(far, near_even, near_odd, far_even, far_odd, *merged)
+    )(far, near_odd, far_even, far_odd, near_even, *merged)
 
 
 def solution(mesh):

time: 24.9 us -> 24.7 us (level)
  the two profiles are of different devices: /device:TPU:2 before, /device:TPU:114 now
where the time goes in v11:
time: 24.7 us; the launch traced here: 24.6 us
  starting transfers between devices  10.7 us (43%)
  Pallas kernels  9.14 us (37%)
  waiting for transfers between devices  4.74 us (19%)
    ppermute x8, starting transfers between devices, swap(): lax.ppermute(x, ('gx', 'gy'), [(place(*a), place(*b)) for a, b in pairs])  8.36 us
    pallas_call x1, Pallas kernels, local(): pl.pallas_call(up_kernel, out_shape=shape(2, ROWS, COLS), in_specs=vmem(3...  2.92 us
    pallas_call x1, Pallas kernels, local(): pl.pallas_call(main_kernel, out_shape=tuple((shape(*dims) for dims in kep...  2.57 us
    ppermute x2, waiting for transfers between devices, swap_far(): return lax.ppermute(x, 'gy', pairs)  2.48 us
    ppermute x2, starting transfers between devices, swap_far(): return lax.ppermute(x, 'gy', pairs)  2.3 us
    ppermute x8, waiting for transfers between devices, swap(): lax.ppermute(x, ('gx', 'gy'), [(place(*a), place(*b)) for a, b in pairs])  2.26 us
    pallas_call x1, Pallas kernels, local(): pl.pallas_call(lookup_kernel, out_shape=(shape(2, ROWS, COLS),) + (shape(...  1.55 us
    pallas_call x1, Pallas kernels, local(): pl.pallas_call(rim_kernel, out_shape=tuple((shape(*dims) for dims in kept...  1.49 us
  transfers between devices with their start and end apart: 10, of which 4 were waited for; matrix products, arithmetic and copies ran while one was open for 0% of the time, Pallas kernels for 13%

profile of v11, /device:TPU:114, one launch (start us, length us, event | category | flops | bytes accessed | tf_op | source)
XLA Modules:
  0.0 24.6 jit_solution(11847859486257358839)
XLA Ops:
  0.0 1.5 %lookup.1 = (f32[2,32,1024]{2,1,0:T(8,128)S(1)}, f32[72,128]{1,0:T(8,128)S(1)}, f32[72,128]{1,0:T(8,128)S(1)}, f32[4,16,1024]{2,1,0:T(8,128)S(1)}, f32[4,16,1024]{2,1,0:T(8,128)S(1)}) custom-call(f32[16]{0:T(128)} %v_table.1, f32[16]{0:T(128)} %d_table.1, f32[2,32,1024]{2,1,0:T(8,128)} %forcing.5, s32[32,1024]{1,0:T(8,128)} %mask.1, s32[32,1024]{1,0:T(8,128)} %v_class.1, ...), custom_call_target="tpu_custom_call" | custom-call | tf_op jit(solution)/shard_map/lookup/pallas_call | solution.py:727
  1.6 0.1 collective-permute-start.2
  1.7 0.6 %collective-permute-start.3 = (f32[4,16,1024]{2,1,0:T(8,128)S(1)}, f32[4,16,1024]{2,1,0:T(8,128)S(1)}, u32[]{:S(2)}, u32[]{:S(2)}) collective-permute-start(f32[4,16,1024]{2,1,0:T(8,128)S(1)} %get-tuple-element.98), channel_id=1, source_target_pairs={{1,2},{2,1},{3,4},{4,3},{5,6},{6,5},{0,8},{7,15},{9,10},{10,9},{11... | collective-permute-start | bytes 786440 | tf_op jit(solution)/shard_map/ppermute | solution.py:706
  2.3 0.4 %collective-permute-start = (f32[72,128]{1,0:T(8,128)S(1)}, f32[72,128]{1,0:T(8,128)S(1)}, u32[]{:S(2)}, u32[]{:S(2)}) collective-permute-start(f32[72,128]{1,0:T(8,128)S(1)} %get-tuple-element.94), channel_id=1, source_target_pairs={{8,16},{16,8},{24,32},{32,24},{40,48},{48,40},{56,64},{64,56},{72,... | collective-permute-start | bytes 110600 | tf_op jit(solution)/shard_map/ppermute | solution.py:706
  2.7 3.6 %collective-permute-start.1 = (f32[72,128]{1,0:T(8,128)S(1)}, f32[72,128]{1,0:T(8,128)S(1)}, u32[]{:S(2)}, u32[]{:S(2)}) collective-permute-start(f32[72,128]{1,0:T(8,128)S(1)} %get-tuple-element.95), channel_id=1, source_target_pairs={{0,8},{8,0},{16,24},{24,16},{32,40},{40,32},{48,56},{56,48},{64,72... | collective-permute-start | bytes 110600 | tf_op jit(solution)/shard_map/ppermute | solution.py:706
  6.4 0.2 collective-permute-done.got_odd
  6.6 2.0 %collective-permute-done.1.got_even = f32[72,128]{1,0:T(8,128)S(1)} collective-permute-done((f32[72,128]{1,0:T(8,128)S(1)}, f32[72,128]{1,0:T(8,128)S(1)}, u32[]{:S(2)}, u32[]{:S(2)}) %collective-permute-start.1) | collective-permute-done | bytes 36896 | tf_op jit(solution)/shard_map/ppermute | solution.py:706
  8.6 0.1 corners.1
  8.8 0.1 collective-permute-start.4
  8.8 1.5 %collective-permute-start.5 = (f32[4,16,256]{2,1,0:T(8,128)S(1)}, f32[4,16,256]{2,1,0:T(8,128)S(1)}, u32[]{:S(2)}, u32[]{:S(2)}) collective-permute-start(f32[4,16,256]{2,1,0:T(8,128)S(1)} %get-tuple-element.100), channel_id=1, source_target_pairs={{0,1},{1,0},{2,3},{3,2},{4,5},{5,4},{6,7},{7,6},{8,9},{9,8},{10,11... | collective-permute-start | bytes 196616 | tf_op jit(solution)/shard_map/ppermute | solution.py:706
  10.3 0.0 collective-permute-done.2.rows_even
  10.3 0.0 collective-permute-done.3.rows_odd
  10.3 2.6 %main.1 = (f32[8,8,1024]{2,1,0:T(8,128)S(1)}, f32[8,8,1024]{2,1,0:T(8,128)S(1)}, f32[8,8,1024]{2,1,0:T(8,128)S(1)}, f32[8,8,1024]{2,1,0:T(8,128)S(1)}, f32[9,8,1...) custom-call(f32[2,32,1024]{2,1,0:T(8,128)S(1)} %copy-done, ...), custom_call_target="tpu_custom_call" | custom-call | tf_op jit(solution)/shard_map/main/pallas_call | solution.py:764
  12.9 0.0 collective-permute-done.4.corner_odd
  12.9 1.5 %rim.1 = (f32[8,8,512]{2,1,0:T(8,128)S(1)}, f32[8,8,512]{2,1,0:T(8,128)S(1)}, f32[8,8,512]{2,1,0:T(8,128)S(1)}, f32[8,8,512]{2,1,0:T(8,128)S(1)}, f32[9,8,512]{2...) custom-call(f32[2,32,1024]{2,1,0:T(8,128)S(1)} %copy-done, ...), custom_call_target="tpu_custom_call" | custom-call | tf_op jit(solution)/shard_map/rim/pallas_call | solution.py:774
  14.4 2.0 %collective-permute-start.6 = (f32[8,896]{1,0:T(8,128)S(1)}, f32[8,896]{1,0:T(8,128)S(1)}, u32[]{:S(2)}, u32[]{:S(2)}) collective-permute-start(f32[8,896]{1,0:T(8,128)S(1)} %get-tuple-element.105), channel_id=1, source_target_pairs={{1,2},{2,1},{3,4},{4,3},{5,6},{6,5},{0,8},{7,15},{9,10},{10,9},{11... | collective-permute-start | bytes 86024 | tf_op jit(solution)/shard_map/ppermute | solution.py:706
  16.4 0.0 collective-permute-start.9
  16.4 1.5 %collective-permute-start.7 = (f32[8,512]{1,0:T(8,128)S(1)}, f32[8,512]{1,0:T(8,128)S(1)}, u32[]{:S(2)}, u32[]{:S(2)}) collective-permute-start(f32[8,512]{1,0:T(8,128)S(1)} %get-tuple-element.104.far), channel_id=1, source_target_pairs={{0,2},{2,0},{1,3},{3,1},{4,6},{6,4},{5,7},{7,5},{8,10},{10,8},{9,1... | collective-permute-start | bytes 49160 | tf_op jit(solution)/shard_map/ppermute | solution.py:717
  18.0 0.8 %collective-permute-start.8 = (f32[8,512]{1,0:T(8,128)S(1)}, f32[8,512]{1,0:T(8,128)S(1)}, u32[]{:S(2)}, u32[]{:S(2)}) collective-permute-start(f32[8,512]{1,0:T(8,128)S(1)} %get-tuple-element.104.far), channel_id=1, source_target_pairs={{2,4},{4,2},{3,5},{5,3},{0,1},{1,0},{6,7},{7,6},{10,12},{12,10},{1... | collective-permute-start | bytes 49160 | tf_op jit(solution)/shard_map/ppermute | solution.py:717
  18.7 0.5 %merge.1 = (f32[8,8,1152]{2,1,0:T(8,128)S(1)}, f32[8,8,1152]{2,1,0:T(8,128)S(1)}, f32[8,8,1152]{2,1,0:T(8,128)S(1)}, f32[8,8,1152]{2,1,0:T(8,128)S(1)}, f32[8,8,...) custom-call(f32[8,8,1024]{2,1,0:T(8,128)S(1)} %get-tuple-element.107, ...), custom_call_target="tpu_custom_call" | custom-call | tf_op jit(solution)/shard_map/merge/pallas_call | solution.py:790
  19.2 1.0 %collective-permute-done.7.far_even = f32[8,512]{1,0:T(8,128)S(1)} collective-permute-done((f32[8,512]{1,0:T(8,128)S(1)}, f32[8,512]{1,0:T(8,128)S(1)}, u32[]{:S(2)}, u32[]{:S(2)}) %collective-permute-start.7) | collective-permute-done | bytes 16416 | tf_op jit(solution)/shard_map/ppermute | solution.py:717
  20.2 1.5 %collective-permute-done.8.far_odd = f32[8,512]{1,0:T(8,128)S(1)} collective-permute-done((f32[8,512]{1,0:T(8,128)S(1)}, f32[8,512]{1,0:T(8,128)S(1)}, u32[]{:S(2)}, u32[]{:S(2)}) %collective-permute-start.8) | collective-permute-done | bytes 16416 | tf_op jit(solution)/shard_map/ppermute | solution.py:717
  21.7 0.0 collective-permute-done.6.near_odd
  21.7 2.9 %up.1 = f32[2,32,1024]{2,1,0:T(8,128)} custom-call(f32[8,512]{1,0:T(8,128)S(1)} %get-tuple-element.104.far, f32[8,896]{1,0:T(8,128)S(1)} %collective-permute-done.6.near_odd, f32[8,512]{1,0:T(8,128)S(1)} %collective-permute-done.7.far_even, f32[8,512]{1,0:T(8,128)S(1)} %collective-permute-done.8.far_odd, f32[8,896]{1,0:T(8,128)S(1)} %collective-permute-done.9.near_even, ...), custom_call_target="tpu_custom_call" | custom-call | tf_op jit(solution)/shard_map/up/pallas_call | solution.py:799
  (4 shorter events, 0.0 us)
Async XLA Ops:
  0.0 10.3 %copy-start = (f32[2,32,1024]{2,1,0:T(8,128)S(1)}, f32[2,32,1024]{2,1,0:T(8,128)}, u32[]{:S(2)}) copy-start(f32[2,32,1024]{2,1,0:T(8,128)} %forcing.5) | copy-start | bytes 786436
  1.6 8.8 %collective-permute-start.2 = (f32[4,16,1024]{2,1,0:T(8,128)S(1)}, f32[4,16,1024]{2,1,0:T(8,128)S(1)}, u32[]{:S(2)}, u32[]{:S(2)}) collective-permute-start(f32[4,16,1024]{2,1,0:T(8,128)S(1)} %get-tuple-element.97), channel_id=1, source_target_pairs={{0,1},{1,0},{2,3},{3,2},{4,5},{5,4},{6,7},{7,6},{8,9},{9,8},{10,11... | collective-permute-start | bytes 786440 | tf_op jit(solution)/shard_map/ppermute | solution.py:706
  1.7 8.7 %collective-permute-start.3 = (f32[4,16,1024]{2,1,0:T(8,128)S(1)}, f32[4,16,1024]{2,1,0:T(8,128)S(1)}, u32[]{:S(2)}, u32[]{:S(2)}) collective-permute-start(f32[4,16,1024]{2,1,0:T(8,128)S(1)} %get-tuple-element.98), channel_id=1, source_target_pairs={{1,2},{2,1},{3,4},{4,3},{5,6},{6,5},{0,8},{7,15},{9,10},{10,9},{11... | collective-permute-start | bytes 786440 | tf_op jit(solution)/shard_map/ppermute | solution.py:706
  2.3 4.3 %collective-permute-start = (f32[72,128]{1,0:T(8,128)S(1)}, f32[72,128]{1,0:T(8,128)S(1)}, u32[]{:S(2)}, u32[]{:S(2)}) collective-permute-start(f32[72,128]{1,0:T(8,128)S(1)} %get-tuple-element.94), channel_id=1, source_target_pairs={{8,16},{16,8},{24,32},{32,24},{40,48},{48,40},{56,64},{64,56},{72,... | collective-permute-start | bytes 110600 | tf_op jit(solution)/shard_map/ppermute | solution.py:706
  2.7 5.9 %collective-permute-start.1 = (f32[72,128]{1,0:T(8,128)S(1)}, f32[72,128]{1,0:T(8,128)S(1)}, u32[]{:S(2)}, u32[]{:S(2)}) collective-permute-start(f32[72,128]{1,0:T(8,128)S(1)} %get-tuple-element.95), channel_id=1, source_target_pairs={{0,8},{8,0},{16,24},{24,16},{32,40},{40,32},{48,56},{56,48},{64,72... | collective-permute-start | bytes 110600 | tf_op jit(solution)/shard_map/ppermute | solution.py:706
  8.8 4.2 %collective-permute-start.4 = (f32[4,16,256]{2,1,0:T(8,128)S(1)}, f32[4,16,256]{2,1,0:T(8,128)S(1)}, u32[]{:S(2)}, u32[]{:S(2)}) collective-permute-start(f32[4,16,256]{2,1,0:T(8,128)S(1)} %get-tuple-element.99), channel_id=1, source_target_pairs={{1,2},{2,1},{3,4},{4,3},{5,6},{6,5},{0,8},{7,15},{9,10},{10,9},{11... | collective-permute-start | bytes 196616 | tf_op jit(solution)/shard_map/ppermute | solution.py:706
  8.8 4.1 %collective-permute-start.5 = (f32[4,16,256]{2,1,0:T(8,128)S(1)}, f32[4,16,256]{2,1,0:T(8,128)S(1)}, u32[]{:S(2)}, u32[]{:S(2)}) collective-permute-start(f32[4,16,256]{2,1,0:T(8,128)S(1)} %get-tuple-element.100), channel_id=1, source_target_pairs={{0,1},{1,0},{2,3},{3,2},{4,5},{5,4},{6,7},{7,6},{8,9},{9,8},{10,11... | collective-permute-start | bytes 196616 | tf_op jit(solution)/shard_map/ppermute | solution.py:706
  14.4 7.3 %collective-permute-start.6 = (f32[8,896]{1,0:T(8,128)S(1)}, f32[8,896]{1,0:T(8,128)S(1)}, u32[]{:S(2)}, u32[]{:S(2)}) collective-permute-start(f32[8,896]{1,0:T(8,128)S(1)} %get-tuple-element.105), channel_id=1, source_target_pairs={{1,2},{2,1},{3,4},{4,3},{5,6},{6,5},{0,8},{7,15},{9,10},{10,9},{11... | collective-permute-start | bytes 86024 | tf_op jit(solution)/shard_map/ppermute | solution.py:706
  16.4 5.3 %collective-permute-start.9 = (f32[8,896]{1,0:T(8,128)S(1)}, f32[8,896]{1,0:T(8,128)S(1)}, u32[]{:S(2)}, u32[]{:S(2)}) collective-permute-start(f32[8,896]{1,0:T(8,128)S(1)} %get-tuple-element.106), channel_id=1, source_target_pairs={{0,1},{1,0},{2,3},{3,2},{4,5},{5,4},{6,7},{7,6},{8,9},{9,8},{10,11... | collective-permute-start | bytes 86024 | tf_op jit(solution)/shard_map/ppermute | solution.py:706
  16.4 3.7 %collective-permute-start.7 = (f32[8,512]{1,0:T(8,128)S(1)}, f32[8,512]{1,0:T(8,128)S(1)}, u32[]{:S(2)}, u32[]{:S(2)}) collective-permute-start(f32[8,512]{1,0:T(8,128)S(1)} %get-tuple-element.104.far), channel_id=1, source_target_pairs={{0,2},{2,0},{1,3},{3,1},{4,6},{6,4},{5,7},{7,5},{8,10},{10,8},{9,1... | collective-permute-start | bytes 49160 | tf_op jit(solution)/shard_map/ppermute | solution.py:717
  18.0 3.7 %collective-permute-start.8 = (f32[8,512]{1,0:T(8,128)S(1)}, f32[8,512]{1,0:T(8,128)S(1)}, u32[]{:S(2)}, u32[]{:S(2)}) collective-permute-start(f32[8,512]{1,0:T(8,128)S(1)} %get-tuple-element.104.far), channel_id=1, source_target_pairs={{2,4},{4,2},{3,5},{5,3},{0,1},{1,0},{6,7},{7,6},{10,12},{12,10},{1... | collective-permute-start | bytes 49160 | tf_op jit(solution)/shard_map/ppermute | solution.py:717
